TPU v7x, 256 devices: a whole 4x4x8 slice. The times are simulated.
256 devices in a mesh: section: 8 (over z), seq: 16 (over y_hi, x, core), tensor: 2 (over y_lo).
Axes of the slice: x: 4, y: 4 (y_hi: 2, y_lo: 2; y = y_hi * 2 + y_lo), z: 8, core: 2. Of those that a mesh axis runs over, the one named last changes fastest.
Arguments:
- hidden: bfloat16 [2048, 8192], P('seq', ('section', 'tensor')), may hold values from -6 to 6
- dec_gain: float32 [8192], P(('section', 'tensor')), may hold values from 0.5 to 1.5
- neigh_states: bfloat16 [4096, 8192], P('seq', ('section', 'tensor')), may hold values from -6 to 6
- enc_gain: float32 [8192], P(('section', 'tensor')), may hold values from 0.5 to 1.5
- w_query: bfloat16 [8192, 8192], P(('section', 'tensor'), 'seq'), may hold values from -0.0625 to 0.0625
- w_key: bfloat16 [8192, 8192], P(('section', 'tensor'), 'seq'), may hold values from -0.0625 to 0.0625
- w_value: bfloat16 [8192, 8192], P(('section', 'tensor'), 'seq'), may hold values from -0.0625 to 0.0625
- w_out: bfloat16 [8192, 8192], P('seq', ('section', 'tensor')), may hold values from -0.0625 to 0.0625
- neighbour_ids: int32 [32], replicated, may hold values from 0 to 31, each once
- neighbour_len: int32 [32], replicated, may hold values from 32 to 128, as said below
- cotangent: bfloat16 [2048, 8192], P('seq', ('section', 'tensor')), may hold values from -6 to 6
Outputs:
- layer_out: bfloat16 [2048, 8192], P('seq', ('section', 'tensor'))
- hidden_grad: float32 [2048, 8192], P('seq', ('section', 'tensor'))
- neighbour_grad: float32 [4096, 8192], P('seq', ('section', 'tensor'))
- dec_gain_grad: float32 [8192], P(('section', 'tensor'))
- enc_gain_grad: float32 [8192], P(('section', 'tensor'))
- query_weight_grad: float32 [8192, 8192], P(('section', 'tensor'), 'seq')
- key_weight_grad: float32 [8192, 8192], P(('section', 'tensor'), 'seq')
- value_weight_grad: float32 [8192, 8192], P(('section', 'tensor'), 'seq')
- out_weight_grad: float32 [8192, 8192], P('seq', ('section', 'tensor'))
Inputs may be any that keep to these rules, and one draw needn't show every extreme that they name: `neighbour_ids`: each stored neighbour serves exactly one slot. `neighbour_len`: some stored neighbour is full.
All inputs are finite; a program needn't handle non-finite values.
Results may differ from a plain program's by a relative error of at most 0.0095.
Values may be sent and summed in bfloat16 or wider, within the bound.
A program may use at most 128 MiB of HBM per device.

v0:
```python
import jax
import jax.numpy as jnp
from jax import lax
from jax.sharding import PartitionSpec as P

HEAD = 128
BLOCK = 64
NEIGH = 1
NLEN = 128


EPS = 1e-05


def attend(queries, key_values, lengths, heads_here):
    width = heads_here * HEAD
    blocks = queries.shape[0] // BLOCK
    q_four = queries.reshape(blocks, BLOCK, heads_here, HEAD)
    k_four = key_values[:, :width].reshape(blocks, NEIGH * NLEN, heads_here, HEAD)
    v_four = key_values[:, width:].reshape(blocks, NEIGH * NLEN, heads_here, HEAD)
    scale = HEAD ** (-0.5)
    scores = (
        jnp.einsum("cihd,cjhd->chij", q_four, k_four, preferred_element_type=jnp.float32) * scale
    )
    positions = jnp.arange(NEIGH * NLEN, dtype=jnp.int32)
    valid = (positions % NLEN)[None, :] < jnp.repeat(lengths.reshape(blocks, NEIGH), NLEN, axis=1)
    scores = jnp.where(valid[:, None, None, :], scores, -jnp.inf)
    top = jnp.max(scores, axis=-1, keepdims=True)
    expo = jnp.exp(scores - top)
    probs = expo / jnp.sum(expo, axis=-1, keepdims=True)
    probs_low = probs.astype(jnp.bfloat16)
    attended = jnp.einsum("chij,cjhd->cihd", probs_low, v_four, preferred_element_type=jnp.float32)
    return (
        attended.reshape(-1, width).astype(jnp.bfloat16),
        probs,
        probs_low,
        q_four,
        k_four,
        v_four,
    )


def attend_back(attended_grad, probs, probs_low, q_four, k_four, v_four):
    blocks, rows, heads_here, size = q_four.shape
    width = heads_here * size
    grad_four = attended_grad.reshape(blocks, rows, heads_here, size)
    scale = HEAD ** (-0.5)
    value_grad = jnp.einsum(
        "chij,cihd->cjhd", probs_low, grad_four, preferred_element_type=jnp.float32
    )
    prob_grad = jnp.einsum("cihd,cjhd->chij", grad_four, v_four, preferred_element_type=jnp.float32)
    score_grad = probs * (prob_grad - jnp.sum(probs * prob_grad, axis=-1, keepdims=True)) * scale
    query_grad = jnp.einsum(
        "chij,cjhd->cihd", score_grad, k_four.astype(jnp.float32), precision=lax.Precision.HIGHEST
    )
    key_grad = jnp.einsum(
        "chij,cihd->cjhd", score_grad, q_four.astype(jnp.float32), precision=lax.Precision.HIGHEST
    )
    query_grad = query_grad.reshape(-1, width).astype(jnp.bfloat16)
    pair_grad = jnp.concatenate(
        [key_grad.reshape(-1, width), value_grad.reshape(-1, width)], axis=1
    ).astype(jnp.bfloat16)
    return (query_grad, pair_grad)


def body(
    hidden,
    dec_gain,
    neigh_states,
    enc_gain,
    w_query,
    w_key,
    w_value,
    w_out,
    neighbour_ids,
    neighbour_len,
    cotangent,
):
    n_feature = lax.axis_size(("section", "tensor"))
    n_group = lax.axis_size("seq")
    store_here = neigh_states.shape[0]
    full_width = hidden.shape[1] * n_feature
    width_here = w_query.shape[1]
    heads_here = width_here // HEAD
    stored_all = store_here * n_group
    stored_count = neighbour_ids.shape[0]
    dec_rows = hidden.astype(jnp.float32)
    enc_rows = neigh_states.astype(jnp.float32)
    dec_squares, enc_squares = lax.psum(
        (jnp.sum(dec_rows * dec_rows, axis=1), jnp.sum(enc_rows * enc_rows, axis=1)),
        ("section", "tensor"),
    )
    dec_scale = lax.rsqrt(dec_squares[:, None] / full_width + EPS)
    enc_scale = lax.rsqrt(enc_squares[:, None] / full_width + EPS)
    dec_hat = dec_rows * dec_scale
    enc_hat = enc_rows * enc_scale
    dec_local = (dec_hat * dec_gain).astype(jnp.bfloat16)
    enc_local = (enc_hat * enc_gain).astype(jnp.bfloat16)
    dec_normed, enc_normed = (
        lax.all_gather(dec_local, "seq", axis=0, tiled=True),
        lax.all_gather(enc_local, "seq", axis=0, tiled=True),
    )
    offsets = jnp.arange(NLEN, dtype=jnp.int32)
    row_index = (neighbour_ids[:, None] * NLEN + offsets[None, :]).reshape(-1)
    ordered = enc_normed[row_index]
    lengths = neighbour_len[neighbour_ids]
    pair_weight = jnp.concatenate([w_key, w_value], axis=1)
    block_owner = lax.axis_index(("section", "tensor"))
    neigh_slice = stored_all // n_feature
    rows = dec_normed
    queries = lax.psum_scatter(
        jnp.dot(rows, w_query, preferred_element_type=jnp.float32),
        ("section", "tensor"),
        scatter_dimension=0,
        tiled=True,
    ).astype(jnp.bfloat16)
    rows = ordered
    key_values = lax.psum_scatter(
        jnp.dot(rows, pair_weight, preferred_element_type=jnp.float32),
        ("section", "tensor"),
        scatter_dimension=0,
        tiled=True,
    ).astype(jnp.bfloat16)
    slots_here = neigh_slice // NLEN
    lengths_here = lax.dynamic_slice_in_dim(lengths, block_owner * slots_here, slots_here, 0)
    attended, probs, probs_low, q_four, k_four, v_four = attend(
        queries, key_values, lengths_here, heads_here
    )
    attended_all = lax.all_gather(attended, ("section", "tensor"), axis=0, tiled=True)
    rows = attended_all
    out_total = lax.psum_scatter(
        jnp.dot(rows, w_out, preferred_element_type=jnp.float32),
        "seq",
        scatter_dimension=0,
        tiled=True,
    )
    layer_out = (dec_rows + out_total).astype(jnp.bfloat16)
    grad_rows = lax.all_gather(cotangent, "seq", axis=0, tiled=True)
    out_weight_grad = jnp.dot(attended_all.T, grad_rows, preferred_element_type=jnp.float32)
    rows = grad_rows
    attended_grad = lax.psum_scatter(
        jnp.dot(rows, w_out.T, preferred_element_type=jnp.float32),
        ("section", "tensor"),
        scatter_dimension=0,
        tiled=True,
    ).astype(jnp.bfloat16)
    query_grad, pair_grad = attend_back(attended_grad, probs, probs_low, q_four, k_four, v_four)
    query_grad_all, pair_grad_all = (
        lax.all_gather(query_grad, ("section", "tensor"), axis=0, tiled=True),
        lax.all_gather(pair_grad, ("section", "tensor"), axis=0, tiled=True),
    )
    query_weight_grad = jnp.dot(dec_normed.T, query_grad_all, preferred_element_type=jnp.float32)
    pair_weight_grad = jnp.dot(ordered.T, pair_grad_all, preferred_element_type=jnp.float32)
    key_weight_grad = pair_weight_grad[:, :width_here]
    value_weight_grad = pair_weight_grad[:, width_here:]
    rows = query_grad_all
    dec_input = lax.psum_scatter(
        jnp.dot(rows, w_query.T, preferred_element_type=jnp.float32),
        "seq",
        scatter_dimension=0,
        tiled=True,
    )
    inverse = (
        jnp.zeros((stored_count,), jnp.int32)
        .at[neighbour_ids]
        .set(jnp.arange(stored_count, dtype=jnp.int32))
    )
    back_index = (inverse[:, None] * NLEN + offsets[None, :]).reshape(-1)
    enc_input = lax.psum_scatter(
        jnp.dot(pair_grad_all[back_index], pair_weight.T, preferred_element_type=jnp.float32),
        "seq",
        scatter_dimension=0,
        tiled=True,
    )
    dec_scaled = dec_gain * dec_input
    enc_scaled = enc_gain * enc_input
    dec_inner, enc_inner = lax.psum(
        (jnp.sum(dec_scaled * dec_hat, axis=1), jnp.sum(enc_scaled * enc_hat, axis=1)),
        ("section", "tensor"),
    )
    hidden_grad = cotangent.astype(jnp.float32) + dec_scale * (
        dec_scaled - dec_hat * (dec_inner[:, None] / full_width)
    )
    neighbour_grad = enc_scale * (enc_scaled - enc_hat * (enc_inner[:, None] / full_width))
    dec_gain_grad, enc_gain_grad = lax.psum(
        (jnp.sum(dec_input * dec_hat, axis=0), jnp.sum(enc_input * enc_hat, axis=0)), "seq"
    )
    return (
        layer_out,
        hidden_grad,
        neighbour_grad,
        dec_gain_grad,
        enc_gain_grad,
        query_weight_grad,
        key_weight_grad,
        value_weight_grad,
        out_weight_grad,
    )


def solution(mesh):
    in_specs = (
        P("seq", ("section", "tensor")),
        P(("section", "tensor")),
        P("seq", ("section", "tensor")),
        P(("section", "tensor")),
        P(("section", "tensor"), "seq"),
        P(("section", "tensor"), "seq"),
        P(("section", "tensor"), "seq"),
        P("seq", ("section", "tensor")),
        P(),
        P(),
        P("seq", ("section", "tensor")),
    )
    out_specs = (
        P("seq", ("section", "tensor")),
        P("seq", ("section", "tensor")),
        P("seq", ("section", "tensor")),
        P(("section", "tensor")),
        P(("section", "tensor")),
        P(("section", "tensor"), "seq"),
        P(("section", "tensor"), "seq"),
        P(("section", "tensor"), "seq"),
        P("seq", ("section", "tensor")),
    )
    return jax.shard_map(body, mesh=mesh, in_specs=in_specs, out_specs=out_specs, check_vma=False)
```

profile of v0, /device:TPU:1, one launch (start us, length us, event | category | flops | bytes accessed | tf_op | source)
XLA Modules:
  0.0 1418.0 jit_solution(1921085817406868299)
XLA Ops:
  7.2 1.1 fusion.28
  8.3 1.1 fusion.17
  9.4 31.3 %all-reduce.1 = (f32[256]{0:T(256)S(1)}, f32[128]{0:T(128)S(1)}) all-reduce(f32[256]{0:T(256)S(1)} %fusion.17, f32[128]{0:T(128)S(1)} %fusion.28), channel_id=1, replica_groups=mesh['section'=8,'seq'=16,'tensor'=2] {'section','tensor'}, use_global_device_ids=true, to_apply=%region_1.0 | all-reduce | flops 384 | bytes 3072 | tf_op jit(solution)/shard_map/psum | solution.py:89
  40.7 1.7 fusion.22
  42.5 0.7 all-gather.13.cloned.1.call-update
  43.2 1.8 fusion.12
  45.1 55.8 %all-gather.9.cloned.1.call-done = bf16[2048,512]{1,0:T(8,128)(2,1)} async-done(((bf16[128,512]{1,0:T(8,128)(2,1)}), bf16[2048,512]{1,0:T(8,128)(2,1)}) %all-gather.9.cloned.1.call-update) | async-done | bytes 2097168 | tf_op jit(solution)/shard_map/all_gather | solution.py:100
  100.8 4.8 fusion.49
  105.7 50.3 %all-gather.13.cloned.1.call-done = bf16[2048,512]{1,0:T(8,128)(2,1)} async-done(((bf16[128,512]{1,0:T(8,128)(2,1)}), bf16[2048,512]{1,0:T(8,128)(2,1)}) %all-gather.13.cloned.1.call-update) | async-done | bytes 2097168 | tf_op jit(solution)/shard_map/all_gather | solution.py:138
  156.0 4.8 fusion.51
  160.9 1.0 copy-done.10
  162.2 57.1 %all-gather.7.cloned.1.call-done = bf16[4096,512]{1,0:T(8,128)(2,1)} async-done(((bf16[256,512]{1,0:T(8,128)(2,1)}), bf16[4096,512]{1,0:T(8,128)(2,1)}) %all-gather.7.cloned.1.call-update) | async-done | bytes 4194320 | tf_op jit(solution)/shard_map/all_gather | solution.py:101
  219.4 20.2 %gather_fusion = bf16[4096,512]{1,0:T(8,128)(2,1)} fusion(bf16[4096,512]{1,0:T(8,128)(2,1)} %all-gather.7.cloned.1.call-done, s32[4096]{0:T(1024)S(1)} %broadcast_clamp_fusion.1), kind=kCustom, calls=%fused_computation | custom fusion | bytes 8404992 | tf_op jit(solution)/shard_map/gather | solution.py:105
  239.6 10.4 fusion.48
  251.4 67.0 %reduce-scatter.9.cloned.1.call-done = f32[128,512]{1,0:T(8,128)} async-done(((f32[2048,512]{1,0:T(8,128)}), f32[128,512]{1,0:T(8,128)}) %reduce-scatter.9.cloned.1.call-update) | async-done | bytes 262160 | tf_op jit(solution)/shard_map/reduce_scatter | solution.py:111
  318.4 1.0 convert_element_type.56
  319.4 101.2 %reduce-scatter.13.cloned.1.call-done = f32[128,512]{1,0:T(8,128)} async-done(((f32[2048,512]{1,0:T(8,128)}), f32[128,512]{1,0:T(8,128)}) %reduce-scatter.13.cloned.1.call-update) | async-done | bytes 262160 | tf_op jit(solution)/shard_map/reduce_scatter | solution.py:141
  420.6 1.0 convert_element_type.63
  421.6 354.7 %reduce-scatter.7.cloned.1.call-done = f32[256,1024]{1,0:T(8,128)} async-done(((f32[4096,1024]{1,0:T(8,128)}), f32[256,1024]{1,0:T(8,128)}) %reduce-scatter.7.cloned.1.call-update) | async-done | bytes 1048592 | tf_op jit(solution)/shard_map/reduce_scatter | solution.py:118
  776.2 1.3 convert_element_type.54
  778.0 1.4 fusion.47
  781.1 2.3 fusion.2
  783.4 1.1 copy.37
  784.6 1.1 fusion.4
  785.9 0.9 pad_maximum_fusion
  786.9 0.9 fusion.7
  788.7 57.2 %all-gather.15.cloned.1.call-done = bf16[2048,512]{1,0:T(8,128)(2,1)} async-done(((bf16[128,512]{1,0:T(8,128)(2,1)}), bf16[2048,512]{1,0:T(8,128)(2,1)}) %all-gather.15.cloned.1.call-update) | async-done | bytes 2097168 | tf_op jit(solution)/shard_map/all_gather | solution.py:149
  845.8 4.8 fusion.52
  850.7 0.9 scatter_custom_fusion
  851.7 186.1 %all-gather.17.cloned.1.call-done = bf16[4096,1024]{1,0:T(8,128)(2,1)} async-done(((bf16[256,1024]{1,0:T(8,128)(2,1)}), bf16[4096,1024]{1,0:T(8,128)(2,1)}) %all-gather.17.cloned.1.call-update) | async-done | bytes 8388624 | tf_op jit(solution)/shard_map/all_gather | solution.py:150
  1037.8 25.4 %gather_fusion.2 = bf16[4096,1024]{1,0:T(8,128)(2,1)} fusion(bf16[4096,1024]{1,0:T(8,128)(2,1)} %all-gather.17.cloned.1.call-done, s32[4096]{0:T(1024)S(1)} %broadcast_clamp_fusion), kind=kCustom, calls=%fused_computation.2 | custom fusion | bytes 16793600 | tf_op jit(solution)/shard_map/gather | solution.py:170
  1063.2 10.2 fusion.53
  1073.5 31.4 %all-gather.11.cloned.1.call-done = bf16[2048,512]{1,0:T(8,128)(2,1)} async-done(((bf16[128,512]{1,0:T(8,128)(2,1)}), bf16[2048,512]{1,0:T(8,128)(2,1)}) %all-gather.11.cloned.1.call-update) | async-done | bytes 2097168 | tf_op jit(solution)/shard_map/all_gather | solution.py:129
  1104.9 4.8 fusion.50
  1109.7 1.6 copy-done.3
  1111.3 4.0 fusion.56
  1115.3 2.2 fusion.54
  1117.5 85.4 %reduce-scatter.15.cloned.1.call-done = f32[128,512]{1,0:T(8,128)} async-done(((f32[2048,512]{1,0:T(8,128)}), f32[128,512]{1,0:T(8,128)}) %reduce-scatter.15.cloned.1.call-update) | async-done | bytes 262160 | tf_op jit(solution)/shard_map/reduce_scatter | solution.py:157
  1202.9 1.2 fusion.27
  1204.1 8.3 fusion.55
  1212.4 1.5 fusion.45
  1213.9 103.6 %reduce-scatter.17.cloned.1.call-done = f32[256,512]{1,0:T(8,128)} async-done(((f32[4096,512]{1,0:T(8,128)}), f32[256,512]{1,0:T(8,128)}) %reduce-scatter.17.cloned.1.call-update) | async-done | bytes 524304 | tf_op jit(solution)/shard_map/reduce_scatter | solution.py:169
  1317.6 1.3 fusion.16
  1318.9 26.9 %all-reduce = (f32[128]{0:T(128)S(1)}, f32[256]{0:T(256)S(1)}) all-reduce(f32[128]{0:T(128)S(1)} %get-tuple-element.12, f32[256]{0:T(256)S(1)} %get-tuple-element.10), channel_id=1, replica_groups=mesh['section'=8,'seq'=16,'tensor'=2] {'section','tensor'}, use_global_device_ids=true, to_apply=%region_13.14 | all-reduce | flops 384 | bytes 3072 | tf_op jit(solution)/shard_map/psum | solution.py:177
  1345.7 42.4 %all-reduce.2 = (f32[512]{0:T(512)}, f32[512]{0:T(512)}) all-reduce(f32[512]{0:T(512)S(1)} %get-tuple-element.11, f32[512]{0:T(512)S(1)} %get-tuple-element.9), channel_id=1, replica_groups=mesh['section'=8,'seq'=16,'tensor'=2] {'seq'}, use_global_device_ids=true, to_apply=%region_19.20 | all-reduce | flops 1024 | bytes 8192 | tf_op jit(solution)/shard_map/psum | solution.py:185
  1388.1 2.0 fusion.15
  1390.2 19.1 %reduce-scatter.11.cloned.1.call-done = f32[128,512]{1,0:T(8,128)} async-done(((f32[2048,512]{1,0:T(8,128)}), f32[128,512]{1,0:T(8,128)}) %reduce-scatter.11.cloned.1.call-update) | async-done | bytes 262160 | tf_op jit(solution)/shard_map/reduce_scatter | solution.py:131
  1409.3 1.8 fusion.26
  (91 shorter events, 5.8 us)
Async XLA Ops:
  7.2 93.7 %copy-start = (bf16[512,512]{1,0:T(8,128)(2,1)S(1)}, bf16[512,512]{1,0:T(8,128)(2,1)}, u32[]{:S(2)}) copy-start(bf16[512,512]{1,0:T(8,128)(2,1)} %param.15) | copy-start | bytes 1572868
  7.2 93.7 %all-gather.9.cloned.1.call-start = ((), (), s32[]{:S(2)}) async-start(), calls=%async_computation.8 | async-start | bytes 2228224 | tf_op jit(solution)/shard_map/all_gather | solution.py:100
  42.4 113.6 %all-gather.13.cloned.1.call-start = ((), (), s32[]{:S(2)}) async-start(), calls=%async_computation.12 | async-start | bytes 2228224 | tf_op jit(solution)/shard_map/all_gather | solution.py:138
  43.2 176.2 %all-gather.7.cloned.1.call-start = ((), (), s32[]{:S(2)}) async-start(), calls=%async_computation.6 | async-start | bytes 4456448 | tf_op jit(solution)/shard_map/all_gather | solution.py:101
  45.0 273.4 %reduce-scatter.9.cloned.1.call-start = ((), (), s32[]{:S(2)}) async-start(), calls=%async_computation.9 | async-start | bytes 4456448 | tf_op jit(solution)/shard_map/reduce_scatter | solution.py:111
  105.6 50.4 %copy-start.7 = (bf16[512,512]{1,0:T(8,128)(2,1)S(1)}, bf16[512,512]{1,0:T(8,128)(2,1)}, u32[]{:S(2)}) copy-start(bf16[512,512]{1,0:T(8,128)(2,1)} %param.18) | copy-start | bytes 1572868
  105.7 314.9 %reduce-scatter.13.cloned.1.call-start = ((), (), s32[]{:S(2)}) async-start(), calls=%async_computation.13 | async-start | bytes 4456448 | tf_op jit(solution)/shard_map/reduce_scatter | solution.py:141
  160.8 1.0 copy-start.10
  160.8 1.2 copy-start.11
  160.8 1.3 copy-start.15
  160.9 615.4 %reduce-scatter.7.cloned.1.call-start = ((), (), s32[]{:S(2)}) async-start(), calls=%async_computation.7 | async-start | bytes 17825792 | tf_op jit(solution)/shard_map/reduce_scatter | solution.py:118
  249.9 0.7 copy-start.2
  250.0 595.9 %all-gather.15.cloned.1.call-start = ((), (), s32[]{:S(2)}) async-start(), calls=%async_computation.14 | async-start | bytes 2228224 | tf_op jit(solution)/shard_map/all_gather | solution.py:149
  779.8 1.3 copy-start.16
  779.8 1.3 copy-start.17
  781.1 256.7 %all-gather.17.cloned.1.call-start = ((), (), s32[]{:S(2)}) async-start(), calls=%async_computation.16 | async-start | bytes 8912896 | tf_op jit(solution)/shard_map/all_gather | solution.py:150
  786.8 318.1 %all-gather.11.cloned.1.call-start = ((), (), s32[]{:S(2)}) async-start(), calls=%async_computation.10 | async-start | bytes 2228224 | tf_op jit(solution)/shard_map/all_gather | solution.py:129
  788.6 414.3 %reduce-scatter.15.cloned.1.call-start = ((), (), s32[]{:S(2)}) async-start(), calls=%async_computation.15 | async-start | bytes 4456448 | tf_op jit(solution)/shard_map/reduce_scatter | solution.py:157
  850.7 466.9 %reduce-scatter.17.cloned.1.call-start = ((), (), s32[]{:S(2)}) async-start(), calls=%async_computation.17 | async-start | bytes 8912896 | tf_op jit(solution)/shard_map/reduce_scatter | solution.py:169
  1073.4 335.9 %reduce-scatter.11.cloned.1.call-start = ((), (), s32[]{:S(2)}) async-start(), calls=%async_computation.11 | async-start | bytes 4456448 | tf_op jit(solution)/shard_map/reduce_scatter | solution.py:131
  1109.7 1.6 copy-start.3
  1111.3 4.0 copy-start.4
  1111.3 4.0 copy-start.6
  1115.3 87.6 %copy-start.8 = (bf16[128,512]{1,0:T(8,128)(2,1)S(1)}, bf16[128,512]{1,0:T(8,128)(2,1)}, u32[]{:S(2)}) copy-start(bf16[128,512]{1,0:T(8,128)(2,1)} %param.11) | copy-start | bytes 393220
  1115.3 87.6 %copy-start.14 = (f32[512]{0:T(512)S(1)}, f32[512]{0:T(512)}, u32[]{:S(2)}) copy-start(f32[512]{0:T(512)} %param.12) | copy-start | bytes 6148
  1204.1 207.0 %copy-start.1 = (bf16[512,512]{1,0:T(8,128)(2,1)S(1)}, bf16[512,512]{1,0:T(8,128)(2,1)}, u32[]{:S(2)}) copy-start(bf16[512,512]{1,0:T(8,128)(2,1)} %param.15) | copy-start | bytes 1572868
  1212.4 105.2 %copy-start.5 = (bf16[256,512]{1,0:T(8,128)(2,1)S(1)}, bf16[256,512]{1,0:T(8,128)(2,1)}, u32[]{:S(2)}) copy-start(bf16[256,512]{1,0:T(8,128)(2,1)} %param.13) | copy-start | bytes 786436
  1212.4 105.2 %copy-start.13 = (f32[512]{0:T(512)S(1)}, f32[512]{0:T(512)}, u32[]{:S(2)}) copy-start(f32[512]{0:T(512)} %param.14) | copy-start | bytes 6148
  1212.4 196.9 %copy-start.9 = (f32[128,512]{1,0:T(8,128)S(1)}, f32[128,512]{1,0:T(8,128)}, u32[]{:S(2)}) copy-start(f32[128,512]{1,0:T(8,128)} %reduce-scatter.15.cloned.1.call-done) | copy-start | bytes 786436
  1212.4 196.9 %copy-start.12 = (bf16[128,512]{1,0:T(8,128)(2,1)S(1)}, bf16[128,512]{1,0:T(8,128)(2,1)}, u32[]{:S(2)}) copy-start(bf16[128,512]{1,0:T(8,128)(2,1)} %param.21) | copy-start | bytes 393220
Sparse Core Ops, SparseCore 0:
  42.5 58.2 all-gather.8
  103.6 52.3 all-gather.12
  159.3 60.0 all-gather.6
  221.8 96.5 reduce-scatter.8
  320.8 99.7 reduce-scatter.12
  423.0 353.2 reduce-scatter.6
  781.2 64.5 all-gather.14
  848.2 189.5 all-gather.16
  1040.2 64.6 all-gather.10
  1109.1 93.7 reduce-scatter.14
  1208.2 109.2 reduce-scatter.16
  1322.4 86.8 reduce-scatter.10
where the time goes:
time: 1420 us
  waiting for transfers between devices  1170 us (82%)
  blocking collectives  101 us (7%)
  matrix products  59.7 us (4%)
  local copies, waits for them, and re-layouts  55.3 us (4%)
  other arithmetic  17.7 us (1%)
  between operations  14.5 us (1%)
    reduce_scatter x1, waiting for transfers between devices, body(): lax.psum_scatter(jnp.dot(rows, pair_weight, preferred_element_type=jnp.fl...  355 us
    all_gather x1, waiting for transfers between devices, body(): lax.all_gather(pair_grad, ('section', 'tensor'), axis=0, tiled=True)  186 us
    reduce_scatter x1, waiting for transfers between devices, body(): lax.psum_scatter(jnp.dot(pair_grad_all[back_index], pair_weight.T, prefer...  104 us
    reduce_scatter x1, waiting for transfers between devices, body(): lax.psum_scatter(jnp.dot(rows, w_out.T, preferred_element_type=jnp.float3...  101 us
    reduce_scatter x1, waiting for transfers between devices, body(): lax.psum_scatter(jnp.dot(rows, w_query.T, preferred_element_type=jnp.floa...  85.4 us
    reduce_scatter x1, waiting for transfers between devices, body(): lax.psum_scatter(jnp.dot(rows, w_query, preferred_element_type=jnp.float3...  67 us
    all_gather x1, waiting for transfers between devices, body(): lax.all_gather(query_grad, ('section', 'tensor'), axis=0, tiled=True)  57.2 us
    all_gather x1, waiting for transfers between devices, body(): lax.all_gather(enc_local, 'seq', axis=0, tiled=True)  57.1 us
  transfers between devices with their start and end apart: 12, of which 12 were waited for; matrix products, arithmetic and copies ran while one was open for 8% of the time, Pallas kernels for 0%

commit v1 on v0

v1 whole, which is shorter than its diff:
```python
import functools

import jax
import jax.numpy as jnp
from jax import lax
from jax.experimental import pallas as pl
from jax.experimental.pallas import tpu as pltpu
from jax.sharding import PartitionSpec as P

F32 = jnp.float32
BF16 = jnp.bfloat16
MESH = pl.DeviceIdType.MESH
EPS = 1e-05
WIDTH = 8192
ANY = pl.BlockSpec(memory_space=pl.ANY)
VMEM = pl.BlockSpec(memory_space=pltpu.VMEM)
SMEM = pl.BlockSpec(memory_space=pltpu.SMEM)
DMA = pltpu.SemaphoreType.DMA
RING = 16
DEPTH = 8


def place():
    z = lax.axis_index("section")
    s = lax.axis_index("seq")
    t = lax.axis_index("tensor")
    x = lax.div(lax.rem(s, 8), 2)
    y = lax.div(s, 8) * 2 + t
    return z, s, t, x, y, lax.rem(s, 2)


def ring_position(ring, x, y):
    return (y if ring == 0 else x) * 4 + lax.rem(x + y, 4)


def ring_chip(ring, p):
    a = lax.div(p, 4)
    b = lax.rem(lax.rem(p, 4) + 4 - a, 4)
    return (b, a) if ring == 0 else (a, b)


def seq_tensor(x, y, core):
    return lax.div(y, 2) * 8 + x * 2 + core, lax.rem(y, 2)


def ring_device(ring, p, core):
    x, y = ring_chip(ring, lax.rem(p + RING, RING))
    s, t = seq_tensor(x, y, core)
    return {"seq": s, "tensor": t}


def remote(src, dst, send_sem, recv_sem, device):
    return pltpu.make_async_remote_copy(
        src_ref=src,
        dst_ref=dst,
        send_sem=send_sem,
        recv_sem=recv_sem,
        device_id=device,
        device_id_type=MESH,
    )


def greet(devices):
    barrier = pltpu.get_barrier_semaphore()
    for device in devices:
        pl.semaphore_signal(barrier, inc=1, device_id=device, device_id_type=MESH)
    pl.semaphore_wait(barrier, len(devices))


def plane_neighbours(x, y, core, s):
    p1, p2 = ring_position(0, x, y), ring_position(1, x, y)
    return [
        ring_device(0, p1 + 1, core),
        ring_device(0, p1 - 1, core),
        ring_device(1, p2 + 1, core),
        ring_device(1, p2 - 1, core),
        {"seq": s + 1 - 2 * core},
    ]


def params(cid, mib=None):
    return pltpu.CompilerParams(
        collective_id=cid,
        has_side_effects=True,
        vmem_limit_bytes=None if mib is None else mib * 1024 * 1024,
    )


def small_kernel(groups, *refs):
    n = len(groups)
    ins, outs, slots = refs[:n], refs[n : 2 * n], refs[2 * n : 3 * n]
    send, recv = refs[3 * n], refs[3 * n + 1]
    z, s, t, _, _, _ = place()

    def peer(group, r):
        if group == "st":
            g = lax.rem(z * 2 + t + r, 16)
            return {"section": lax.div(g, 2), "tensor": lax.rem(g, 2)}, g
        g = lax.rem(s + r, 16)
        return {"seq": g}, g

    barrier = pltpu.get_barrier_semaphore()
    for group in groups:

        def hello(r, _, group=group):
            pl.semaphore_signal(
                barrier, inc=1, device_id=peer(group, r)[0], device_id_type=MESH
            )
            return 0

        lax.fori_loop(1, 16, hello, 0)
    pl.semaphore_wait(barrier, 15 * n)
    for k, group in enumerate(groups):
        mine = peer(group, 0)[1]

        def push(r, _, k=k, group=group, mine=mine):
            device, _g = peer(group, r)
            remote(
                ins[k], slots[k].at[mine], send.at[k, r], recv.at[k, mine], device
            ).start()
            return 0

        lax.fori_loop(1, 16, push, 0)
        slots[k][mine] = ins[k][...]
    for k, group in enumerate(groups):
        mine = peer(group, 0)[1]

        def take(r, _, k=k, group=group, mine=mine):
            device, g = peer(group, r)
            remote(ins[k], slots[k].at[g], send.at[k, r], recv.at[k, g], device).wait_recv()
            return 0

        lax.fori_loop(1, 16, take, 0)
        total = slots[k][0]
        for g in range(1, 16):
            total = total + slots[k][g]
        outs[k][...] = total
    for k, group in enumerate(groups):
        mine = peer(group, 0)[1]

        def drain(r, _, k=k, group=group, mine=mine):
            device, _g = peer(group, r)
            remote(
                ins[k], slots[k].at[mine], send.at[k, r], recv.at[k, mine], device
            ).wait_send()
            return 0

        lax.fori_loop(1, 16, drain, 0)


def small_sums(arrays, groups, cid):
    n = len(groups)
    return pl.pallas_call(
        functools.partial(small_kernel, groups),
        out_shape=[jax.ShapeDtypeStruct((8, 128), F32)] * n,
        in_specs=[VMEM] * n,
        out_specs=[VMEM] * n,
        scratch_shapes=[pltpu.VMEM((16, 8, 128), F32)] * n + [DMA((n, 16)), DMA((n, 16))],
        compiler_params=params(cid),
    )(*arrays)


def gather_kernel(
    cot,
    dec,
    enc,
    wq,
    wk,
    wv,
    wo,
    cot_all,
    dec_all,
    enc_all,
    wq_all,
    wk_all,
    wv_all,
    wo_all,
    send,
    recv,
    sib_send,
    sib_recv,
    own_sem,
    w_send,
    w_recv,
    w_own,
):
    z, s, t, x, y, core = place()
    sibling = {"seq": s + 1 - 2 * core}
    partner = {"tensor": 1 - t}
    greet(plane_neighbours(x, y, core, s))

    def slot(k, chip, c):
        so, to = seq_tensor(chip[0], chip[1], c)
        if k == 0:
            return cot_all.at[to, pl.ds(pl.multiple_of(so * 128, 128), 128)]
        if k == 1:
            return dec_all.at[to, pl.ds(pl.multiple_of(so * 128, 128), 128)]
        return enc_all.at[to, pl.ds(pl.multiple_of(so * 256 + (k - 2) * 128, 128), 128)]

    sources = (cot, dec, enc.at[pl.ds(0, 128)], enc.at[pl.ds(128, 128)])
    position = (ring_position(0, x, y), ring_position(1, x, y))

    def origin(k, j):
        sign = 1 - 2 * (k % 2)
        return ring_chip(k // 2, lax.rem(position[k // 2] + RING - sign * j, RING))

    def onward(k, j, src):
        sign = 1 - 2 * (k % 2)
        device = ring_device(k // 2, position[k // 2] + sign, core)
        return remote(src, slot(k, origin(k, j), core), send.at[k, j], recv.at[k, j], device)

    def across(k, j, src):
        return remote(
            src, slot(k, origin(k, j), core), sib_send.at[k, j], sib_recv.at[k, j], sibling
        )

    for k in range(4):
        onward(k, 0, sources[k]).start()
    half = pl.ds(pl.multiple_of(t * 256, 256), 256)
    rest = pl.ds(pl.multiple_of((1 - t) * 256, 256), 256)
    weights = ((wq, wq_all), (wk, wk_all), (wv, wv_all))
    swaps = [
        remote(w.at[:, rest], w_all.at[t], w_send.at[n], w_recv.at[n], partner)
        for n, (w, w_all) in enumerate(weights)
    ] + [remote(wo.at[rest, :], wo_all.at[t], w_send.at[3], w_recv.at[3], partner)]
    keeps = [
        pltpu.make_async_copy(w.at[:, half], w_all.at[t], w_own.at[n])
        for n, (w, w_all) in enumerate(weights)
    ] + [pltpu.make_async_copy(wo.at[half, :], wo_all.at[t], w_own.at[3])]
    for copy in swaps:
        copy.start()
    for k in range(4):
        across(k, 0, sources[k]).start()
        pltpu.make_async_copy(sources[k], slot(k, (x, y), core), own_sem.at[k]).start()
    for copy in keeps:
        copy.start()

    def step(j, _):
        for k in range(4):
            remote(
                sources[k],
                slot(k, origin(k, j + 1), core),
                send.at[k, j],
                recv.at[k, j],
                sibling,
            ).wait_recv()
            block = slot(k, origin(k, j + 1), core)

            @pl.when(j < RING - 2)
            def _(k=k, block=block):
                onward(k, j + 1, block).start()

            across(k, j + 1, block).start()
        return 0

    lax.fori_loop(0, RING - 1, step, 0)

    for k in range(4):
        pltpu.make_async_copy(sources[k], slot(k, (x, y), core), own_sem.at[k]).wait()

    def finish(j, _):
        for k in range(4):
            remote(
                sources[k],
                slot(k, origin(k, j), 1 - core),
                sib_send.at[k, j],
                sib_recv.at[k, j],
                sibling,
            ).wait_recv()
            across(k, j, sources[k]).wait_send()

            @pl.when(j < RING - 1)
            def _(k=k):
                onward(k, j, sources[k]).wait_send()

        return 0

    lax.fori_loop(0, RING, finish, 0)
    for copy in keeps:
        copy.wait()
    for copy in swaps:
        copy.wait_send()
    for n, (w, w_all) in enumerate(weights):
        remote(w.at[:, rest], w_all.at[1 - t], w_send.at[n], w_recv.at[n], partner).wait_recv()
    remote(wo.at[rest, :], wo_all.at[1 - t], w_send.at[3], w_recv.at[3], partner).wait_recv()


def gather_rows(cot, dec, enc, wq, wk, wv, wo):
    sds = jax.ShapeDtypeStruct
    return pl.pallas_call(
        gather_kernel,
        out_shape=[
            sds((2, 2048, 512), BF16),
            sds((2, 2048, 512), BF16),
            sds((2, 4096, 512), BF16),
            sds((2, 512, 256), BF16),
            sds((2, 512, 256), BF16),
            sds((2, 512, 256), BF16),
            sds((2, 256, 512), BF16),
        ],
        in_specs=[ANY] * 7,
        out_specs=[ANY] * 7,
        scratch_shapes=[
            DMA((4, 15)),
            DMA((4, 15)),
            DMA((4, 16)),
            DMA((4, 16)),
            DMA((4,)),
            DMA((4,)),
            DMA((4,)),
            DMA((4,)),
        ],
        compiler_params=params(1),
    )(cot, dec, enc, wq, wk, wv, wo)


def reorder_kernel(index, *refs):
    n = len(refs) // 2
    ins, outs, sem = refs[:n], refs[n : 2 * n], refs[2 * n]

    def copy(j, k):
        src = pl.ds(pl.multiple_of(index[j] * 64, 64), 64)
        dst = pl.ds(pl.multiple_of(j * 64, 64), 64)
        return pltpu.make_async_copy(ins[k].at[:, src], outs[k].at[:, dst], sem.at[k, j])

    def start(j, _):
        for k in range(n):
            copy(j, k).start()
        return 0

    def wait(j, _):
        for k in range(n):
            copy(j, k).wait()
        return 0

    lax.fori_loop(0, 32, start, 0)
    lax.fori_loop(0, 32, wait, 0)


def reorder(index, *arrays):
    n = len(arrays)
    return pl.pallas_call(
        reorder_kernel,
        out_shape=[jax.ShapeDtypeStruct(a.shape, a.dtype) for a in arrays],
        in_specs=[SMEM] + [ANY] * n,
        out_specs=[ANY] * n,
        scratch_shapes=[DMA((n, 32))],
    )(index, *arrays)


def dot(a, b):
    return jnp.dot(a, b, preferred_element_type=F32)


def dot_t(a, b):
    return lax.dot_general(a, b, (((1,), (1,)), ((), ())), preferred_element_type=F32)


def t_dot(a, b):
    return lax.dot_general(a, b, (((0,), (0,)), ((), ())), preferred_element_type=F32)


def split(a):
    high = a.astype(BF16)
    return high, (a - high.astype(F32)).astype(BF16)


def attend(q, a, k, v, bias):
    scale = 128 ** (-0.5)
    scores = dot_t(q, k) * scale + bias
    top = jnp.max(scores, axis=1, keepdims=True)
    expo = jnp.exp(scores - top)
    probs = expo / jnp.sum(expo, axis=1, keepdims=True)
    low = probs.astype(BF16)
    attended = dot(low, v).astype(BF16)
    value_grad = t_dot(low, a).astype(BF16)
    prob_grad = dot_t(a, v)
    inner = jnp.sum(probs * prob_grad, axis=1, keepdims=True)
    score_grad = probs * (prob_grad - inner) * scale
    high, rest = split(score_grad)
    query_grad = (dot(high, k) + dot(rest, k)).astype(BF16)
    key_grad = (t_dot(high, q) + t_dot(rest, q)).astype(BF16)
    return attended, query_grad, key_grad, value_grad


def ring_kernel(
    dec,
    enc,
    cot,
    wq,
    wk,
    wv,
    wo,
    bias,
    att_all,
    qg_all,
    kg_all,
    vg_all,
    sendb,
    recvb,
    fin,
    att,
    qg,
    kg,
    vg,
    send,
    recv,
    g_send,
    g_recv,
    own_sem,
):
    z = lax.axis_index("section")
    ahead = {"section": lax.rem(z + 1, DEPTH)}
    behind = {"section": lax.rem(z + DEPTH - 1, DEPTH)}
    greet([ahead, behind])

    def partial(d, h):
        j = d * 4 + h * 2
        blocks = pl.ds(pl.multiple_of(j * 64, 128), 128)
        stored = pl.ds(pl.multiple_of(j * 128, 256), 256)
        q = a = k = v = 0.0
        for f in range(2):
            q = q + dot(dec[f, blocks, :], wq[f])
            a = a + dot_t(cot[f, blocks, :], wo[f])
            rows = enc[f, stored, :]
            k = k + dot(rows, wk[f])
            v = v + dot(rows, wv[f])
        return ((0, 128, q), (128, 256, a), (256, 512, k), (512, 768, v))

    def stream(n):
        h = lax.rem(n, 2)
        way = lax.rem(h + lax.div(n, 2), 2)
        return h, 1 - 2 * way, 4 - lax.div(n, 2)

    def chain(n, t, sign):
        device = {"section": lax.rem(z + DEPTH + sign, DEPTH)}
        return remote(
            sendb.at[n, t], recvb.at[n, t + 1], send.at[n, t], recv.at[n, t], device
        )

    def zero(n, _):
        recvb[n, 0] = jnp.zeros((768, 256), BF16)
        return 0

    lax.fori_loop(0, 4, zero, 0)

    def item(w, _):
        n, t = lax.rem(w, 4), lax.div(w, 4)
        h, sign, length = stream(n)
        parts = partial(lax.rem(z + DEPTH + sign * (length - t), DEPTH), h)

        @pl.when(t > 0)
        def _():
            chain(n, t - 1, sign).wait_recv()

        for lo, hi, part in parts:
            sendb[n, t, lo:hi] = (part + recvb[n, t, lo:hi].astype(F32)).astype(BF16)
        chain(n, t, sign).start()
        return 0

    lax.fori_loop(0, 14, item, 0)

    def last(h, _):
        parts = partial(z, h)
        chain(h, 3, 1).wait_recv()
        chain(h + 2, 2, 1).wait_recv()
        for lo, hi, part in parts:
            total = part + recvb[h, 4, lo:hi].astype(F32) + recvb[h + 2, 3, lo:hi].astype(F32)
            fin[h, lo:hi] = total.astype(BF16)
        return 0

    lax.fori_loop(0, 2, last, 0)

    for h in range(2):
        for u in range(2):
            n = h * 2 + u
            for g in range(2):
                head = slice(g * 128, (g + 1) * 128)
                attended, query_grad, key_grad, value_grad = attend(
                    fin[h, u * 64 : (u + 1) * 64, head],
                    fin[h, 128 + u * 64 : 128 + (u + 1) * 64, head],
                    fin[h, 256 + u * 128 : 256 + (u + 1) * 128, head],
                    fin[h, 512 + u * 128 : 512 + (u + 1) * 128, head],
                    bias[pl.ds(z * 4 + n, 1), :],
                )
                att[n * 64 : (n + 1) * 64, head] = attended
                qg[n * 64 : (n + 1) * 64, head] = query_grad
                kg[n * 128 : (n + 1) * 128, head] = key_grad
                vg[n * 128 : (n + 1) * 128, head] = value_grad

    arrays = ((kg, kg_all, 1), (vg, vg_all, -1), (att, att_all, 1), (qg, qg_all, -1))

    def origin(n, j):
        return lax.rem(z + DEPTH - arrays[n][2] * j, DEPTH)

    def onward(n, j, src):
        device = ahead if arrays[n][2] == 1 else behind
        return remote(
            src, arrays[n][1].at[origin(n, j)], g_send.at[n, j], g_recv.at[n, j], device
        )

    for n in range(4):
        onward(n, 0, arrays[n][0]).start()
    for n in range(4):
        pltpu.make_async_copy(arrays[n][0], arrays[n][1].at[z], own_sem.at[n]).start()

    def step(j, _):
        for n in range(4):
            block = arrays[n][1].at[origin(n, j + 1)]
            remote(arrays[n][0], block, g_send.at[n, j], g_recv.at[n, j], ahead).wait_recv()

            @pl.when(j < DEPTH - 2)
            def _(n=n, block=block):
                onward(n, j + 1, block).start()

        return 0

    lax.fori_loop(0, DEPTH - 1, step, 0)

    def drain(j, _):
        for n in range(4):
            onward(n, j, arrays[n][0]).wait_send()
        return 0

    lax.fori_loop(0, DEPTH - 1, drain, 0)

    def drain_chain(w, _):
        chain(lax.rem(w, 4), lax.div(w, 4), 1).wait_send()
        return 0

    lax.fori_loop(0, 14, drain_chain, 0)
    for n in range(4):
        pltpu.make_async_copy(arrays[n][0], arrays[n][1].at[z], own_sem.at[n]).wait()


def ring_attention(dec, enc, cot, wq, wk, wv, wo, bias):
    sds = jax.ShapeDtypeStruct
    return pl.pallas_call(
        ring_kernel,
        out_shape=[
            sds((8, 256, 256), BF16),
            sds((8, 256, 256), BF16),
            sds((8, 512, 256), BF16),
            sds((8, 512, 256), BF16),
        ],
        in_specs=[VMEM] * 8,
        out_specs=[ANY] * 4,
        scratch_shapes=[
            pltpu.VMEM((4, 4, 768, 256), BF16),
            pltpu.VMEM((4, 5, 768, 256), BF16),
            pltpu.VMEM((2, 768, 256), BF16),
            pltpu.VMEM((256, 256), BF16),
            pltpu.VMEM((256, 256), BF16),
            pltpu.VMEM((512, 256), BF16),
            pltpu.VMEM((512, 256), BF16),
            DMA((4, 4)),
            DMA((4, 4)),
            DMA((4, 7)),
            DMA((4, 7)),
            DMA((4,)),
        ],
        compiler_params=params(2, 56),
    )(dec, enc, cot, wq, wk, wv, wo, bias)


def scatter_kernel(
    qg,
    att,
    kg,
    vg,
    wq,
    wk,
    wv,
    wo,
    wg,
    wog,
    dec_out,
    out_out,
    enc_out,
    wg_out,
    wog_out,
    sib_out,
    sib_in,
    chain_out,
    chain_in,
    s_send,
    s_recv,
    c_send,
    c_recv,
    w_send,
    w_recv,
):
    z, s, t, x, y, core = place()
    sibling = {"seq": s + 1 - 2 * core}
    partner = {"tensor": 1 - t}
    position = (ring_position(0, x, y), ring_position(1, x, y))
    greet(plane_neighbours(x, y, core, s))
    swaps = (
        remote(wg, wg_out, w_send.at[0], w_recv.at[0], partner),
        remote(wog, wog_out, w_send.at[1], w_recv.at[1], partner),
    )

    def partial(k, offset, c):
        cx, cy = ring_chip(k // 2, lax.rem(position[k // 2] + offset, RING))
        sd, td = seq_tensor(cx, cy, c)
        if k < 2:
            rows = pl.ds(pl.multiple_of(sd * 128, 128), 128)
            return dot_t(qg[rows, :], wq[td]) if k == 0 else dot(att[rows, :], wo[td])
        stored = pl.ds(pl.multiple_of(sd * 256 + (k - 2) * 128, 128), 128)
        return dot_t(kg[stored, :], wk[td]) + dot_t(vg[stored, :], wv[td])

    def across(k, i):
        return remote(
            sib_out.at[k, i], sib_in.at[k, i], s_send.at[k, i], s_recv.at[k, i], sibling
        )

    def give(i):
        offset = 8 + (1 - 2 * lax.rem(i, 2)) * lax.div(i + 1, 2)
        for k in range(4):
            sib_out[k, i] = partial(k, offset, 1 - core).astype(BF16)
            across(k, i).start()

    def onward(k, way, j):
        device = ring_device(k // 2, position[k // 2] + 1 - 2 * way, core)
        return remote(
            chain_out.at[k, way, j],
            chain_in.at[k, way, j + 1],
            c_send.at[k, way, j],
            c_recv.at[k, way, j],
            device,
        )

    for k in range(4):
        for way in range(2):
            chain_in[k, way, 0] = jnp.zeros((128, 512), BF16)

    lax.fori_loop(0, 3, lambda i, _: (give(i), 0)[1], 0)
    for copy in swaps:
        copy.start()

    def step(j, _):
        def ahead(i, _):
            @pl.when(i < RING)
            def _():
                give(i)

            return 0

        lax.fori_loop(2 * j + 3, 2 * j + 5, ahead, 0)

        def way_step(way, _):
            for k in range(4):
                length = 8 - way if k % 2 == 0 else 7 + way
                distance = length - j

                @pl.when(distance > 0)
                def _(k=k, distance=distance):
                    m = 8 - distance
                    i = jnp.maximum(2 * m - 1 + way, 0)
                    total = partial(k, RING + (1 - 2 * way) * distance, core)
                    across(k, i).wait_recv()

                    @pl.when(j > 0)
                    def _():
                        onward(k, way, j - 1).wait_recv()

                    total = total + sib_in[k, i].astype(F32)
                    total = total + chain_in[k, way, j].astype(F32)
                    chain_out[k, way, j] = total.astype(BF16)
                    onward(k, way, j).start()

            return 0

        lax.fori_loop(0, 2, way_step, 0)
        return 0

    lax.fori_loop(0, 8, step, 0)

    outs = (
        dec_out,
        out_out,
        enc_out.at[pl.ds(0, 128)],
        enc_out.at[pl.ds(128, 128)],
    )
    for k in range(4):
        total = partial(k, RING, core)
        across(k, 15).wait_recv()
        total = total + sib_in[k, 15].astype(F32)
        for way in range(2):
            length = 8 - way if k % 2 == 0 else 7 + way
            onward(k, way, length - 1).wait_recv()
            total = total + chain_in[k, way, length].astype(F32)
        outs[k][...] = total

    def drain(i, _):
        for k in range(4):
            across(k, i).wait_send()
        return 0

    lax.fori_loop(0, RING, drain, 0)

    def drain_chain(j, _):
        for k in range(4):
            for way in range(2):
                onward(k, way, j).wait_send()
        return 0

    lax.fori_loop(0, 7, drain_chain, 0)
    for k in range(4):
        onward(k, k % 2, 7).wait_send()
    for copy in swaps:
        copy.wait()


def scatter_rows(qg, att, kg, vg, wq, wk, wv, wo, wg, wog):
    sds = jax.ShapeDtypeStruct
    return pl.pallas_call(
        scatter_kernel,
        out_shape=[
            sds((128, 512), F32),
            sds((128, 512), F32),
            sds((256, 512), F32),
            sds((3, 512, 256), BF16),
            sds((256, 512), BF16),
        ],
        in_specs=[VMEM] * 8 + [ANY] * 2,
        out_specs=[VMEM] * 3 + [ANY] * 2,
        scratch_shapes=[
            pltpu.VMEM((4, 16, 128, 512), BF16),
            pltpu.VMEM((4, 16, 128, 512), BF16),
            pltpu.VMEM((4, 2, 8, 128, 512), BF16),
            pltpu.VMEM((4, 2, 9, 128, 512), BF16),
            DMA((4, 16)),
            DMA((4, 16)),
            DMA((4, 2, 8)),
            DMA((4, 2, 8)),
            DMA((2,)),
            DMA((2,)),
        ],
        compiler_params=params(3, 56),
    )(qg, att, kg, vg, wq, wk, wv, wo, wg, wog)


def pack(*vectors):
    flat = jnp.concatenate(vectors)
    return jnp.pad(flat, (0, 1024 - flat.shape[0])).reshape(8, 128)


def body(
    hidden,
    dec_gain,
    neigh_states,
    enc_gain,
    w_query,
    w_key,
    w_value,
    w_out,
    neighbour_ids,
    neighbour_len,
    cotangent,
):
    t = lax.axis_index("tensor")
    rows = hidden.shape[0]
    dec_rows = hidden.astype(F32)
    enc_rows = neigh_states.astype(F32)
    (squares,) = small_sums(
        [pack(jnp.sum(dec_rows * dec_rows, axis=1), jnp.sum(enc_rows * enc_rows, axis=1))],
        ("st",),
        0,
    )
    scales = lax.rsqrt(squares.reshape(-1)[:384] / WIDTH + EPS)
    dec_scale, enc_scale = scales[:rows, None], scales[rows:, None]
    dec_hat = dec_rows * dec_scale
    enc_hat = enc_rows * enc_scale
    dec_local = (dec_hat * dec_gain).astype(BF16)
    enc_local = (enc_hat * enc_gain).astype(BF16)
    cot_all, dec_all, enc_all, wq, wk, wv, wo = gather_rows(
        cotangent, dec_local, enc_local, w_query, w_key, w_value, w_out
    )
    count = neighbour_ids.shape[0]
    inverse = jnp.sum(
        jnp.where(
            neighbour_ids[None, :] == jnp.arange(count, dtype=jnp.int32)[:, None],
            jnp.arange(count, dtype=jnp.int32)[None, :],
            0,
        ),
        axis=1,
    )
    dec_all, cot_all = reorder(inverse, dec_all, cot_all)
    slots = jnp.arange(128, dtype=jnp.int32)[None, :]
    bias = jnp.where(slots < neighbour_len[:, None], 0.0, -jnp.inf).astype(F32)
    att, qg, kg, vg = ring_attention(dec_all, enc_all, cot_all, wq, wk, wv, wo, bias)
    att, qg = att.reshape(2048, 256), qg.reshape(2048, 256)
    kg, vg = kg.reshape(4096, 256), vg.reshape(4096, 256)
    att_rows, qg_rows = reorder(neighbour_ids, att[None], qg[None])

    def weight(left, right):
        return jnp.einsum("tnf,nh->tfh", left, right, preferred_element_type=F32)

    grads = (weight(dec_all, qg), weight(enc_all, kg), weight(enc_all, vg))
    out_grad = jnp.einsum("nh,tnf->thf", att, cot_all, preferred_element_type=F32)

    def mine(g):
        return jnp.where(t == 0, g[0], g[1])

    def other(g):
        return jnp.where(t == 0, g[1], g[0]).astype(BF16)

    dec_input, out_total, enc_input, wg, wog = scatter_rows(
        qg_rows[0],
        att_rows[0],
        kg,
        vg,
        wq,
        wk,
        wv,
        wo,
        jnp.stack([other(g) for g in grads]),
        other(out_grad),
    )

    def join(own, got, axis):
        got = got.astype(F32)
        return jnp.where(
            t == 0, jnp.concatenate([own, got], axis), jnp.concatenate([got, own], axis)
        )

    weight_grads = [join(mine(g), wg[n], 1) for n, g in enumerate(grads)]
    out_weight_grad = join(mine(out_grad), wog, 0)
    layer_out = (dec_rows + out_total).astype(BF16)
    dec_scaled = dec_gain * dec_input
    enc_scaled = enc_gain * enc_input
    inner, gains = small_sums(
        [
            pack(jnp.sum(dec_scaled * dec_hat, axis=1), jnp.sum(enc_scaled * enc_hat, axis=1)),
            pack(jnp.sum(dec_input * dec_hat, axis=0), jnp.sum(enc_input * enc_hat, axis=0)),
        ],
        ("st", "seq"),
        4,
    )
    inner = inner.reshape(-1)[:384] / WIDTH
    gains = gains.reshape(-1)
    hidden_grad = cotangent.astype(F32) + dec_scale * (
        dec_scaled - dec_hat * inner[:rows, None]
    )
    neighbour_grad = enc_scale * (enc_scaled - enc_hat * inner[rows:, None])
    return (
        layer_out,
        hidden_grad,
        neighbour_grad,
        gains[:512],
        gains[512:],
        weight_grads[0],
        weight_grads[1],
        weight_grads[2],
        out_weight_grad,
    )


def solution(mesh):
    features = ("section", "tensor")
    rows = P("seq", features)
    vector = P(features)
    columns = P(features, "seq")
    return jax.shard_map(
        body,
        mesh=mesh,
        in_specs=(
            rows,
            vector,
            rows,
            vector,
            columns,
            columns,
            columns,
            rows,
            P(),
            P(),
            rows,
        ),
        out_specs=(rows, rows, rows, vector, vector, columns, columns, columns, rows),
        check_vma=False,
    )
```

time: 1420 us -> 724 us (0.51)
  waiting for transfers between devices: 1170 us -> 0 us
  Pallas kernels: 0 us -> 686 us
  blocking collectives: 101 us -> 0 us
  local copies, waits for them, and re-layouts: 55.3 us -> 1.43 us
  matrix products: 59.7 us -> 14.5 us
    reduce_scatter x6 -> x0, waiting for transfers between devices: 731 us -> none  [the longest x1 355 us: body(): lax.psum_scatter(jnp.dot(rows, pair_weight, preferred_element_type=jnp.fl...]
    pallas_call x0 -> x7, Pallas kernels: none -> 686 us  [the longest x2 322 us: reorder(): pl.pallas_call(reorder_kernel, out_shape=[jax.ShapeDtypeStruct(a.shape, a...]
    all_gather x6 -> x0, waiting for transfers between devices: 438 us -> none  [the longest x1 186 us: body(): lax.all_gather(pair_grad, ('section', 'tensor'), axis=0, tiled=True)]
    psum x3 -> x0, blocking collectives: 101 us -> none  [the longest x1 42.4 us: body(): lax.psum((jnp.sum(dec_input * dec_hat, axis=0), jnp.sum(enc_input * enc_h...]
    gather x3 -> x0, local copies, waits for them, and re-layouts: 46.2 us -> none  [the longest x1 25.4 us: body(): pair_grad_all[back_index]]
    dot_general x15 -> x4, matrix products: 59.7 us -> 14.5 us  [the longest x3 11.9 us: weight(): return jnp.einsum('tnf,nh->tfh', left, right, preferred_element_type=F32)]
  transfers between devices with their start and end apart: 12 -> 0, of which waited for: 12 -> 0; matrix products, arithmetic and copies ran while one was open for 8% -> 0% of each run, Pallas kernels for 0% -> 0%
where the time goes in v1:
time: 724 us; the launch traced here: 723 us
  Pallas kernels  686 us (95%)
  other arithmetic  20.9 us (3%)
  matrix products  14.5 us (2%)
    pallas_call x2, Pallas kernels, reorder(): pl.pallas_call(reorder_kernel, out_shape=[jax.ShapeDtypeStruct(a.shape, a...  322 us
    pallas_call x1, Pallas kernels, ring_attention(): pl.pallas_call(ring_kernel, out_shape=[sds((8, 256, 256), BF16), sds((8,...  140 us
    pallas_call x1, Pallas kernels, gather_rows(): pl.pallas_call(gather_kernel, out_shape=[sds((2, 2048, 512), BF16), sds((...  104 us
    pallas_call x1, Pallas kernels, scatter_rows(): pl.pallas_call(scatter_kernel, out_shape=[sds((128, 512), F32), sds((128,...  86.4 us
    pallas_call x2, Pallas kernels, small_sums(): pl.pallas_call(functools.partial(small_kernel, groups), out_shape=[jax.Sh...  32.7 us

profile of v1, /device:TPU:1, one launch (start us, length us, event | category | flops | bytes accessed | tf_op | source)
XLA Modules:
  0.0 723.4 jit_solution(12945699344623515147)
XLA Ops:
  0.6 1.1 fusion.9
  1.7 1.0 fusion.20
  2.7 0.6 fusion.25.refs_0_
  3.3 13.8 %shard_map.178 = f32[8,128]{1,0:T(8,128)} custom-call(f32[8,128]{1,0:T(8,128)} %fusion.25.refs_0_), custom_call_target="tpu_custom_call" | custom-call | tf_op jit(solution)/shard_map/pallas_call | solution.py:153
  17.2 0.7 add_rsqrt_fusion
  17.8 1.8 fusion.4.enc
  19.6 1.7 fusion.14.dec
  21.3 104.1 %shard_map.179 = (bf16[2,2048,512]{2,1,0:T(8,128)(2,1)}, bf16[2,2048,512]{2,1,0:T(8,128)(2,1)}, bf16[2,4096,512]{2,1,0:T(8,128)(2,1)}, bf16[2,512,256]{2,1,0:T(8...) custom-call(bf16[128,512]{1,0:T(8,128)(2,1)} %cot.1, ...), custom_call_target="tpu_custom_call" | custom-call | tf_op jit(solution)/shard_map/pallas_call | solution.py:290
  125.4 1.3 select_reduce_fusion.index
  126.6 256.6 %shard_map.180 = (bf16[2,2048,512]{2,1,0:T(8,128)(2,1)}, bf16[2,2048,512]{2,1,0:T(8,128)(2,1)}) custom-call(s32[32]{0:T(128)} %select_reduce_fusion.index, bf16[2,2048,512]{2,1,0:T(8,128)(2,1)} %get-tuple-element.31.refs_0_, bf16[2,2048,512]{2,1,0:T(8,128)(2,1)} %get-tuple-element.32.refs_1_), custom_call_target="tpu_custom_call" | custom-call | tf_op jit(solution)/shard_map/pallas_call | solution.py:342
  383.2 0.7 fusion.23.bias
  383.9 140.0 %shard_map.181 = (bf16[8,256,256]{2,1,0:T(8,128)(2,1)}, bf16[8,256,256]{2,1,0:T(8,128)(2,1)}, bf16[8,512,256]{2,1,0:T(8,128)(2,1)}, bf16[8,512,256]{2,1,0:T(8,128)(2,1)}) custom-call(bf16[2,2048,512]{2,1,0:T(8,128)(2,1)} %get-tuple-element.33.dec, bf16[2,4096,512]{2,1,0:T(8,128)(2,1)} %get-tuple-element.34.enc, bf16[2,2048,512]{2,1,0:T(8,128)(2,1)} %get-tuple-element.35.cot, ...), custom_call_target="tpu_custom_call" | custom-call | tf_op jit(solution)/shard_map/pallas_call | solution.py:538
  524.0 2.6 convolution_bitcast_fusion
  526.6 0.0 copy-start.4
  526.6 0.8 fusion.22.wog
  527.5 3.6 fusion.26
  531.1 0.1 select_convert_fusion.3
  531.2 0.0 copy-done
  531.2 0.0 slice-start.1
  531.2 5.9 fusion.27
  537.1 0.1 select_convert_fusion.2
  537.2 2.4 fusion.28
  539.6 0.1 select_convert_fusion.1
  539.6 1.0 pad_maximum_fusion.wg
  540.6 65.9 %shard_map.182 = (bf16[1,2048,256]{2,1,0:T(8,128)(2,1)}, bf16[1,2048,256]{2,1,0:T(8,128)(2,1)}) custom-call(s32[32]{0:T(128)} %index.1, bf16[1,2048,256]{2,1,0:T(8,128)(2,1)} %bitcast.72, bf16[1,2048,256]{2,1,0:T(8,128)(2,1)} %bitcast.73), custom_call_target="tpu_custom_call" | custom-call | tf_op jit(solution)/shard_map/pallas_call | solution.py:342
  606.5 0.0 copy-start.5
  606.5 86.4 %shard_map.183 = (f32[128,512]{1,0:T(8,128)}, f32[128,512]{1,0:T(8,128)}, f32[256,512]{1,0:T(8,128)}, bf16[3,512,256]{2,1,0:T(8,128)(2,1)}, bf16[256,512]{1,0:T(8,128)(2,1)}) custom-call(bf16[2048,256]{1,0:T(8,128)(2,1)} %bitcast.70, bf16[2048,256]{1,0:T(8,128)(2,1)} %bitcast.69, bf16[4096,256]{1,0:T(8,128)(2,1)} %bitcast.65, bf16[4096,256]{1,0:T(8,128)(2,1)} %bitcast.67, ...), custom_call_target="tpu_custom_call" | custom-call | tf_op jit(solution)/shard_map/pallas_call | solution.py:717
  692.9 1.2 bitcast_convert_fusion
  694.1 1.0 convert_element_type.76
  695.2 0.1 select_bitcast_fusion
  695.2 0.1 select_bitcast_fusion.1
  695.3 1.7 maximum_select_fusion.2
  697.0 0.0 copy-start.6
  697.0 0.0 copy-start.13
  697.0 0.1 select_bitcast_fusion.3
  697.1 0.0 copy-start.7
  697.1 0.0 copy-start.11
  697.1 0.1 select_bitcast_fusion.2
  697.2 1.7 maximum_select_fusion
  698.9 0.2 fusion.16
  699.1 0.3 fusion.6
  699.4 0.6 pad_maximum_fusion.1.refs_1_
  700.0 0.6 fusion.24.refs_0_
  700.6 18.9 %shard_map.184 = (f32[8,128]{1,0:T(8,128)}, f32[8,128]{1,0:T(8,128)}) custom-call(f32[8,128]{1,0:T(8,128)} %fusion.24.refs_0_, f32[8,128]{1,0:T(8,128)} %pad_maximum_fusion.1.refs_1_), custom_call_target="tpu_custom_call" | custom-call | tf_op jit(solution)/shard_map/pallas_call | solution.py:153
  719.5 0.7 slice_multiply_fusion
  720.2 1.0 fusion.8
  721.2 0.9 fusion.19
  722.1 1.3 slice_bitcast_fusion
  (33 shorter events, 0.1 us)
Async XLA Ops:
  126.6 256.6 %copy-start.15 = (s32[32]{0:T(128)S(1)}, s32[32]{0:T(128)}, u32[]{:S(2)}) copy-start(s32[32]{0:T(128)} %param.20) | copy-start | bytes 388
  383.9 140.0 %copy-start.3 = (bf16[2,2048,512]{2,1,0:T(8,128)(2,1)S(1)}, bf16[2,2048,512]{2,1,0:T(8,128)(2,1)}, u32[]{:S(2)}) copy-start(bf16[2,2048,512]{2,1,0:T(8,128)(2,1)} %get-tuple-element.35.cot) | copy-start | bytes 12582916
  524.0 3.5 copy-start.9
  526.6 4.5 copy-start.4
  527.5 3.7 copy-start
  527.5 9.7 %slice-start = ((s8[8388608]{0:T(1024)(128)(4,1)}), s8[4194304]{0:T(1024)(128)(4,1)S(1)}, s32[]{:S(2)}) async-start(s8[8388608]{0:T(1024)(128)(4,1)} %bitcast.63), calls=%async_computation | async-start | bytes 8388608
  531.2 6.0 slice-start.1
  531.2 6.0 copy-start.1
  606.5 88.7 %copy-start.5 = (f32[2,256,512]{2,1,0:T(8,128)S(1)}, f32[2,256,512]{2,1,0:T(8,128)}, u32[]{:S(2)}) copy-start(f32[2,256,512]{2,1,0:T(8,128)} %copy-done.4) | copy-start | bytes 3145732
  697.0 1.9 copy-start.8
  697.0 1.9 copy-start.10
  697.0 1.9 copy-start.14
  697.0 2.1 copy-start.2
  697.0 2.1 copy-start.6
  697.0 2.1 copy-start.13
  697.1 23.1 %copy-start.7 = (f32[256,512]{1,0:T(8,128)S(1)}, f32[256,512]{1,0:T(8,128)}, u32[]{:S(2)}) copy-start(f32[256,512]{1,0:T(8,128)} %get-tuple-element.48) | copy-start | bytes 1572868
  697.1 24.1 %copy-start.11 = (bf16[128,512]{1,0:T(8,128)(2,1)S(1)}, bf16[128,512]{1,0:T(8,128)(2,1)}, u32[]{:S(2)}) copy-start(bf16[128,512]{1,0:T(8,128)(2,1)} %cot.1) | copy-start | bytes 393220
  697.1 24.1 %copy-start.12 = (f32[128,512]{1,0:T(8,128)S(1)}, f32[128,512]{1,0:T(8,128)}, u32[]{:S(2)}) copy-start(f32[128,512]{1,0:T(8,128)} %get-tuple-element.46) | copy-start | bytes 786436

commit v2 on v1

--- a/solution.py
+++ b/solution.py
@@ -160,181 +160,17 @@
     )(*arrays)
 
 
-def gather_kernel(
-    cot,
-    dec,
-    enc,
-    wq,
-    wk,
-    wv,
-    wo,
-    cot_all,
-    dec_all,
-    enc_all,
-    wq_all,
-    wk_all,
-    wv_all,
-    wo_all,
-    send,
-    recv,
-    sib_send,
-    sib_recv,
-    own_sem,
-    w_send,
-    w_recv,
-    w_own,
-):
-    z, s, t, x, y, core = place()
-    sibling = {"seq": s + 1 - 2 * core}
-    partner = {"tensor": 1 - t}
-    greet(plane_neighbours(x, y, core, s))
-
-    def slot(k, chip, c):
-        so, to = seq_tensor(chip[0], chip[1], c)
-        if k == 0:
-            return cot_all.at[to, pl.ds(pl.multiple_of(so * 128, 128), 128)]
-        if k == 1:
-            return dec_all.at[to, pl.ds(pl.multiple_of(so * 128, 128), 128)]
-        return enc_all.at[to, pl.ds(pl.multiple_of(so * 256 + (k - 2) * 128, 128), 128)]
-
-    sources = (cot, dec, enc.at[pl.ds(0, 128)], enc.at[pl.ds(128, 128)])
-    position = (ring_position(0, x, y), ring_position(1, x, y))
-
-    def origin(k, j):
-        sign = 1 - 2 * (k % 2)
-        return ring_chip(k // 2, lax.rem(position[k // 2] + RING - sign * j, RING))
-
-    def onward(k, j, src):
-        sign = 1 - 2 * (k % 2)
-        device = ring_device(k // 2, position[k // 2] + sign, core)
-        return remote(src, slot(k, origin(k, j), core), send.at[k, j], recv.at[k, j], device)
-
-    def across(k, j, src):
-        return remote(
-            src, slot(k, origin(k, j), core), sib_send.at[k, j], sib_recv.at[k, j], sibling
-        )
-
-    for k in range(4):
-        onward(k, 0, sources[k]).start()
-    half = pl.ds(pl.multiple_of(t * 256, 256), 256)
-    rest = pl.ds(pl.multiple_of((1 - t) * 256, 256), 256)
-    weights = ((wq, wq_all), (wk, wk_all), (wv, wv_all))
-    swaps = [
-        remote(w.at[:, rest], w_all.at[t], w_send.at[n], w_recv.at[n], partner)
-        for n, (w, w_all) in enumerate(weights)
-    ] + [remote(wo.at[rest, :], wo_all.at[t], w_send.at[3], w_recv.at[3], partner)]
-    keeps = [
-        pltpu.make_async_copy(w.at[:, half], w_all.at[t], w_own.at[n])
-        for n, (w, w_all) in enumerate(weights)
-    ] + [pltpu.make_async_copy(wo.at[half, :], wo_all.at[t], w_own.at[3])]
-    for copy in swaps:
-        copy.start()
-    for k in range(4):
-        across(k, 0, sources[k]).start()
-        pltpu.make_async_copy(sources[k], slot(k, (x, y), core), own_sem.at[k]).start()
-    for copy in keeps:
-        copy.start()
-
-    def step(j, _):
-        for k in range(4):
-            remote(
-                sources[k],
-                slot(k, origin(k, j + 1), core),
-                send.at[k, j],
-                recv.at[k, j],
-                sibling,
-            ).wait_recv()
-            block = slot(k, origin(k, j + 1), core)
-
-            @pl.when(j < RING - 2)
-            def _(k=k, block=block):
-                onward(k, j + 1, block).start()
-
-            across(k, j + 1, block).start()
-        return 0
-
-    lax.fori_loop(0, RING - 1, step, 0)
-
-    for k in range(4):
-        pltpu.make_async_copy(sources[k], slot(k, (x, y), core), own_sem.at[k]).wait()
-
-    def finish(j, _):
-        for k in range(4):
-            remote(
-                sources[k],
-                slot(k, origin(k, j), 1 - core),
-                sib_send.at[k, j],
-                sib_recv.at[k, j],
-                sibling,
-            ).wait_recv()
-            across(k, j, sources[k]).wait_send()
-
-            @pl.when(j < RING - 1)
-            def _(k=k):
-                onward(k, j, sources[k]).wait_send()
-
-        return 0
-
-    lax.fori_loop(0, RING, finish, 0)
-    for copy in keeps:
-        copy.wait()
-    for copy in swaps:
-        copy.wait_send()
-    for n, (w, w_all) in enumerate(weights):
-        remote(w.at[:, rest], w_all.at[1 - t], w_send.at[n], w_recv.at[n], partner).wait_recv()
-    remote(wo.at[rest, :], wo_all.at[1 - t], w_send.at[3], w_recv.at[3], partner).wait_recv()
-
-
-def gather_rows(cot, dec, enc, wq, wk, wv, wo):
-    sds = jax.ShapeDtypeStruct
-    return pl.pallas_call(
-        gather_kernel,
-        out_shape=[
-            sds((2, 2048, 512), BF16),
-            sds((2, 2048, 512), BF16),
-            sds((2, 4096, 512), BF16),
-            sds((2, 512, 256), BF16),
-            sds((2, 512, 256), BF16),
-            sds((2, 512, 256), BF16),
-            sds((2, 256, 512), BF16),
-        ],
-        in_specs=[ANY] * 7,
-        out_specs=[ANY] * 7,
-        scratch_shapes=[
-            DMA((4, 15)),
-            DMA((4, 15)),
-            DMA((4, 16)),
-            DMA((4, 16)),
-            DMA((4,)),
-            DMA((4,)),
-            DMA((4,)),
-            DMA((4,)),
-        ],
-        compiler_params=params(1),
-    )(cot, dec, enc, wq, wk, wv, wo)
-
-
 def reorder_kernel(index, *refs):
     n = len(refs) // 2
-    ins, outs, sem = refs[:n], refs[n : 2 * n], refs[2 * n]
-
-    def copy(j, k):
+
+    def move(j, _):
         src = pl.ds(pl.multiple_of(index[j] * 64, 64), 64)
         dst = pl.ds(pl.multiple_of(j * 64, 64), 64)
-        return pltpu.make_async_copy(ins[k].at[:, src], outs[k].at[:, dst], sem.at[k, j])
-
-    def start(j, _):
         for k in range(n):
-            copy(j, k).start()
-        return 0
-
-    def wait(j, _):
-        for k in range(n):
-            copy(j, k).wait()
-        return 0
-
-    lax.fori_loop(0, 32, start, 0)
-    lax.fori_loop(0, 32, wait, 0)
+            refs[n + k][dst, :] = refs[k][src, :]
+        return 0
+
+    lax.fori_loop(0, 32, move, 0)
 
 
 def reorder(index, *arrays):
@@ -342,9 +178,8 @@
     return pl.pallas_call(
         reorder_kernel,
         out_shape=[jax.ShapeDtypeStruct(a.shape, a.dtype) for a in arrays],
-        in_specs=[SMEM] + [ANY] * n,
-        out_specs=[ANY] * n,
-        scratch_shapes=[DMA((n, 32))],
+        in_specs=[SMEM] + [VMEM] * n,
+        out_specs=[VMEM] * n,
     )(index, *arrays)
 
 
@@ -383,46 +218,181 @@
     return attended, query_grad, key_grad, value_grad
 
 
-def ring_kernel(
+def hops(k, way):
+    return 8 - way if k % 2 == 0 else 7 + way
+
+
+def front_kernel(
+    cot,
     dec,
     enc,
-    cot,
+    wq_own,
+    wk_own,
+    wv_own,
+    wo_own,
+    bias,
+    inverse,
+    cot_all,
+    dec_all,
+    enc_all,
     wq,
     wk,
     wv,
     wo,
-    bias,
     att_all,
     qg_all,
     kg_all,
     vg_all,
+    cot_v,
+    dec_v,
+    enc_v,
     sendb,
     recvb,
     fin,
-    att,
-    qg,
-    kg,
-    vg,
+    p_send,
+    p_recv,
+    s_send,
+    s_recv,
+    own_sem,
+    w_send,
+    w_recv,
+    w_own,
+    out_sem,
     send,
     recv,
     g_send,
     g_recv,
-    own_sem,
 ):
-    z = lax.axis_index("section")
+    z, s, t, x, y, core = place()
+    sibling = {"seq": s + 1 - 2 * core}
+    partner = {"tensor": 1 - t}
     ahead = {"section": lax.rem(z + 1, DEPTH)}
     behind = {"section": lax.rem(z + DEPTH - 1, DEPTH)}
-    greet([ahead, behind])
+    greet(plane_neighbours(x, y, core, s) + [ahead, behind])
+
+
+    def slot(k, chip, c):
+        so, to = seq_tensor(chip[0], chip[1], c)
+        if k == 0:
+            return cot_v.at[to, pl.ds(so * 2, 2)]
+        if k == 1:
+            return dec_v.at[to, pl.ds(so * 2, 2)]
+        return enc_v.at[to, pl.ds(pl.multiple_of(so * 256 + (k - 2) * 128, 128), 128)]
+
+    sources = (cot, dec, enc.at[pl.ds(0, 128)], enc.at[pl.ds(128, 128)])
+    position = (ring_position(0, x, y), ring_position(1, x, y))
+
+    def origin(k, way, j):
+        return ring_chip(
+            k // 2, lax.rem(position[k // 2] + RING - (1 - 2 * way) * j, RING)
+        )
+
+    def onward(k, way, j, src):
+        device = ring_device(k // 2, position[k // 2] + 1 - 2 * way, core)
+        block = slot(k, origin(k, way, j), core)
+        return remote(src, block, p_send.at[k, way, j], p_recv.at[k, way, j], device)
+
+    def arrival(k, way, j):
+        block = slot(k, origin(k, way, j + 1), core)
+        return remote(block, block, p_send.at[k, way, j], p_recv.at[k, way, j], sibling), block
+
+    def across(k, way, j, src, c):
+        block = slot(k, origin(k, way, j), c)
+        return remote(src, block, s_send.at[k, way, j], s_recv.at[k, way, j], sibling)
+
+    def keep(k):
+        return pltpu.make_async_copy(sources[k], slot(k, (x, y), core), own_sem.at[k])
+
+    for k in range(4):
+        for way in range(2):
+            onward(k, way, 0, sources[k]).start()
+    half = pl.ds(pl.multiple_of(t * 256, 256), 256)
+    rest = pl.ds(pl.multiple_of((1 - t) * 256, 256), 256)
+    weights = ((wq_own, wq), (wk_own, wk), (wv_own, wv))
+    swaps = [
+        remote(w.at[:, rest], w_all.at[t], w_send.at[n], w_recv.at[n], partner)
+        for n, (w, w_all) in enumerate(weights)
+    ] + [remote(wo_own.at[rest, :], wo.at[t], w_send.at[3], w_recv.at[3], partner)]
+    keeps = [
+        pltpu.make_async_copy(w.at[:, half], w_all.at[t], w_own.at[n])
+        for n, (w, w_all) in enumerate(weights)
+    ] + [pltpu.make_async_copy(wo_own.at[half, :], wo.at[t], w_own.at[3])]
+    for copy in swaps:
+        copy.start()
+    for k in range(4):
+        across(k, 0, 0, sources[k], core).start()
+        keep(k).start()
+    for copy in keeps:
+        copy.start()
+
+    def gather_step(j, _):
+        for way in range(2):
+            for k in range(4):
+
+                @pl.when(j < hops(k, way))
+                def _(k=k, way=way):
+                    wait, block = arrival(k, way, j)
+                    wait.wait_recv()
+
+                    @pl.when(j + 1 < hops(k, way))
+                    def _():
+                        onward(k, way, j + 1, block).start()
+
+                    across(k, way, j + 1, block, core).start()
+
+        return 0
+
+    lax.fori_loop(0, 8, gather_step, 0)
+
+    def zero(n, _):
+        recvb[n, 0] = jnp.zeros((768, 256), BF16)
+        return 0
+
+    lax.fori_loop(0, 4, zero, 0)
+
+    def gather_end(j, _):
+        for way in range(2):
+            for k in range(4):
+
+                @pl.when(j < hops(k, way))
+                def _(k=k, way=way):
+                    onward(k, way, j, sources[k]).wait_send()
+                    across(k, way, j + 1, sources[k], core).wait_send()
+                    across(k, way, j + 1, sources[k], 1 - core).wait_recv()
+
+        return 0
+
+    lax.fori_loop(0, 8, gather_end, 0)
+    for k in range(4):
+        across(k, 0, 0, sources[k], core).wait_send()
+        across(k, 0, 0, sources[k], 1 - core).wait_recv()
+        keep(k).wait()
+    for copy in keeps:
+        copy.wait()
+    for copy in swaps:
+        copy.wait_send()
+    for n, (w, w_all) in enumerate(weights):
+        remote(w.at[:, rest], w_all.at[1 - t], w_send.at[n], w_recv.at[n], partner).wait_recv()
+    remote(wo_own.at[rest, :], wo.at[1 - t], w_send.at[3], w_recv.at[3], partner).wait_recv()
+    stores = [
+        pltpu.make_async_copy(src, dst, out_sem.at[n])
+        for n, (src, dst) in enumerate(((cot_v, cot_all), (dec_v, dec_all), (enc_v, enc_all)))
+    ]
+    for copy in stores:
+        copy.start()
+
 
     def partial(d, h):
         j = d * 4 + h * 2
-        blocks = pl.ds(pl.multiple_of(j * 64, 128), 128)
+        b0, b1 = inverse[j], inverse[j + 1]
         stored = pl.ds(pl.multiple_of(j * 128, 256), 256)
         q = a = k = v = 0.0
         for f in range(2):
-            q = q + dot(dec[f, blocks, :], wq[f])
-            a = a + dot_t(cot[f, blocks, :], wo[f])
-            rows = enc[f, stored, :]
+            rows = jnp.concatenate([dec_v[f, b0], dec_v[f, b1]], axis=0)
+            q = q + dot(rows, wq[f])
+            rows = jnp.concatenate([cot_v[f, b0], cot_v[f, b1]], axis=0)
+            a = a + dot_t(rows, wo[f])
+            rows = enc_v[f, stored, :]
             k = k + dot(rows, wk[f])
             v = v + dot(rows, wv[f])
         return ((0, 128, q), (128, 256, a), (256, 512, k), (512, 768, v))
@@ -437,12 +407,6 @@
         return remote(
             sendb.at[n, t], recvb.at[n, t + 1], send.at[n, t], recv.at[n, t], device
         )
-
-    def zero(n, _):
-        recvb[n, 0] = jnp.zeros((768, 256), BF16)
-        return 0
-
-    lax.fori_loop(0, 4, zero, 0)
 
     def item(w, _):
         n, t = lax.rem(w, 4), lax.div(w, 4)
@@ -483,84 +447,95 @@
                     fin[h, 512 + u * 128 : 512 + (u + 1) * 128, head],
                     bias[pl.ds(z * 4 + n, 1), :],
                 )
-                att[n * 64 : (n + 1) * 64, head] = attended
-                qg[n * 64 : (n + 1) * 64, head] = query_grad
-                kg[n * 128 : (n + 1) * 128, head] = key_grad
-                vg[n * 128 : (n + 1) * 128, head] = value_grad
-
-    arrays = ((kg, kg_all, 1), (vg, vg_all, -1), (att, att_all, 1), (qg, qg_all, -1))
-
-    def origin(n, j):
-        return lax.rem(z + DEPTH - arrays[n][2] * j, DEPTH)
-
-    def onward(n, j, src):
-        device = ahead if arrays[n][2] == 1 else behind
-        return remote(
-            src, arrays[n][1].at[origin(n, j)], g_send.at[n, j], g_recv.at[n, j], device
-        )
+                att_all[z, n * 64 : (n + 1) * 64, head] = attended
+                qg_all[z, n * 64 : (n + 1) * 64, head] = query_grad
+                kg_all[z, n * 128 : (n + 1) * 128, head] = key_grad
+                vg_all[z, n * 128 : (n + 1) * 128, head] = value_grad
+
+    arrays = ((kg_all, 1), (vg_all, -1), (att_all, 1), (qg_all, -1))
+
+    def ring_block(n, j):
+        return arrays[n][0].at[lax.rem(z + DEPTH - arrays[n][1] * j, DEPTH)]
+
+    def ring_copy(n, j):
+        device = ahead if arrays[n][1] == 1 else behind
+        block = ring_block(n, j)
+        return remote(block, block, g_send.at[n, j], g_recv.at[n, j], device)
 
     for n in range(4):
-        onward(n, 0, arrays[n][0]).start()
-    for n in range(4):
-        pltpu.make_async_copy(arrays[n][0], arrays[n][1].at[z], own_sem.at[n]).start()
-
-    def step(j, _):
+        ring_copy(n, 0).start()
+
+    def ring_step(j, _):
         for n in range(4):
-            block = arrays[n][1].at[origin(n, j + 1)]
-            remote(arrays[n][0], block, g_send.at[n, j], g_recv.at[n, j], ahead).wait_recv()
+            block = ring_block(n, j + 1)
+            remote(block, block, g_send.at[n, j], g_recv.at[n, j], ahead).wait_recv()
 
             @pl.when(j < DEPTH - 2)
-            def _(n=n, block=block):
-                onward(n, j + 1, block).start()
-
-        return 0
-
-    lax.fori_loop(0, DEPTH - 1, step, 0)
-
-    def drain(j, _):
+            def _(n=n):
+                ring_copy(n, j + 1).start()
+
+        return 0
+
+    lax.fori_loop(0, DEPTH - 1, ring_step, 0)
+
+    def ring_end(j, _):
         for n in range(4):
-            onward(n, j, arrays[n][0]).wait_send()
-        return 0
-
-    lax.fori_loop(0, DEPTH - 1, drain, 0)
-
-    def drain_chain(w, _):
+            ring_copy(n, j).wait_send()
+        return 0
+
+    lax.fori_loop(0, DEPTH - 1, ring_end, 0)
+
+    def chain_end(w, _):
         chain(lax.rem(w, 4), lax.div(w, 4), 1).wait_send()
         return 0
 
-    lax.fori_loop(0, 14, drain_chain, 0)
-    for n in range(4):
-        pltpu.make_async_copy(arrays[n][0], arrays[n][1].at[z], own_sem.at[n]).wait()
-
-
-def ring_attention(dec, enc, cot, wq, wk, wv, wo, bias):
+    lax.fori_loop(0, 14, chain_end, 0)
+    for copy in stores:
+        copy.wait()
+
+
+def front(cot, dec, enc, wq, wk, wv, wo, bias, inverse):
     sds = jax.ShapeDtypeStruct
     return pl.pallas_call(
-        ring_kernel,
+        front_kernel,
         out_shape=[
+            sds((2, 32, 64, 512), BF16),
+            sds((2, 32, 64, 512), BF16),
+            sds((2, 4096, 512), BF16),
+            sds((2, 512, 256), BF16),
+            sds((2, 512, 256), BF16),
+            sds((2, 512, 256), BF16),
+            sds((2, 256, 512), BF16),
             sds((8, 256, 256), BF16),
             sds((8, 256, 256), BF16),
             sds((8, 512, 256), BF16),
             sds((8, 512, 256), BF16),
         ],
-        in_specs=[VMEM] * 8,
-        out_specs=[ANY] * 4,
+        in_specs=[VMEM] * 8 + [SMEM],
+        out_specs=[ANY] * 3 + [VMEM] * 8,
         scratch_shapes=[
+            pltpu.VMEM((2, 32, 64, 512), BF16),
+            pltpu.VMEM((2, 32, 64, 512), BF16),
+            pltpu.VMEM((2, 4096, 512), BF16),
             pltpu.VMEM((4, 4, 768, 256), BF16),
             pltpu.VMEM((4, 5, 768, 256), BF16),
             pltpu.VMEM((2, 768, 256), BF16),
-            pltpu.VMEM((256, 256), BF16),
-            pltpu.VMEM((256, 256), BF16),
-            pltpu.VMEM((512, 256), BF16),
-            pltpu.VMEM((512, 256), BF16),
+            DMA((4, 2, 8)),
+            DMA((4, 2, 8)),
+            DMA((4, 2, 9)),
+            DMA((4, 2, 9)),
+            DMA((4,)),
+            DMA((4,)),
+            DMA((4,)),
+            DMA((4,)),
+            DMA((3,)),
             DMA((4, 4)),
             DMA((4, 4)),
             DMA((4, 7)),
             DMA((4, 7)),
-            DMA((4,)),
         ],
-        compiler_params=params(2, 56),
-    )(dec, enc, cot, wq, wk, wv, wo, bias)
+        compiler_params=params(1, 60),
+    )(cot, dec, enc, wq, wk, wv, wo, bias, inverse)
 
 
 def scatter_kernel(
@@ -583,6 +558,7 @@
     sib_in,
     chain_out,
     chain_in,
+    mine,
     s_send,
     s_recv,
     c_send,
@@ -600,14 +576,14 @@
         remote(wog, wog_out, w_send.at[1], w_recv.at[1], partner),
     )
 
-    def partial(k, offset, c):
-        cx, cy = ring_chip(k // 2, lax.rem(position[k // 2] + offset, RING))
-        sd, td = seq_tensor(cx, cy, c)
-        if k < 2:
-            rows = pl.ds(pl.multiple_of(sd * 128, 128), 128)
-            return dot_t(qg[rows, :], wq[td]) if k == 0 else dot(att[rows, :], wo[td])
-        stored = pl.ds(pl.multiple_of(sd * 256 + (k - 2) * 128, 128), 128)
-        return dot_t(kg[stored, :], wk[td]) + dot_t(vg[stored, :], wv[td])
+    def both(ref, sd, size):
+        return jnp.concatenate(
+            [
+                ref[pl.ds(pl.multiple_of((sd + c) * size, 128), size), :]
+                for c in (core, 1 - core)
+            ],
+            axis=0,
+        )
 
     def across(k, i):
         return remote(
@@ -616,9 +592,22 @@
 
     def give(i):
         offset = 8 + (1 - 2 * lax.rem(i, 2)) * lax.div(i + 1, 2)
-        for k in range(4):
-            sib_out[k, i] = partial(k, offset, 1 - core).astype(BF16)
+        place_of = lax.rem(i, 8)
+        cx, cy = ring_chip(0, lax.rem(position[0] + offset, RING))
+        sd, td = seq_tensor(cx, cy, 0)
+        for k, rows, w in ((0, qg, wq), (1, att, wo)):
+            total = dot(both(rows, sd, 128), w[td])
+            sib_out[k, i] = total[128:].astype(BF16)
             across(k, i).start()
+            mine[k, place_of] = total[:128]
+        cx, cy = ring_chip(1, lax.rem(position[1] + offset, RING))
+        sd, td = seq_tensor(cx, cy, 0)
+        total = dot(both(kg, sd, 256), wk[td]) + dot(both(vg, sd, 256), wv[td])
+        for k in (2, 3):
+            lo = (k - 2) * 128
+            sib_out[k, i] = total[256 + lo : 384 + lo].astype(BF16)
+            across(k, i).start()
+            mine[k, place_of] = total[lo : 128 + lo]
 
     def onward(k, way, j):
         device = ring_device(k // 2, position[k // 2] + 1 - 2 * way, core)
@@ -657,14 +646,13 @@
                 def _(k=k, distance=distance):
                     m = 8 - distance
                     i = jnp.maximum(2 * m - 1 + way, 0)
-                    total = partial(k, RING + (1 - 2 * way) * distance, core)
                     across(k, i).wait_recv()
 
                     @pl.when(j > 0)
                     def _():
                         onward(k, way, j - 1).wait_recv()
 
-                    total = total + sib_in[k, i].astype(F32)
+                    total = mine[k, lax.rem(i, 8)] + sib_in[k, i].astype(F32)
                     total = total + chain_in[k, way, j].astype(F32)
                     chain_out[k, way, j] = total.astype(BF16)
                     onward(k, way, j).start()
@@ -683,9 +671,8 @@
         enc_out.at[pl.ds(128, 128)],
     )
     for k in range(4):
-        total = partial(k, RING, core)
         across(k, 15).wait_recv()
-        total = total + sib_in[k, 15].astype(F32)
+        total = mine[k, 7] + sib_in[k, 15].astype(F32)
         for way in range(2):
             length = 8 - way if k % 2 == 0 else 7 + way
             onward(k, way, length - 1).wait_recv()
@@ -730,6 +717,7 @@
             pltpu.VMEM((4, 16, 128, 512), BF16),
             pltpu.VMEM((4, 2, 8, 128, 512), BF16),
             pltpu.VMEM((4, 2, 9, 128, 512), BF16),
+            pltpu.VMEM((4, 8, 128, 512), F32),
             DMA((4, 16)),
             DMA((4, 16)),
             DMA((4, 2, 8)),
@@ -737,7 +725,7 @@
             DMA((2,)),
             DMA((2,)),
         ],
-        compiler_params=params(3, 56),
+        compiler_params=params(2, 60),
     )(qg, att, kg, vg, wq, wk, wv, wo, wg, wog)
 
 
@@ -774,9 +762,6 @@
     enc_hat = enc_rows * enc_scale
     dec_local = (dec_hat * dec_gain).astype(BF16)
     enc_local = (enc_hat * enc_gain).astype(BF16)
-    cot_all, dec_all, enc_all, wq, wk, wv, wo = gather_rows(
-        cotangent, dec_local, enc_local, w_query, w_key, w_value, w_out
-    )
     count = neighbour_ids.shape[0]
     inverse = jnp.sum(
         jnp.where(
@@ -786,13 +771,23 @@
         ),
         axis=1,
     )
-    dec_all, cot_all = reorder(inverse, dec_all, cot_all)
     slots = jnp.arange(128, dtype=jnp.int32)[None, :]
     bias = jnp.where(slots < neighbour_len[:, None], 0.0, -jnp.inf).astype(F32)
-    att, qg, kg, vg = ring_attention(dec_all, enc_all, cot_all, wq, wk, wv, wo, bias)
+    cot_all, dec_all, enc_all, wq, wk, wv, wo, att, qg, kg, vg = front(
+        cotangent.reshape(2, 64, 512),
+        dec_local.reshape(2, 64, 512),
+        enc_local,
+        w_query,
+        w_key,
+        w_value,
+        w_out,
+        bias,
+        inverse,
+    )
+    cot_all, dec_all = cot_all.reshape(2, 2048, 512), dec_all.reshape(2, 2048, 512)
     att, qg = att.reshape(2048, 256), qg.reshape(2048, 256)
     kg, vg = kg.reshape(4096, 256), vg.reshape(4096, 256)
-    att_rows, qg_rows = reorder(neighbour_ids, att[None], qg[None])
+    att, qg = reorder(neighbour_ids, att, qg)
 
     def weight(left, right):
         return jnp.einsum("tnf,nh->tfh", left, right, preferred_element_type=F32)
@@ -807,13 +802,13 @@
         return jnp.where(t == 0, g[1], g[0]).astype(BF16)
 
     dec_input, out_total, enc_input, wg, wog = scatter_rows(
-        qg_rows[0],
-        att_rows[0],
+        qg,
+        att,
         kg,
         vg,
-        wq,
-        wk,
-        wv,
+        jnp.swapaxes(wq, 1, 2),
+        jnp.swapaxes(wk, 1, 2),
+        jnp.swapaxes(wv, 1, 2),
         wo,
         jnp.stack([other(g) for g in grads]),
         other(out_grad),
@@ -836,7 +831,7 @@
             pack(jnp.sum(dec_input * dec_hat, axis=0), jnp.sum(enc_input * enc_hat, axis=0)),
         ],
         ("st", "seq"),
-        4,
+        3,
     )
     inner = inner.reshape(-1)[:384] / WIDTH
     gains = gains.reshape(-1)

time: 724 us -> 383 us (0.53)
  Pallas kernels: 686 us -> 334 us
    pallas_call x2 -> x1, Pallas kernels: 322 us -> 3.35 us  [reorder(): pl.pallas_call(reorder_kernel, out_shape=[jax.ShapeDtypeStruct(a.shape, a...]
    pallas_call x2 -> x1, Pallas kernels: 244 us -> 216 us  [front(): pl.pallas_call(front_kernel, out_shape=[sds((2, 32, 64, 512), BF16), sds(...]
where the time goes in v2:
time: 383 us; the launch traced here: 382 us
  Pallas kernels  334 us (87%)
  other arithmetic  21.5 us (6%)
  matrix products  17 us (4%)
  local copies, waits for them, and re-layouts  8.49 us (2%)
    pallas_call x1, Pallas kernels, front(): pl.pallas_call(front_kernel, out_shape=[sds((2, 32, 64, 512), BF16), sds(...  216 us
    pallas_call x1, Pallas kernels, scatter_rows(): pl.pallas_call(scatter_kernel, out_shape=[sds((128, 512), F32), sds((128,...  84.1 us
    pallas_call x2, Pallas kernels, small_sums(): pl.pallas_call(functools.partial(small_kernel, groups), out_shape=[jax.Sh...  30.6 us
    dot_general x3, matrix products, weight(): return jnp.einsum('tnf,nh->tfh', left, right, preferred_element_type=F32)  15.7 us

profile of v2, /device:TPU:1, one launch (start us, length us, event | category | flops | bytes accessed | tf_op | source)
XLA Modules:
  0.0 381.9 jit_solution(5823508597829972978)
XLA Ops:
  0.6 1.1 fusion.12
  1.7 1.0 fusion.23
  2.7 0.6 fusion.28.refs_0_
  3.3 13.8 %shard_map.178 = f32[8,128]{1,0:T(8,128)} custom-call(f32[8,128]{1,0:T(8,128)} %fusion.28.refs_0_), custom_call_target="tpu_custom_call" | custom-call | tf_op jit(solution)/shard_map/pallas_call | solution.py:153
  17.2 0.7 add_rsqrt_fusion
  17.9 1.8 fusion.7.enc
  19.6 1.7 fusion.17
  21.3 1.3 fusion.26.bias
  22.6 1.3 select_reduce_fusion.inverse
  23.9 216.0 %shard_map.179 = (bf16[2,32,64,512]{3,2,1,0:T(8,128)(2,1)}, bf16[2,32,64,512]{3,2,1,0:T(8,128)(2,1)}, bf16[2,4096,512]{2,1,0:T(8,128)(2,1)}, bf16[2,512,256]{2,1...) custom-call(bf16[2,64,512]{2,1,0:T(8,128)(2,1)} %bitcast.76, ...), custom_call_target="tpu_custom_call" | custom-call | tf_op jit(solution)/shard_map/pallas_call | solution.py:499
  239.9 3.4 shard_map.180
  243.2 3.9 %fusion.1 = f32[2,512,256]{2,1,0:T(8,128)S(1)} fusion(bf16[2,2048,512]{2,1,0:T(8,128)(2,1)} %bitcast.80, bf16[2048,256]{1,0:T(8,128)(2,1)} %get-tuple-element.31.qg), kind=kOutput, calls=%fused_computation.6 | convolution fusion | flops 1073741824 | bytes 6291456 | tf_op jit(solution)/shard_map/tnf,nh->tfh/dot_general | solution.py:793
  247.2 0.0 copy-start.3
  247.2 0.9 copy-done.3
  248.1 0.0 copy-done
  248.1 5.9 %fusion.29 = f32[2,512,256]{2,1,0:T(8,128)S(1)} fusion(bf16[2,4096,512]{2,1,0:T(8,128)(2,1)} %get-tuple-element.40, bf16[4096,256,1]{1,0,2:T(8,128)(2,1)S(1)} %bitcast.67), kind=kOutput, calls=%fused_computation.66 | convolution fusion | flops 2147483648 | bytes 11534336 | tf_op jit(solution)/shard_map/tnf,nh->tfh/dot_general | solution.py:793
  254.0 0.1 select_convert_fusion.2
  254.1 0.0 copy-start.7
  254.1 5.9 %fusion.30 = f32[2,512,256]{2,1,0:T(8,128)S(1)} fusion(bf16[2,4096,512]{2,1,0:T(8,128)(2,1)} %get-tuple-element.40, bf16[4096,256,1]{1,0,2:T(8,128)(2,1)S(1)} %bitcast.69), kind=kOutput, calls=%fused_computation.67 | convolution fusion | flops 2147483648 | bytes 11534336 | tf_op jit(solution)/shard_map/tnf,nh->tfh/dot_general | solution.py:793
  260.0 0.1 select_convert_fusion.1
  260.1 1.0 pad_maximum_fusion.wg
  261.1 1.3 convolution_bitcast_fusion
  262.4 0.8 fusion.25.wog
  263.1 2.1 copy.30
  265.2 2.1 copy.31
  267.2 2.0 copy.29
  269.3 84.1 %shard_map.181 = (f32[128,512]{1,0:T(8,128)}, f32[128,512]{1,0:T(8,128)}, f32[256,512]{1,0:T(8,128)}, bf16[3,512,256]{2,1,0:T(8,128)(2,1)}, bf16[256,512]{1,0:T(8,128)(2,1)}) custom-call(bf16[2048,256]{1,0:T(8,128)(2,1)} %get-tuple-element.31.qg, bf16[2048,256]{1,0:T(8,128)(2,1)} %get-tuple-element.32.att, bf16[4096,256]{1,0:T(8,128)(2,1)} %bitcast.66, ...), custom_call_target="tpu_custom_call" | custom-call | tf_op jit(solution)/shard_map/pallas_call | solution.py:704
  353.4 1.2 bitcast_convert_fusion
  354.7 0.0 copy-start.4
  354.7 1.1 convert_element_type.76
  355.8 0.1 select_bitcast_fusion
  355.9 0.1 select_bitcast_fusion.1
  356.0 1.7 maximum_select_fusion.2
  357.6 0.0 copy-start.11
  357.7 0.1 select_bitcast_fusion.3
  357.7 0.0 copy-start.9
  357.8 0.1 select_bitcast_fusion.2
  357.8 1.7 maximum_select_fusion
  359.5 0.2 fusion.19
  359.7 0.0 copy-done.5
  359.8 0.3 fusion.9
  360.0 0.6 pad_maximum_fusion.1.refs_1_
  360.6 0.6 fusion.27.refs_0_
  361.2 16.8 %shard_map.182 = (f32[8,128]{1,0:T(8,128)}, f32[8,128]{1,0:T(8,128)}) custom-call(f32[8,128]{1,0:T(8,128)} %fusion.27.refs_0_, f32[8,128]{1,0:T(8,128)} %pad_maximum_fusion.1.refs_1_), custom_call_target="tpu_custom_call" | custom-call | tf_op jit(solution)/shard_map/pallas_call | solution.py:153
  378.0 0.7 slice_multiply_fusion
  378.7 1.0 fusion.11
  379.7 0.9 fusion.22
  380.6 1.3 slice_bitcast_fusion
  (25 shorter events, 0.1 us)
Async XLA Ops:
  243.2 4.9 %copy-start = (bf16[8,512,256]{2,1,0:T(8,128)(2,1)S(1)}, bf16[8,512,256]{2,1,0:T(8,128)(2,1)}, u32[]{:S(2)}) copy-start(bf16[8,512,256]{2,1,0:T(8,128)(2,1)} %get-tuple-element.33) | copy-start | bytes 6291460
  247.2 1.0 copy-start.3
  248.1 6.0 %copy-start.1 = (bf16[8,512,256]{2,1,0:T(8,128)(2,1)S(1)}, bf16[8,512,256]{2,1,0:T(8,128)(2,1)}, u32[]{:S(2)}) copy-start(bf16[8,512,256]{2,1,0:T(8,128)(2,1)} %get-tuple-element.34) | copy-start | bytes 6291460
  254.1 7.0 %copy-start.7 = (bf16[2048,256]{1,0:T(8,128)(2,1)S(1)}, bf16[2048,256]{1,0:T(8,128)(2,1)}, u32[]{:S(2)}) copy-start(bf16[2048,256]{1,0:T(8,128)(2,1)} %get-tuple-element.32.att) | copy-start | bytes 3145732
  254.1 6.9 %copy-start.13 = (bf16[2,32,64,512]{3,2,1,0:T(8,128)(2,1)S(1)}, bf16[2,32,64,512]{3,2,1,0:T(8,128)(2,1)}, u32[]{:S(2)}) copy-start(bf16[2,32,64,512]{3,2,1,0:T(8,128)(2,1)} %get-tuple-element.41) | copy-start | bytes 12582916
  354.7 3.0 copy-start.4
  357.6 1.9 copy-start.6
  357.6 1.9 copy-start.8
  357.6 1.9 copy-start.12
  357.6 2.1 copy-start.2
  357.6 2.1 copy-start.5
  357.6 2.1 copy-start.11
  357.7 22.0 %copy-start.9 = (bf16[128,512]{1,0:T(8,128)(2,1)S(1)}, bf16[128,512]{1,0:T(8,128)(2,1)}, u32[]{:S(2)}) copy-start(bf16[128,512]{1,0:T(8,128)(2,1)} %param.21) | copy-start | bytes 393220
  357.7 22.0 %copy-start.10 = (f32[128,512]{1,0:T(8,128)S(1)}, f32[128,512]{1,0:T(8,128)}, u32[]{:S(2)}) copy-start(f32[128,512]{1,0:T(8,128)} %get-tuple-element.42) | copy-start | bytes 786436

commit v3 on v2

--- a/solution.py
+++ b/solution.py
@@ -78,6 +78,13 @@
     ]
 
 
+def ring_neighbours(z):
+    return [
+        {"section": lax.rem(z + 1, DEPTH)},
+        {"section": lax.rem(z + DEPTH - 1, DEPTH)},
+    ]
+
+
 def params(cid, mib=None):
     return pltpu.CompilerParams(
         collective_id=cid,
@@ -158,29 +165,6 @@
         scratch_shapes=[pltpu.VMEM((16, 8, 128), F32)] * n + [DMA((n, 16)), DMA((n, 16))],
         compiler_params=params(cid),
     )(*arrays)
-
-
-def reorder_kernel(index, *refs):
-    n = len(refs) // 2
-
-    def move(j, _):
-        src = pl.ds(pl.multiple_of(index[j] * 64, 64), 64)
-        dst = pl.ds(pl.multiple_of(j * 64, 64), 64)
-        for k in range(n):
-            refs[n + k][dst, :] = refs[k][src, :]
-        return 0
-
-    lax.fori_loop(0, 32, move, 0)
-
-
-def reorder(index, *arrays):
-    n = len(arrays)
-    return pl.pallas_call(
-        reorder_kernel,
-        out_shape=[jax.ShapeDtypeStruct(a.shape, a.dtype) for a in arrays],
-        in_specs=[SMEM] + [VMEM] * n,
-        out_specs=[VMEM] * n,
-    )(index, *arrays)
 
 
 def dot(a, b):
@@ -239,10 +223,10 @@
     wk,
     wv,
     wo,
-    att_all,
-    qg_all,
-    kg_all,
-    vg_all,
+    att,
+    qg,
+    kg,
+    vg,
     cot_v,
     dec_v,
     enc_v,
@@ -260,15 +244,11 @@
     out_sem,
     send,
     recv,
-    g_send,
-    g_recv,
 ):
     z, s, t, x, y, core = place()
     sibling = {"seq": s + 1 - 2 * core}
     partner = {"tensor": 1 - t}
-    ahead = {"section": lax.rem(z + 1, DEPTH)}
-    behind = {"section": lax.rem(z + DEPTH - 1, DEPTH)}
-    greet(plane_neighbours(x, y, core, s) + [ahead, behind])
+    greet(plane_neighbours(x, y, core, s) + ring_neighbours(z))
 
 
     def slot(k, chip, c):
@@ -303,7 +283,7 @@
     def keep(k):
         return pltpu.make_async_copy(sources[k], slot(k, (x, y), core), own_sem.at[k])
 
-    for k in range(4):
+    for k in (0, 2, 1, 3):
         for way in range(2):
             onward(k, way, 0, sources[k]).start()
     half = pl.ds(pl.multiple_of(t * 256, 256), 256)
@@ -326,8 +306,8 @@
         copy.start()
 
     def gather_step(j, _):
-        for way in range(2):
-            for k in range(4):
+        for k in (0, 2, 1, 3):
+            for way in range(2):
 
                 @pl.when(j < hops(k, way))
                 def _(k=k, way=way):
@@ -447,43 +427,10 @@
                     fin[h, 512 + u * 128 : 512 + (u + 1) * 128, head],
                     bias[pl.ds(z * 4 + n, 1), :],
                 )
-                att_all[z, n * 64 : (n + 1) * 64, head] = attended
-                qg_all[z, n * 64 : (n + 1) * 64, head] = query_grad
-                kg_all[z, n * 128 : (n + 1) * 128, head] = key_grad
-                vg_all[z, n * 128 : (n + 1) * 128, head] = value_grad
-
-    arrays = ((kg_all, 1), (vg_all, -1), (att_all, 1), (qg_all, -1))
-
-    def ring_block(n, j):
-        return arrays[n][0].at[lax.rem(z + DEPTH - arrays[n][1] * j, DEPTH)]
-
-    def ring_copy(n, j):
-        device = ahead if arrays[n][1] == 1 else behind
-        block = ring_block(n, j)
-        return remote(block, block, g_send.at[n, j], g_recv.at[n, j], device)
-
-    for n in range(4):
-        ring_copy(n, 0).start()
-
-    def ring_step(j, _):
-        for n in range(4):
-            block = ring_block(n, j + 1)
-            remote(block, block, g_send.at[n, j], g_recv.at[n, j], ahead).wait_recv()
-
-            @pl.when(j < DEPTH - 2)
-            def _(n=n):
-                ring_copy(n, j + 1).start()
-
-        return 0
-
-    lax.fori_loop(0, DEPTH - 1, ring_step, 0)
-
-    def ring_end(j, _):
-        for n in range(4):
-            ring_copy(n, j).wait_send()
-        return 0
-
-    lax.fori_loop(0, DEPTH - 1, ring_end, 0)
+                att[n, :, head] = attended
+                qg[n, :, head] = query_grad
+                kg[n * 128 : (n + 1) * 128, head] = key_grad
+                vg[n * 128 : (n + 1) * 128, head] = value_grad
 
     def chain_end(w, _):
         chain(lax.rem(w, 4), lax.div(w, 4), 1).wait_send()
@@ -506,10 +453,10 @@
             sds((2, 512, 256), BF16),
             sds((2, 512, 256), BF16),
             sds((2, 256, 512), BF16),
-            sds((8, 256, 256), BF16),
-            sds((8, 256, 256), BF16),
-            sds((8, 512, 256), BF16),
-            sds((8, 512, 256), BF16),
+            sds((4, 64, 256), BF16),
+            sds((4, 64, 256), BF16),
+            sds((512, 256), BF16),
+            sds((512, 256), BF16),
         ],
         in_specs=[VMEM] * 8 + [SMEM],
         out_specs=[ANY] * 3 + [VMEM] * 8,
@@ -531,34 +478,49 @@
             DMA((3,)),
             DMA((4, 4)),
             DMA((4, 4)),
-            DMA((4, 7)),
-            DMA((4, 7)),
         ],
         compiler_params=params(1, 60),
     )(cot, dec, enc, wq, wk, wv, wo, bias, inverse)
 
 
-def scatter_kernel(
-    qg,
-    att,
-    kg,
-    vg,
+def back_kernel(
+    att_own,
+    qg_own,
+    kg_own,
+    vg_own,
     wq,
     wk,
     wv,
     wo,
-    wg,
-    wog,
+    cot_hbm,
+    dec_hbm,
+    enc_hbm,
+    ids,
     dec_out,
     out_out,
     enc_out,
-    wg_out,
-    wog_out,
+    grads,
+    grads_in,
+    att_all,
+    qg_all,
+    kg_all,
+    vg_all,
+    att,
+    qg,
+    cot,
+    dec,
+    enc,
     sib_out,
     sib_in,
     chain_out,
     chain_in,
     mine,
+    acc,
+    grads_out,
+    g_send,
+    g_recv,
+    own_sem,
+    x_sem,
     s_send,
     s_recv,
     c_send,
@@ -570,163 +532,301 @@
     sibling = {"seq": s + 1 - 2 * core}
     partner = {"tensor": 1 - t}
     position = (ring_position(0, x, y), ring_position(1, x, y))
-    greet(plane_neighbours(x, y, core, s))
-    swaps = (
-        remote(wg, wg_out, w_send.at[0], w_recv.at[0], partner),
-        remote(wog, wog_out, w_send.at[1], w_recv.at[1], partner),
-    )
-
-    def both(ref, sd, size):
+    loads = [
+        pltpu.make_async_copy(src, dst, x_sem.at[n])
+        for n, (src, dst) in enumerate(((cot_hbm, cot), (dec_hbm, dec), (enc_hbm, enc)))
+    ]
+    owns = (att_own, qg_own, kg_own, vg_own)
+    alls = (att_all, qg_all, kg_all, vg_all)
+    greet(plane_neighbours(x, y, core, s) + ring_neighbours(z))
+
+
+    def ring_block(n, place_z):
+        if n < 2:
+            return alls[n].at[pl.ds(place_z * 4, 4)]
+        return alls[n].at[pl.ds(pl.multiple_of(place_z * 512, 512), 512)]
+
+    def ring_hops(n, way):
+        return 4 if n % 2 == way else 3
+
+    def ring_copy(n, way, j, src=None):
+        sign = 1 - 2 * way
+        block = ring_block(n, lax.rem(z + DEPTH - sign * j, DEPTH))
+        device = {"section": lax.rem(z + DEPTH + sign, DEPTH)}
+        return remote(
+            block if src is None else src, block, g_send.at[n, way, j], g_recv.at[n, way, j], device
+        )
+
+    def ring_first(ns):
+        for n in ns:
+            for way in range(2):
+                ring_copy(n, way, 0, owns[n]).start()
+
+    def ring_step(ns, j):
+        for n in ns:
+            for way in range(2):
+
+                @pl.when(j < ring_hops(n, way))
+                def _(n=n, way=way):
+                    sign = 1 - 2 * way
+                    block = ring_block(n, lax.rem(z + DEPTH - sign * (j + 1), DEPTH))
+                    remote(
+                        block,
+                        block,
+                        g_send.at[n, way, j],
+                        g_recv.at[n, way, j],
+                        ring_neighbours(z)[0],
+                    ).wait_recv()
+
+                    @pl.when(j + 1 < ring_hops(n, way))
+                    def _():
+                        ring_copy(n, way, j + 1).start()
+
+    def keep(n):
+        return pltpu.make_async_copy(owns[n], ring_block(n, z), own_sem.at[n])
+
+    ring_first((0, 1))
+    for n in range(4):
+        keep(n).start()
+    for copy in loads:
+        copy.start()
+    for k in range(4):
+        for way in range(2):
+            for sub in range(2):
+                chain_in[k, way, sub, 0] = jnp.zeros((64, 512), BF16)
+
+    def first_steps(j, _):
+        ring_step((0, 1), j)
+
+        @pl.when(j == 2)
+        def _():
+            ring_first((2, 3))
+
+        return 0
+
+    lax.fori_loop(0, 4, first_steps, 0)
+    for n in range(4):
+        keep(n).wait()
+
+    def token_order(b, _):
+        rows = pl.ds(pl.multiple_of(b * 64, 64), 64)
+        att[rows, :] = att_all[ids[b]]
+        qg[rows, :] = qg_all[ids[b]]
+        return 0
+
+    lax.fori_loop(0, 32, token_order, 0)
+
+
+    def dest(ring, offset):
+        cx, cy = ring_chip(ring, lax.rem(position[ring] + offset, RING))
+        return seq_tensor(cx, cy, 0)
+
+    def both(ref, base, stride):
         return jnp.concatenate(
             [
-                ref[pl.ds(pl.multiple_of((sd + c) * size, 128), size), :]
+                ref[pl.ds(pl.multiple_of(base + c * stride, 128), 128), :]
                 for c in (core, 1 - core)
             ],
             axis=0,
         )
 
+    def product(k, offset):
+        sd, td = dest(k % 2, offset)
+        if k == 0:
+            return dot(both(qg, sd * 128, 128), wq[td])
+        if k == 1:
+            return dot(both(att, sd * 128, 128), wo[td])
+        base = sd * 256 + (k - 2) * 128
+        return dot(both(kg_all, base, 256), wk[td]) + dot(both(vg_all, base, 256), wv[td])
+
     def across(k, i):
         return remote(
-            sib_out.at[k, i], sib_in.at[k, i], s_send.at[k, i], s_recv.at[k, i], sibling
+            sib_out.at[k, lax.rem(i, 4)],
+            sib_in.at[k, i],
+            s_send.at[k, i],
+            s_recv.at[k, i],
+            sibling,
         )
 
-    def give(i):
-        offset = 8 + (1 - 2 * lax.rem(i, 2)) * lax.div(i + 1, 2)
-        place_of = lax.rem(i, 8)
-        cx, cy = ring_chip(0, lax.rem(position[0] + offset, RING))
-        sd, td = seq_tensor(cx, cy, 0)
-        for k, rows, w in ((0, qg, wq), (1, att, wo)):
-            total = dot(both(rows, sd, 128), w[td])
-            sib_out[k, i] = total[128:].astype(BF16)
+    def give(ks, i):
+        half = lax.div(i, 2)
+        offset = 8 - half + lax.rem(i, 2) * (2 * half + 1)
+        for k in ks:
+            total = product(k, offset)
+
+            @pl.when(i >= 4)
+            def _(k=k):
+                across(k, i - 4).wait_send()
+
+            sib_out[k, lax.rem(i, 4)] = total[128:].astype(BF16)
             across(k, i).start()
-            mine[k, place_of] = total[:128]
-        cx, cy = ring_chip(1, lax.rem(position[1] + offset, RING))
-        sd, td = seq_tensor(cx, cy, 0)
-        total = dot(both(kg, sd, 256), wk[td]) + dot(both(vg, sd, 256), wv[td])
-        for k in (2, 3):
-            lo = (k - 2) * 128
-            sib_out[k, i] = total[256 + lo : 384 + lo].astype(BF16)
-            across(k, i).start()
-            mine[k, place_of] = total[lo : 128 + lo]
-
-    def onward(k, way, j):
-        device = ring_device(k // 2, position[k // 2] + 1 - 2 * way, core)
+            mine[k % 2, lax.rem(i, 4)] = total[:128]
+
+    def onward(k, way, sub, j):
+        device = ring_device(k % 2, position[k % 2] + 1 - 2 * way, core)
         return remote(
-            chain_out.at[k, way, j],
-            chain_in.at[k, way, j + 1],
-            c_send.at[k, way, j],
-            c_recv.at[k, way, j],
+            chain_out.at[k, way, sub, lax.rem(j, 2)],
+            chain_in.at[k, way, sub, j + 1],
+            c_send.at[k, way, sub, j],
+            c_recv.at[k, way, sub, j],
             device,
         )
 
-    for k in range(4):
+    def chain_step(ks, j):
+        for sub in range(2):
+            part = slice(sub * 64, (sub + 1) * 64)
+            for way in range(2):
+                for k in ks:
+
+                    @pl.when(j < 8 - way)
+                    def _(k=k, way=way, sub=sub, part=part):
+                        i = 2 * j + way
+                        if sub == 0:
+                            across(k, i).wait_recv()
+
+                        @pl.when(j > 0)
+                        def _():
+                            onward(k, way, sub, j - 1).wait_recv()
+
+                        @pl.when(j > 1)
+                        def _():
+                            onward(k, way, sub, j - 2).wait_send()
+
+                        total = mine[k % 2, lax.rem(i, 4), part] + sib_in[k, i, part].astype(F32)
+                        total = total + chain_in[k, way, sub, j].astype(F32)
+                        chain_out[k, way, sub, lax.rem(j, 2)] = total.astype(BF16)
+                        onward(k, way, sub, j).start()
+
+    def weight_swap(n):
+        return remote(
+            grads_out.at[n], grads_in.at[n], w_send.at[n], w_recv.at[n], partner
+        )
+
+    def weight_step(pairs, rows, j):
+        f = 1 - t + lax.div(j, 4) * (2 * t - 1)
+        here = pl.ds(pl.multiple_of(lax.rem(j, 4) * rows, rows), rows)
+        for a, (n, left, right) in enumerate(pairs):
+
+            @pl.when(lax.rem(j, 4) == 0)
+            def _(a=a):
+                acc[a] = jnp.zeros((256, 512), F32)
+
+            acc[a] += t_dot(left[here, :], right[f, here, :])
+
+            @pl.when(j == 3)
+            def _(a=a, n=n):
+                grads_out[n] = acc[a].astype(BF16)
+                weight_swap(n).start()
+
+            @pl.when(j == 7)
+            def _(a=a, n=n):
+                grads[n] = acc[a]
+
+    def scatter(ks, filler):
+        give(ks, 0)
+        give(ks, 1)
+
+        def step(j, _):
+            chain_step(ks, j)
+
+            @pl.when(j < 7)
+            def _():
+                lax.fori_loop(2 * j + 2, 2 * j + 4, lambda i, _: (give(ks, i), 0)[1], 0)
+
+            filler(j)
+            return 0
+
+        lax.fori_loop(0, 8, step, 0)
+        outs = {
+            0: dec_out,
+            1: out_out,
+            2: enc_out.at[pl.ds(0, 128)],
+            3: enc_out.at[pl.ds(128, 128)],
+        }
+        for k in ks:
+            across(k, 15).wait_recv()
+            for sub in range(2):
+                part = pl.ds(sub * 64, 64)
+                total = mine[k % 2, 3, part] + sib_in[k, 15, part].astype(F32)
+                for way in range(2):
+                    onward(k, way, sub, 7 - way).wait_recv()
+                    total = total + chain_in[k, way, sub, 8 - way].astype(F32)
+                outs[k][part, :] = total
+        for k in ks:
+            for i in range(12, 16):
+                across(k, i).wait_send()
+            for way in range(2):
+                for sub in range(2):
+                    onward(k, way, sub, 6 - way).wait_send()
+                    onward(k, way, sub, 7 - way).wait_send()
+
+    def token_filler(j):
+        @pl.when(j == 0)
+        def _():
+            loads[0].wait()
+            loads[1].wait()
+
+        weight_step(((0, qg, dec), (3, att, cot)), 512, j)
+
+        @pl.when(lax.rem(j, 2) == 1)
+        def _():
+            ring_step((2, 3), lax.div(j, 2))
+
+    scatter((0, 1), token_filler)
+    loads[2].wait()
+    scatter((2, 3), lambda j: weight_step(((1, kg_all, enc), (2, vg_all, enc)), 1024, j))
+
+    for n in range(4):
         for way in range(2):
-            chain_in[k, way, 0] = jnp.zeros((128, 512), BF16)
-
-    lax.fori_loop(0, 3, lambda i, _: (give(i), 0)[1], 0)
-    for copy in swaps:
-        copy.start()
-
-    def step(j, _):
-        def ahead(i, _):
-            @pl.when(i < RING)
-            def _():
-                give(i)
-
-            return 0
-
-        lax.fori_loop(2 * j + 3, 2 * j + 5, ahead, 0)
-
-        def way_step(way, _):
-            for k in range(4):
-                length = 8 - way if k % 2 == 0 else 7 + way
-                distance = length - j
-
-                @pl.when(distance > 0)
-                def _(k=k, distance=distance):
-                    m = 8 - distance
-                    i = jnp.maximum(2 * m - 1 + way, 0)
-                    across(k, i).wait_recv()
-
-                    @pl.when(j > 0)
-                    def _():
-                        onward(k, way, j - 1).wait_recv()
-
-                    total = mine[k, lax.rem(i, 8)] + sib_in[k, i].astype(F32)
-                    total = total + chain_in[k, way, j].astype(F32)
-                    chain_out[k, way, j] = total.astype(BF16)
-                    onward(k, way, j).start()
-
-            return 0
-
-        lax.fori_loop(0, 2, way_step, 0)
-        return 0
-
-    lax.fori_loop(0, 8, step, 0)
-
-    outs = (
-        dec_out,
-        out_out,
-        enc_out.at[pl.ds(0, 128)],
-        enc_out.at[pl.ds(128, 128)],
-    )
-    for k in range(4):
-        across(k, 15).wait_recv()
-        total = mine[k, 7] + sib_in[k, 15].astype(F32)
-        for way in range(2):
-            length = 8 - way if k % 2 == 0 else 7 + way
-            onward(k, way, length - 1).wait_recv()
-            total = total + chain_in[k, way, length].astype(F32)
-        outs[k][...] = total
-
-    def drain(i, _):
-        for k in range(4):
-            across(k, i).wait_send()
-        return 0
-
-    lax.fori_loop(0, RING, drain, 0)
-
-    def drain_chain(j, _):
-        for k in range(4):
-            for way in range(2):
-                onward(k, way, j).wait_send()
-        return 0
-
-    lax.fori_loop(0, 7, drain_chain, 0)
-    for k in range(4):
-        onward(k, k % 2, 7).wait_send()
-    for copy in swaps:
-        copy.wait()
-
-
-def scatter_rows(qg, att, kg, vg, wq, wk, wv, wo, wg, wog):
+            for j in range(ring_hops(n, way)):
+                ring_copy(n, way, j).wait_send()
+    for n in range(4):
+        weight_swap(n).wait()
+
+
+def back(*args):
     sds = jax.ShapeDtypeStruct
     return pl.pallas_call(
-        scatter_kernel,
+        back_kernel,
         out_shape=[
             sds((128, 512), F32),
             sds((128, 512), F32),
             sds((256, 512), F32),
-            sds((3, 512, 256), BF16),
-            sds((256, 512), BF16),
+            sds((4, 256, 512), F32),
+            sds((4, 256, 512), BF16),
         ],
-        in_specs=[VMEM] * 8 + [ANY] * 2,
-        out_specs=[VMEM] * 3 + [ANY] * 2,
+        in_specs=[VMEM] * 8 + [ANY] * 3 + [SMEM],
+        out_specs=[VMEM] * 5,
         scratch_shapes=[
+            pltpu.VMEM((32, 64, 256), BF16),
+            pltpu.VMEM((32, 64, 256), BF16),
+            pltpu.VMEM((4096, 256), BF16),
+            pltpu.VMEM((4096, 256), BF16),
+            pltpu.VMEM((2048, 256), BF16),
+            pltpu.VMEM((2048, 256), BF16),
+            pltpu.VMEM((2, 2048, 512), BF16),
+            pltpu.VMEM((2, 2048, 512), BF16),
+            pltpu.VMEM((2, 4096, 512), BF16),
+            pltpu.VMEM((4, 4, 128, 512), BF16),
             pltpu.VMEM((4, 16, 128, 512), BF16),
-            pltpu.VMEM((4, 16, 128, 512), BF16),
-            pltpu.VMEM((4, 2, 8, 128, 512), BF16),
-            pltpu.VMEM((4, 2, 9, 128, 512), BF16),
-            pltpu.VMEM((4, 8, 128, 512), F32),
+            pltpu.VMEM((4, 2, 2, 2, 64, 512), BF16),
+            pltpu.VMEM((4, 2, 2, 9, 64, 512), BF16),
+            pltpu.VMEM((2, 4, 128, 512), F32),
+            pltpu.VMEM((2, 256, 512), F32),
+            pltpu.VMEM((4, 256, 512), BF16),
+            DMA((4, 2, 4)),
+            DMA((4, 2, 4)),
+            DMA((4,)),
+            DMA((3,)),
             DMA((4, 16)),
             DMA((4, 16)),
-            DMA((4, 2, 8)),
-            DMA((4, 2, 8)),
-            DMA((2,)),
-            DMA((2,)),
+            DMA((4, 2, 2, 8)),
+            DMA((4, 2, 2, 8)),
+            DMA((4,)),
+            DMA((4,)),
         ],
-        compiler_params=params(2, 60),
-    )(qg, att, kg, vg, wq, wk, wv, wo, wg, wog)
+        compiler_params=params(2, 62),
+    )(*args)
 
 
 def pack(*vectors):
@@ -784,44 +884,26 @@
         bias,
         inverse,
     )
-    cot_all, dec_all = cot_all.reshape(2, 2048, 512), dec_all.reshape(2, 2048, 512)
-    att, qg = att.reshape(2048, 256), qg.reshape(2048, 256)
-    kg, vg = kg.reshape(4096, 256), vg.reshape(4096, 256)
-    att, qg = reorder(neighbour_ids, att, qg)
-
-    def weight(left, right):
-        return jnp.einsum("tnf,nh->tfh", left, right, preferred_element_type=F32)
-
-    grads = (weight(dec_all, qg), weight(enc_all, kg), weight(enc_all, vg))
-    out_grad = jnp.einsum("nh,tnf->thf", att, cot_all, preferred_element_type=F32)
-
-    def mine(g):
-        return jnp.where(t == 0, g[0], g[1])
-
-    def other(g):
-        return jnp.where(t == 0, g[1], g[0]).astype(BF16)
-
-    dec_input, out_total, enc_input, wg, wog = scatter_rows(
+    dec_input, out_total, enc_input, own, got = back(
+        att,
         qg,
-        att,
         kg,
         vg,
         jnp.swapaxes(wq, 1, 2),
         jnp.swapaxes(wk, 1, 2),
         jnp.swapaxes(wv, 1, 2),
         wo,
-        jnp.stack([other(g) for g in grads]),
-        other(out_grad),
-    )
-
-    def join(own, got, axis):
-        got = got.astype(F32)
-        return jnp.where(
-            t == 0, jnp.concatenate([own, got], axis), jnp.concatenate([got, own], axis)
-        )
-
-    weight_grads = [join(mine(g), wg[n], 1) for n, g in enumerate(grads)]
-    out_weight_grad = join(mine(out_grad), wog, 0)
+        cot_all.reshape(2, 2048, 512),
+        dec_all.reshape(2, 2048, 512),
+        enc_all,
+        neighbour_ids,
+    )
+    got = got.astype(F32)
+    joined = jnp.where(
+        t == 0, jnp.concatenate([own, got], 1), jnp.concatenate([got, own], 1)
+    )
+    weight_grads = [joined[n].T for n in range(3)]
+    out_weight_grad = joined[3]
     layer_out = (dec_rows + out_total).astype(BF16)
     dec_scaled = dec_gain * dec_input
     enc_scaled = enc_gain * enc_input

time: 383 us -> 331 us (0.86)
  Pallas kernels: 334 us -> 299 us
  matrix products: 17 us -> 0 us
  local copies, waits for them, and re-layouts: 8.49 us -> 12.9 us
    pallas_call x1, Pallas kernels: 216 us -> 149 us  [front(): pl.pallas_call(front_kernel, out_shape=[sds((2, 32, 64, 512), BF16), sds(...]
    pallas_call x2 -> x1, Pallas kernels: 87.5 us -> 124 us  [back(): pl.pallas_call(back_kernel, out_shape=[sds((128, 512), F32), sds((128, 51...]
    dot_general x4 -> x0, matrix products: 17 us -> none  [the longest x3 15.7 us: weight(): return jnp.einsum('tnf,nh->tfh', left, right, preferred_element_type=F32)]
    pallas_call x2, Pallas kernels: 30.6 us -> 25.1 us  [small_sums(): pl.pallas_call(functools.partial(small_kernel, groups), out_shape=[jax.Sh...]
where the time goes in v3:
time: 331 us; the launch traced here: 330 us
  Pallas kernels  299 us (90%)
  other arithmetic  18.2 us (5%)
  local copies, waits for them, and re-layouts  12.9 us (4%)
    pallas_call x1, Pallas kernels, front(): pl.pallas_call(front_kernel, out_shape=[sds((2, 32, 64, 512), BF16), sds(...  149 us
    pallas_call x1, Pallas kernels, back(): pl.pallas_call(back_kernel, out_shape=[sds((128, 512), F32), sds((128, 51...  124 us
    pallas_call x2, Pallas kernels, small_sums(): pl.pallas_call(functools.partial(small_kernel, groups), out_shape=[jax.Sh...  25.1 us

profile of v3, /device:TPU:1, one launch (start us, length us, event | category | flops | bytes accessed | tf_op | source)
XLA Modules:
  0.0 330.3 jit_solution(18036641711408843346)
XLA Ops:
  0.6 1.1 fusion.9
  1.7 1.0 fusion.20
  2.7 0.6 fusion.24.refs_0_
  3.3 13.8 %shard_map.178 = f32[8,128]{1,0:T(8,128)} custom-call(f32[8,128]{1,0:T(8,128)} %fusion.24.refs_0_), custom_call_target="tpu_custom_call" | custom-call | tf_op jit(solution)/shard_map/pallas_call | solution.py:160
  17.2 0.7 add_rsqrt_fusion
  17.9 1.8 fusion.4.enc
  19.7 1.7 fusion.14
  21.3 1.3 fusion.22.bias
  22.6 1.3 select_reduce_fusion.inverse
  23.9 149.3 %shard_map.179 = (bf16[2,32,64,512]{3,2,1,0:T(8,128)(2,1)}, bf16[2,32,64,512]{3,2,1,0:T(8,128)(2,1)}, bf16[2,4096,512]{2,1,0:T(8,128)(2,1)}, bf16[2,512,256]{2,1...) custom-call(bf16[2,64,512]{2,1,0:T(8,128)(2,1)} %bitcast.45, ...), custom_call_target="tpu_custom_call" | custom-call | tf_op jit(solution)/shard_map/pallas_call | solution.py:446
  173.2 2.0 copy.26
  175.2 2.0 copy.27
  177.3 2.0 copy.28
  179.3 124.2 %shard_map.180 = (f32[128,512]{1,0:T(8,128)}, f32[128,512]{1,0:T(8,128)}, f32[256,512]{1,0:T(8,128)}, f32[4,256,512]{2,1,0:T(8,128)}, bf16[4,256,512]{2,1,0:T(8,128)(2,1)}) custom-call(bf16[4,64,256]{2,1,0:T(8,128)(2,1)} %get-tuple-element.27.att_own, bf16[4,64,256]{2,1,0:T(8,128)(2,1)} %get-tuple-element.28.qg_own, ...), custom_call_target="tpu_custom_call" | custom-call | tf_op jit(solution)/shard_map/pallas_call | solution.py:789
  303.5 1.5 convert_element_type.30
  305.0 3.0 maximum_select_fusion
  308.1 1.4 slice_bitcast_fusion
  309.5 0.0 copy-start.2
  309.5 0.0 copy-start.7
  309.5 0.0 copy-start
  309.5 0.0 copy-start.6
  309.5 1.3 copy.29
  310.8 0.0 copy-start.3
  310.8 0.0 copy-start.1
  310.8 0.0 copy-start.4
  310.8 1.3 copy.30
  312.1 0.0 copy-start.5
  312.1 1.3 copy.31
  313.4 0.0 copy-done.2
  313.4 0.0 copy-done.7
  313.4 0.0 copy-done.3
  313.4 0.2 fusion.16
  313.6 0.0 copy-done
  313.6 0.0 copy-done.6
  313.6 0.0 copy-done.1
  313.7 0.3 fusion.6
  313.9 0.6 pad_maximum_fusion.refs_1_
  314.5 0.6 fusion.23.refs_0_
  315.1 11.3 %shard_map.181 = (f32[8,128]{1,0:T(8,128)}, f32[8,128]{1,0:T(8,128)}) custom-call(f32[8,128]{1,0:T(8,128)} %fusion.23.refs_0_, f32[8,128]{1,0:T(8,128)} %pad_maximum_fusion.refs_1_), custom_call_target="tpu_custom_call" | custom-call | tf_op jit(solution)/shard_map/pallas_call | solution.py:160
  326.5 0.7 slice_multiply_fusion
  327.1 1.0 fusion.8
  328.1 0.0 copy-done.4
  328.1 0.0 copy-done.5
  328.1 0.9 fusion.19
  329.0 1.3 slice_bitcast_fusion.4
  (4 shorter events, 0.0 us)
Async XLA Ops:
  309.5 3.9 %copy-start.2 = (bf16[128,512]{1,0:T(8,128)(2,1)S(1)}, bf16[128,512]{1,0:T(8,128)(2,1)}, u32[]{:S(2)}) copy-start(bf16[128,512]{1,0:T(8,128)(2,1)} %param.11) | copy-start | bytes 393220
  309.5 3.9 %copy-start.7 = (f32[512]{0:T(512)S(1)}, f32[512]{0:T(512)}, u32[]{:S(2)}) copy-start(f32[512]{0:T(512)} %param.12) | copy-start | bytes 6148
  309.5 4.2 %copy-start = (bf16[256,512]{1,0:T(8,128)(2,1)S(1)}, bf16[256,512]{1,0:T(8,128)(2,1)}, u32[]{:S(2)}) copy-start(bf16[256,512]{1,0:T(8,128)(2,1)} %param.13) | copy-start | bytes 786436
  309.5 4.2 %copy-start.6 = (f32[512]{0:T(512)S(1)}, f32[512]{0:T(512)}, u32[]{:S(2)}) copy-start(f32[512]{0:T(512)} %param.14) | copy-start | bytes 6148
  310.8 2.6 copy-start.3
  310.8 2.9 copy-start.1
  310.8 17.3 %copy-start.4 = (bf16[128,512]{1,0:T(8,128)(2,1)S(1)}, bf16[128,512]{1,0:T(8,128)(2,1)}, u32[]{:S(2)}) copy-start(bf16[128,512]{1,0:T(8,128)(2,1)} %param.21) | copy-start | bytes 393220
  312.1 16.0 %copy-start.5 = (f32[128,512]{1,0:T(8,128)S(1)}, f32[128,512]{1,0:T(8,128)}, u32[]{:S(2)}) copy-start(f32[128,512]{1,0:T(8,128)} %get-tuple-element.38) | copy-start | bytes 786436

commit v4 on v3

--- a/solution.py
+++ b/solution.py
@@ -202,14 +202,12 @@
     return attended, query_grad, key_grad, value_grad
 
 
-def hops(k, way):
-    return 8 - way if k % 2 == 0 else 7 + way
-
-
 def front_kernel(
     cot,
-    dec,
-    enc,
+    hidden,
+    neigh,
+    dec_gain,
+    enc_gain,
     wq_own,
     wk_own,
     wv_own,
@@ -219,20 +217,33 @@
     cot_all,
     dec_all,
     enc_all,
-    wq,
-    wk,
-    wv,
+    wq_t,
+    wk_t,
+    wv_t,
     wo,
     att,
     qg,
     kg,
     vg,
+    squares,
     cot_v,
     dec_v,
     enc_v,
-    sendb,
-    recvb,
-    fin,
+    wq,
+    wk,
+    wv,
+    dec,
+    enc,
+    stat,
+    stats,
+    kv_send,
+    kv_recv,
+    qa_send,
+    qa_recv,
+    kv_fin,
+    qa_fin,
+    st_send,
+    st_recv,
     p_send,
     p_recv,
     s_send,
@@ -242,53 +253,144 @@
     w_recv,
     w_own,
     out_sem,
-    send,
-    recv,
+    kv_ssem,
+    kv_rsem,
+    qa_ssem,
+    qa_rsem,
 ):
     z, s, t, x, y, core = place()
     sibling = {"seq": s + 1 - 2 * core}
     partner = {"tensor": 1 - t}
-    greet(plane_neighbours(x, y, core, s) + ring_neighbours(z))
-
-
-    def slot(k, chip, c):
+    group = z * 2 + t
+
+    def peer(r):
+        g = lax.rem(group + r, 16)
+        return {"section": lax.div(g, 2), "tensor": lax.rem(g, 2)}, g
+
+    barrier = pltpu.get_barrier_semaphore()
+    near = plane_neighbours(x, y, core, s)
+    for device in near:
+        pl.semaphore_signal(barrier, inc=1, device_id=device, device_id_type=MESH)
+
+    def hello(r, _):
+        pl.semaphore_signal(barrier, inc=1, device_id=peer(r)[0], device_id_type=MESH)
+        return 0
+
+    lax.fori_loop(1, 16, hello, 0)
+    dec_rows = hidden[...].reshape(128, 512).astype(F32)
+    enc_rows = neigh[...].astype(F32)
+    sums = jnp.concatenate(
+        [
+            jnp.sum(dec_rows * dec_rows, axis=1, keepdims=True),
+            jnp.sum(enc_rows * enc_rows, axis=1, keepdims=True),
+        ],
+        axis=0,
+    )
+    stat[...] = jnp.broadcast_to(sums, (384, 128)).T[:8]
+    pl.semaphore_wait(barrier, len(near) + 15)
+
+
+    def slot(k, sub, chip, c):
         so, to = seq_tensor(chip[0], chip[1], c)
         if k == 0:
-            return cot_v.at[to, pl.ds(so * 2, 2)]
+            return cot_v.at[to, so * 2 + sub]
         if k == 1:
-            return dec_v.at[to, pl.ds(so * 2, 2)]
-        return enc_v.at[to, pl.ds(pl.multiple_of(so * 256 + (k - 2) * 128, 128), 128)]
-
-    sources = (cot, dec, enc.at[pl.ds(0, 128)], enc.at[pl.ds(128, 128)])
+            return dec_v.at[to, so * 2 + sub]
+        return enc_v.at[to, pl.ds(pl.multiple_of(so * 256 + (k - 2) * 128 + sub * 64, 64), 64)]
+
+    def source(k, sub):
+        if k == 0:
+            return cot.at[sub]
+        if k == 1:
+            return dec.at[sub]
+        return enc.at[pl.ds((k - 2) * 128 + sub * 64, 64)]
+
     position = (ring_position(0, x, y), ring_position(1, x, y))
 
     def origin(k, way, j):
-        return ring_chip(
-            k // 2, lax.rem(position[k // 2] + RING - (1 - 2 * way) * j, RING)
+        return ring_chip(k % 2, lax.rem(position[k % 2] + RING - (1 - 2 * way) * j, RING))
+
+    def onward(k, way, sub, j, src):
+        device = ring_device(k % 2, position[k % 2] + 1 - 2 * way, core)
+        block = slot(k, sub, origin(k, way, j), core)
+        return remote(
+            src, block, p_send.at[k, way, sub, j], p_recv.at[k, way, sub, j], device
         )
 
-    def onward(k, way, j, src):
-        device = ring_device(k // 2, position[k // 2] + 1 - 2 * way, core)
-        block = slot(k, origin(k, way, j), core)
-        return remote(src, block, p_send.at[k, way, j], p_recv.at[k, way, j], device)
-
-    def arrival(k, way, j):
-        block = slot(k, origin(k, way, j + 1), core)
-        return remote(block, block, p_send.at[k, way, j], p_recv.at[k, way, j], sibling), block
-
-    def across(k, way, j, src, c):
-        block = slot(k, origin(k, way, j), c)
-        return remote(src, block, s_send.at[k, way, j], s_recv.at[k, way, j], sibling)
-
-    def keep(k):
-        return pltpu.make_async_copy(sources[k], slot(k, (x, y), core), own_sem.at[k])
-
-    for k in (0, 2, 1, 3):
-        for way in range(2):
-            onward(k, way, 0, sources[k]).start()
+    def across(k, way, sub, j, src, c):
+        block = slot(k, sub, origin(k, way, j), c)
+        return remote(
+            src, block, s_send.at[k, way, sub, j], s_recv.at[k, way, sub, j], sibling
+        )
+
+    def keep(k, sub):
+        return pltpu.make_async_copy(
+            source(k, sub), slot(k, sub, (x, y), core), own_sem.at[k, sub]
+        )
+
+    def begin(ks):
+        for sub in range(2):
+            for way in range(2):
+                for k in ks:
+                    onward(k, way, sub, 0, source(k, sub)).start()
+        for k in ks:
+            for sub in range(2):
+                across(k, 0, sub, 0, source(k, sub), core).start()
+                keep(k, sub).start()
+
+    def gather_step(ks, j):
+        for sub in range(2):
+            for way in range(2):
+                for k in ks:
+
+                    @pl.when(j < 8 - way)
+                    def _(k=k, way=way, sub=sub):
+                        block = slot(k, sub, origin(k, way, j + 1), core)
+                        remote(
+                            block,
+                            block,
+                            p_send.at[k, way, sub, j],
+                            p_recv.at[k, way, sub, j],
+                            sibling,
+                        ).wait_recv()
+
+                        @pl.when(j < 7 - way)
+                        def _():
+                            onward(k, way, sub, j + 1, block).start()
+
+                        across(k, way, sub, j + 1, block, core).start()
+
+    def gather_end(ks):
+        def one(j, _):
+            for k in ks:
+                for sub in range(2):
+                    for way in range(2):
+
+                        @pl.when(j < 8 - way)
+                        def _(k=k, way=way, sub=sub):
+                            src = source(k, sub)
+                            onward(k, way, sub, j, src).wait_send()
+                            across(k, way, sub, j + 1, src, core).wait_send()
+                            across(k, way, sub, j + 1, src, 1 - core).wait_recv()
+
+            return 0
+
+        lax.fori_loop(0, 8, one, 0)
+        for k in ks:
+            for sub in range(2):
+                across(k, 0, sub, 0, source(k, sub), core).wait_send()
+                across(k, 0, sub, 0, source(k, sub), 1 - core).wait_recv()
+                keep(k, sub).wait()
+
+
+    def tell(r):
+        device, g = peer(r)
+        return remote(stat, stats.at[group], st_send.at[r], st_recv.at[group], device)
+
+    lax.fori_loop(1, 16, lambda r, _: (tell(r).start(), 0)[1], 0)
     half = pl.ds(pl.multiple_of(t * 256, 256), 256)
     rest = pl.ds(pl.multiple_of((1 - t) * 256, 256), 256)
-    weights = ((wq_own, wq), (wk_own, wk), (wv_own, wv))
+    weights = ((wk_own, wk), (wv_own, wv), (wq_own, wq))
     swaps = [
         remote(w.at[:, rest], w_all.at[t], w_send.at[n], w_recv.at[n], partner)
         for n, (w, w_all) in enumerate(weights)
@@ -297,123 +399,142 @@
         pltpu.make_async_copy(w.at[:, half], w_all.at[t], w_own.at[n])
         for n, (w, w_all) in enumerate(weights)
     ] + [pltpu.make_async_copy(wo_own.at[half, :], wo.at[t], w_own.at[3])]
+    begin((0,))
+    for copy in keeps:
+        copy.start()
+    stats[group] = stat[...]
+
+    def hear(r, _):
+        device, g = peer(r)
+        remote(stat, stats.at[g], st_send.at[r], st_recv.at[g], device).wait_recv()
+        return 0
+
+    lax.fori_loop(1, 16, hear, 0)
+    total = stats[0]
+    for g in range(1, 16):
+        total = total + stats[g]
+    squares[...] = total
+    scale = lax.rsqrt(total[:1] / WIDTH + EPS)
+    scale = jnp.broadcast_to(scale, (128, 384)).T[:, :1]
+    enc[...] = (neigh[...].astype(F32) * scale[128:] * enc_gain[...]).astype(BF16)
+    begin((2, 3))
+    rows = hidden[...].reshape(128, 512).astype(F32)
+    dec[...] = (rows * scale[:128] * dec_gain[...]).astype(BF16).reshape(2, 64, 512)
     for copy in swaps:
         copy.start()
-    for k in range(4):
-        across(k, 0, 0, sources[k], core).start()
-        keep(k).start()
-    for copy in keeps:
-        copy.start()
-
-    def gather_step(j, _):
-        for k in (0, 2, 1, 3):
-            for way in range(2):
-
-                @pl.when(j < hops(k, way))
-                def _(k=k, way=way):
-                    wait, block = arrival(k, way, j)
-                    wait.wait_recv()
-
-                    @pl.when(j + 1 < hops(k, way))
-                    def _():
-                        onward(k, way, j + 1, block).start()
-
-                    across(k, way, j + 1, block, core).start()
+
+    def enc_step(j, _):
+        gather_step((2, 3), j)
+
+        @pl.when(j == 4)
+        def _():
+            begin((1,))
+
+        @pl.when(j >= 6)
+        def _():
+            gather_step((0, 1), j - 6)
 
         return 0
 
-    lax.fori_loop(0, 8, gather_step, 0)
+    lax.fori_loop(0, 8, enc_step, 0)
 
     def zero(n, _):
-        recvb[n, 0] = jnp.zeros((768, 256), BF16)
+        kv_recv[n, 0] = jnp.zeros((512, 256), BF16)
+        qa_recv[n, 0] = jnp.zeros((256, 256), BF16)
         return 0
 
     lax.fori_loop(0, 4, zero, 0)
-
-    def gather_end(j, _):
-        for way in range(2):
-            for k in range(4):
-
-                @pl.when(j < hops(k, way))
-                def _(k=k, way=way):
-                    onward(k, way, j, sources[k]).wait_send()
-                    across(k, way, j + 1, sources[k], core).wait_send()
-                    across(k, way, j + 1, sources[k], 1 - core).wait_recv()
-
-        return 0
-
-    lax.fori_loop(0, 8, gather_end, 0)
-    for k in range(4):
-        across(k, 0, 0, sources[k], core).wait_send()
-        across(k, 0, 0, sources[k], 1 - core).wait_recv()
-        keep(k).wait()
-    for copy in keeps:
+    for n, copy in enumerate(keeps):
         copy.wait()
-    for copy in swaps:
-        copy.wait_send()
+        swaps[n].wait_send()
     for n, (w, w_all) in enumerate(weights):
         remote(w.at[:, rest], w_all.at[1 - t], w_send.at[n], w_recv.at[n], partner).wait_recv()
     remote(wo_own.at[rest, :], wo.at[1 - t], w_send.at[3], w_recv.at[3], partner).wait_recv()
+    gather_end((2, 3))
     stores = [
         pltpu.make_async_copy(src, dst, out_sem.at[n])
         for n, (src, dst) in enumerate(((cot_v, cot_all), (dec_v, dec_all), (enc_v, enc_all)))
     ]
-    for copy in stores:
-        copy.start()
-
-
-    def partial(d, h):
+    stores[2].start()
+
+
+    def pair_part(d, h):
+        stored = pl.ds(pl.multiple_of(d * 512 + h * 256, 256), 256)
+        first, second = enc_v[0, stored, :], enc_v[1, stored, :]
+        k = dot(first, wk[0]) + dot(second, wk[1])
+        v = dot(first, wv[0]) + dot(second, wv[1])
+        return ((0, 256, k), (256, 512, v))
+
+    def query_part(d, h):
         j = d * 4 + h * 2
         b0, b1 = inverse[j], inverse[j + 1]
-        stored = pl.ds(pl.multiple_of(j * 128, 256), 256)
-        q = a = k = v = 0.0
+        q = a = 0.0
         for f in range(2):
-            rows = jnp.concatenate([dec_v[f, b0], dec_v[f, b1]], axis=0)
-            q = q + dot(rows, wq[f])
-            rows = jnp.concatenate([cot_v[f, b0], cot_v[f, b1]], axis=0)
-            a = a + dot_t(rows, wo[f])
-            rows = enc_v[f, stored, :]
-            k = k + dot(rows, wk[f])
-            v = v + dot(rows, wv[f])
-        return ((0, 128, q), (128, 256, a), (256, 512, k), (512, 768, v))
-
-    def stream(n):
-        h = lax.rem(n, 2)
-        way = lax.rem(h + lax.div(n, 2), 2)
-        return h, 1 - 2 * way, 4 - lax.div(n, 2)
-
-    def chain(n, t, sign):
+            q = q + dot(jnp.concatenate([dec_v[f, b0], dec_v[f, b1]], axis=0), wq[f])
+            a = a + dot_t(jnp.concatenate([cot_v[f, b0], cot_v[f, b1]], axis=0), wo[f])
+        return ((0, 128, q), (128, 256, a))
+
+    pairs = (kv_send, kv_recv, kv_ssem, kv_rsem, kv_fin, pair_part)
+    queries = (qa_send, qa_recv, qa_ssem, qa_rsem, qa_fin, query_part)
+
+    def chain(which, n, j, sign):
+        sendb, recvb, ssem, rsem = which[:4]
         device = {"section": lax.rem(z + DEPTH + sign, DEPTH)}
         return remote(
-            sendb.at[n, t], recvb.at[n, t + 1], send.at[n, t], recv.at[n, t], device
+            sendb.at[n, j], recvb.at[n, j + 1], ssem.at[n, j], rsem.at[n, j], device
         )
 
-    def item(w, _):
-        n, t = lax.rem(w, 4), lax.div(w, 4)
-        h, sign, length = stream(n)
-        parts = partial(lax.rem(z + DEPTH + sign * (length - t), DEPTH), h)
-
-        @pl.when(t > 0)
+    def item(which, w):
+        n, j = lax.rem(w, 4), lax.div(w, 4)
+        h = lax.rem(n, 2)
+        sign = 1 - 2 * lax.rem(h + lax.div(n, 2), 2)
+        length = 4 - lax.div(n, 2)
+        parts = which[5](lax.rem(z + DEPTH + sign * (length - j), DEPTH), h)
+
+        @pl.when(j > 0)
         def _():
-            chain(n, t - 1, sign).wait_recv()
+            chain(which, n, j - 1, sign).wait_recv()
 
         for lo, hi, part in parts:
-            sendb[n, t, lo:hi] = (part + recvb[n, t, lo:hi].astype(F32)).astype(BF16)
-        chain(n, t, sign).start()
+            which[0][n, j, lo:hi] = (part + which[1][n, j, lo:hi].astype(F32)).astype(BF16)
+        chain(which, n, j, sign).start()
+
+    def last(which):
+        def one(h, _):
+            parts = which[5](z, h)
+            chain(which, h, 3, 1).wait_recv()
+            chain(which, h + 2, 2, 1).wait_recv()
+            for lo, hi, part in parts:
+                total = part + which[1][h, 4, lo:hi].astype(F32)
+                total = total + which[1][h + 2, 3, lo:hi].astype(F32)
+                which[4][h, lo:hi] = total.astype(BF16)
+            return 0
+
+        lax.fori_loop(0, 2, one, 0)
+
+    def pair_item(w, _):
+        item(pairs, w)
+
+        @pl.when((lax.rem(w, 2) == 1) & (w < 12))
+        def _():
+            gather_step((0, 1), lax.div(w, 2) + 2)
+
+        for n, (src, dst) in enumerate(((wq, wq_t), (wk, wk_t), (wv, wv_t))):
+
+            @pl.when(w == 4 + 2 * n)
+            def _(src=src, dst=dst):
+                for f in range(2):
+                    dst[f] = src[f].T
+
         return 0
 
-    lax.fori_loop(0, 14, item, 0)
-
-    def last(h, _):
-        parts = partial(z, h)
-        chain(h, 3, 1).wait_recv()
-        chain(h + 2, 2, 1).wait_recv()
-        for lo, hi, part in parts:
-            total = part + recvb[h, 4, lo:hi].astype(F32) + recvb[h + 2, 3, lo:hi].astype(F32)
-            fin[h, lo:hi] = total.astype(BF16)
-        return 0
-
-    lax.fori_loop(0, 2, last, 0)
+    lax.fori_loop(0, 14, pair_item, 0)
+    gather_end((0, 1))
+    stores[0].start()
+    stores[1].start()
+    lax.fori_loop(0, 14, lambda w, _: (item(queries, w), 0)[1], 0)
+    last(pairs)
+    last(queries)
 
     for h in range(2):
         for u in range(2):
@@ -421,10 +542,10 @@
             for g in range(2):
                 head = slice(g * 128, (g + 1) * 128)
                 attended, query_grad, key_grad, value_grad = attend(
-                    fin[h, u * 64 : (u + 1) * 64, head],
-                    fin[h, 128 + u * 64 : 128 + (u + 1) * 64, head],
-                    fin[h, 256 + u * 128 : 256 + (u + 1) * 128, head],
-                    fin[h, 512 + u * 128 : 512 + (u + 1) * 128, head],
+                    qa_fin[h, u * 64 : (u + 1) * 64, head],
+                    qa_fin[h, 128 + u * 64 : 128 + (u + 1) * 64, head],
+                    kv_fin[h, u * 128 : (u + 1) * 128, head],
+                    kv_fin[h, 256 + u * 128 : 256 + (u + 1) * 128, head],
                     bias[pl.ds(z * 4 + n, 1), :],
                 )
                 att[n, :, head] = attended
@@ -433,15 +554,17 @@
                 vg[n * 128 : (n + 1) * 128, head] = value_grad
 
     def chain_end(w, _):
-        chain(lax.rem(w, 4), lax.div(w, 4), 1).wait_send()
+        chain(pairs, lax.rem(w, 4), lax.div(w, 4), 1).wait_send()
+        chain(queries, lax.rem(w, 4), lax.div(w, 4), 1).wait_send()
         return 0
 
     lax.fori_loop(0, 14, chain_end, 0)
+    lax.fori_loop(1, 16, lambda r, _: (tell(r).wait_send(), 0)[1], 0)
     for copy in stores:
         copy.wait()
 
 
-def front(cot, dec, enc, wq, wk, wv, wo, bias, inverse):
+def front(*args):
     sds = jax.ShapeDtypeStruct
     return pl.pallas_call(
         front_kernel,
@@ -449,38 +572,53 @@
             sds((2, 32, 64, 512), BF16),
             sds((2, 32, 64, 512), BF16),
             sds((2, 4096, 512), BF16),
-            sds((2, 512, 256), BF16),
-            sds((2, 512, 256), BF16),
-            sds((2, 512, 256), BF16),
+            sds((2, 256, 512), BF16),
+            sds((2, 256, 512), BF16),
+            sds((2, 256, 512), BF16),
             sds((2, 256, 512), BF16),
             sds((4, 64, 256), BF16),
             sds((4, 64, 256), BF16),
             sds((512, 256), BF16),
             sds((512, 256), BF16),
+            sds((8, 384), F32),
         ],
-        in_specs=[VMEM] * 8 + [SMEM],
-        out_specs=[ANY] * 3 + [VMEM] * 8,
+        in_specs=[VMEM] * 10 + [SMEM],
+        out_specs=[ANY] * 3 + [VMEM] * 9,
         scratch_shapes=[
             pltpu.VMEM((2, 32, 64, 512), BF16),
             pltpu.VMEM((2, 32, 64, 512), BF16),
             pltpu.VMEM((2, 4096, 512), BF16),
-            pltpu.VMEM((4, 4, 768, 256), BF16),
-            pltpu.VMEM((4, 5, 768, 256), BF16),
-            pltpu.VMEM((2, 768, 256), BF16),
-            DMA((4, 2, 8)),
-            DMA((4, 2, 8)),
-            DMA((4, 2, 9)),
-            DMA((4, 2, 9)),
-            DMA((4,)),
+            pltpu.VMEM((2, 512, 256), BF16),
+            pltpu.VMEM((2, 512, 256), BF16),
+            pltpu.VMEM((2, 512, 256), BF16),
+            pltpu.VMEM((2, 64, 512), BF16),
+            pltpu.VMEM((256, 512), BF16),
+            pltpu.VMEM((8, 384), F32),
+            pltpu.VMEM((16, 8, 384), F32),
+            pltpu.VMEM((4, 4, 512, 256), BF16),
+            pltpu.VMEM((4, 5, 512, 256), BF16),
+            pltpu.VMEM((4, 4, 256, 256), BF16),
+            pltpu.VMEM((4, 5, 256, 256), BF16),
+            pltpu.VMEM((2, 512, 256), BF16),
+            pltpu.VMEM((2, 256, 256), BF16),
+            DMA((16,)),
+            DMA((16,)),
+            DMA((4, 2, 2, 8)),
+            DMA((4, 2, 2, 8)),
+            DMA((4, 2, 2, 9)),
+            DMA((4, 2, 2, 9)),
+            DMA((4, 2)),
             DMA((4,)),
             DMA((4,)),
             DMA((4,)),
             DMA((3,)),
             DMA((4, 4)),
             DMA((4, 4)),
+            DMA((4, 4)),
+            DMA((4, 4)),
         ],
         compiler_params=params(1, 60),
-    )(cot, dec, enc, wq, wk, wv, wo, bias, inverse)
+    )(*args)
 
 
 def back_kernel(
@@ -851,17 +989,6 @@
     rows = hidden.shape[0]
     dec_rows = hidden.astype(F32)
     enc_rows = neigh_states.astype(F32)
-    (squares,) = small_sums(
-        [pack(jnp.sum(dec_rows * dec_rows, axis=1), jnp.sum(enc_rows * enc_rows, axis=1))],
-        ("st",),
-        0,
-    )
-    scales = lax.rsqrt(squares.reshape(-1)[:384] / WIDTH + EPS)
-    dec_scale, enc_scale = scales[:rows, None], scales[rows:, None]
-    dec_hat = dec_rows * dec_scale
-    enc_hat = enc_rows * enc_scale
-    dec_local = (dec_hat * dec_gain).astype(BF16)
-    enc_local = (enc_hat * enc_gain).astype(BF16)
     count = neighbour_ids.shape[0]
     inverse = jnp.sum(
         jnp.where(
@@ -873,10 +1000,12 @@
     )
     slots = jnp.arange(128, dtype=jnp.int32)[None, :]
     bias = jnp.where(slots < neighbour_len[:, None], 0.0, -jnp.inf).astype(F32)
-    cot_all, dec_all, enc_all, wq, wk, wv, wo, att, qg, kg, vg = front(
+    cot_all, dec_all, enc_all, wq, wk, wv, wo, att, qg, kg, vg, squares = front(
         cotangent.reshape(2, 64, 512),
-        dec_local.reshape(2, 64, 512),
-        enc_local,
+        hidden.reshape(2, 64, 512),
+        neigh_states,
+        dec_gain[None],
+        enc_gain[None],
         w_query,
         w_key,
         w_value,
@@ -889,15 +1018,19 @@
         qg,
         kg,
         vg,
-        jnp.swapaxes(wq, 1, 2),
-        jnp.swapaxes(wk, 1, 2),
-        jnp.swapaxes(wv, 1, 2),
+        wq,
+        wk,
+        wv,
         wo,
         cot_all.reshape(2, 2048, 512),
         dec_all.reshape(2, 2048, 512),
         enc_all,
         neighbour_ids,
     )
+    scales = lax.rsqrt(squares[0] / WIDTH + EPS)
+    dec_scale, enc_scale = scales[:rows, None], scales[rows:, None]
+    dec_hat = dec_rows * dec_scale
+    enc_hat = enc_rows * enc_scale
     got = got.astype(F32)
     joined = jnp.where(
         t == 0, jnp.concatenate([own, got], 1), jnp.concatenate([got, own], 1)

time: 331 us -> 307 us (0.927)
  Pallas kernels: 299 us -> 287 us
  local copies, waits for them, and re-layouts: 12.9 us -> 6.7 us
  other arithmetic: 18.2 us -> 12.1 us
    pallas_call x2 -> x1, Pallas kernels: 25.1 us -> 12.3 us  [small_sums(): pl.pallas_call(functools.partial(small_kernel, groups), out_shape=[jax.Sh...]
    pallas_call x3 -> x0, local copies, waits for them, and re-layouts: 6.14 us -> none  [front(): pl.pallas_call(front_kernel, out_shape=[sds((2, 32, 64, 512), BF16), sds(...]
    convert_element_type x2 -> x0, other arithmetic: 3.45 us -> none  [the longest x1 1.79 us: body(): enc_local = (enc_hat * enc_gain).astype(BF16)]
where the time goes in v4:
time: 307 us; the launch traced here: 306 us
  Pallas kernels  287 us (93%)
  other arithmetic  12.1 us (4%)
  local copies, waits for them, and re-layouts  6.7 us (2%)
    pallas_call x1, Pallas kernels, front(): pl.pallas_call(front_kernel, out_shape=[sds((2, 32, 64, 512), BF16), sds(...  150 us
    pallas_call x1, Pallas kernels, back(): pl.pallas_call(back_kernel, out_shape=[sds((128, 512), F32), sds((128, 51...  125 us
    pallas_call x1, Pallas kernels, small_sums(): pl.pallas_call(functools.partial(small_kernel, groups), out_shape=[jax.Sh...  12.3 us

profile of v4, /device:TPU:1, one launch (start us, length us, event | category | flops | bytes accessed | tf_op | source)
XLA Modules:
  0.0 306.3 jit_solution(11181675232447486909)
XLA Ops:
  0.6 1.3 fusion.9.bias
  2.0 1.3 select_reduce_fusion.inverse
  3.3 149.8 %shard_map.178 = (bf16[2,32,64,512]{3,2,1,0:T(8,128)(2,1)}, bf16[2,32,64,512]{3,2,1,0:T(8,128)(2,1)}, bf16[2,4096,512]{2,1,0:T(8,128)(2,1)}, bf16[2,256,512]{2,1...) custom-call(bf16[2,64,512]{2,1,0:T(8,128)(2,1)} %bitcast.38, ...), custom_call_target="tpu_custom_call" | custom-call | tf_op jit(solution)/shard_map/pallas_call | solution.py:569
  153.1 124.6 %shard_map.179 = (f32[128,512]{1,0:T(8,128)}, f32[128,512]{1,0:T(8,128)}, f32[256,512]{1,0:T(8,128)}, f32[4,256,512]{2,1,0:T(8,128)}, bf16[4,256,512]{2,1,0:T(8,128)(2,1)}) custom-call(bf16[4,64,256]{2,1,0:T(8,128)(2,1)} %get-tuple-element.28.att_own, bf16[4,64,256]{2,1,0:T(8,128)(2,1)} %get-tuple-element.29.qg_own, ...), custom_call_target="tpu_custom_call" | custom-call | tf_op jit(solution)/shard_map/pallas_call | solution.py:927
  277.7 1.5 convert_element_type.21
  279.2 3.1 %maximum_select_fusion = f32[4,512,512]{2,1,0:T(8,128)S(1)} fusion(f32[4,256,512]{2,1,0:T(8,128)S(1)} %convert_element_type.21, f32[4,256,512]{2,1,0:T(8,128)} %get-tuple-element.45, pred[]{:T(512)S(6)} %eq.19), kind=kLoop, calls=%fused_computation | loop fusion | flops 3145728 | bytes 8388609 | tf_op jit(solution)/shard_map/jit(_where)/select_n | solution.py:1035
  282.3 1.4 slice_bitcast_fusion
  283.7 0.0 copy-start.2
  283.7 0.0 copy-start.7
  283.7 0.0 copy-start
  283.7 0.0 copy-start.6
  283.7 1.3 copy.23
  285.0 0.0 copy-start.3
  285.0 0.0 copy-start.1
  285.0 0.0 copy-start.4
  285.0 1.3 copy.24
  286.3 0.0 copy-start.5
  286.3 1.3 copy.25
  287.6 0.7 add_rsqrt_fusion
  288.4 0.0 copy-done.2
  288.4 0.0 copy-done.7
  288.4 0.0 copy-done.3
  288.4 0.2 fusion.4
  288.6 0.0 copy-done
  288.6 0.0 copy-done.6
  288.6 0.0 copy-done.1
  288.6 0.3 multiply_reduce_fusion
  288.9 0.6 pad_maximum_fusion.refs_1_
  289.5 0.6 fusion.10.refs_0_
  290.1 12.3 %shard_map.180 = (f32[8,128]{1,0:T(8,128)}, f32[8,128]{1,0:T(8,128)}) custom-call(f32[8,128]{1,0:T(8,128)} %fusion.10.refs_0_, f32[8,128]{1,0:T(8,128)} %pad_maximum_fusion.refs_1_), custom_call_target="tpu_custom_call" | custom-call | tf_op jit(solution)/shard_map/pallas_call | solution.py:160
  302.4 0.7 slice_multiply_fusion
  303.1 1.0 subtract_multiply_fusion
  304.1 0.0 copy-done.4
  304.1 0.0 copy-done.5
  304.1 0.9 fusion.7
  305.0 1.3 slice_bitcast_fusion.4
  (4 shorter events, 0.0 us)
Async XLA Ops:
  283.7 4.7 %copy-start.2 = (bf16[128,512]{1,0:T(8,128)(2,1)S(1)}, bf16[128,512]{1,0:T(8,128)(2,1)}, u32[]{:S(2)}) copy-start(bf16[128,512]{1,0:T(8,128)(2,1)} %param.11) | copy-start | bytes 393220
  283.7 4.7 %copy-start.7 = (f32[512]{0:T(512)S(1)}, f32[512]{0:T(512)}, u32[]{:S(2)}) copy-start(f32[512]{0:T(512)} %param.12) | copy-start | bytes 6148
  283.7 4.9 %copy-start = (bf16[256,512]{1,0:T(8,128)(2,1)S(1)}, bf16[256,512]{1,0:T(8,128)(2,1)}, u32[]{:S(2)}) copy-start(bf16[256,512]{1,0:T(8,128)(2,1)} %neigh.1) | copy-start | bytes 786436
  283.7 4.9 %copy-start.6 = (f32[512]{0:T(512)S(1)}, f32[512]{0:T(512)}, u32[]{:S(2)}) copy-start(f32[512]{0:T(512)} %param.14) | copy-start | bytes 6148
  285.0 3.4 %copy-start.3 = (f32[128,512]{1,0:T(8,128)S(1)}, f32[128,512]{1,0:T(8,128)}, u32[]{:S(2)}) copy-start(f32[128,512]{1,0:T(8,128)} %get-tuple-element.41) | copy-start | bytes 786436
  285.0 3.6 %copy-start.1 = (f32[256,512]{1,0:T(8,128)S(1)}, f32[256,512]{1,0:T(8,128)}, u32[]{:S(2)}) copy-start(f32[256,512]{1,0:T(8,128)} %get-tuple-element.42) | copy-start | bytes 1572868
  285.0 19.1 %copy-start.4 = (bf16[128,512]{1,0:T(8,128)(2,1)S(1)}, bf16[128,512]{1,0:T(8,128)(2,1)}, u32[]{:S(2)}) copy-start(bf16[128,512]{1,0:T(8,128)(2,1)} %param.21) | copy-start | bytes 393220
  286.3 17.8 %copy-start.5 = (f32[128,512]{1,0:T(8,128)S(1)}, f32[128,512]{1,0:T(8,128)}, u32[]{:S(2)}) copy-start(f32[128,512]{1,0:T(8,128)} %get-tuple-element.39) | copy-start | bytes 786436

commit v5 on v4

--- a/solution.py
+++ b/solution.py
@@ -93,80 +93,6 @@
     )
 
 
-def small_kernel(groups, *refs):
-    n = len(groups)
-    ins, outs, slots = refs[:n], refs[n : 2 * n], refs[2 * n : 3 * n]
-    send, recv = refs[3 * n], refs[3 * n + 1]
-    z, s, t, _, _, _ = place()
-
-    def peer(group, r):
-        if group == "st":
-            g = lax.rem(z * 2 + t + r, 16)
-            return {"section": lax.div(g, 2), "tensor": lax.rem(g, 2)}, g
-        g = lax.rem(s + r, 16)
-        return {"seq": g}, g
-
-    barrier = pltpu.get_barrier_semaphore()
-    for group in groups:
-
-        def hello(r, _, group=group):
-            pl.semaphore_signal(
-                barrier, inc=1, device_id=peer(group, r)[0], device_id_type=MESH
-            )
-            return 0
-
-        lax.fori_loop(1, 16, hello, 0)
-    pl.semaphore_wait(barrier, 15 * n)
-    for k, group in enumerate(groups):
-        mine = peer(group, 0)[1]
-
-        def push(r, _, k=k, group=group, mine=mine):
-            device, _g = peer(group, r)
-            remote(
-                ins[k], slots[k].at[mine], send.at[k, r], recv.at[k, mine], device
-            ).start()
-            return 0
-
-        lax.fori_loop(1, 16, push, 0)
-        slots[k][mine] = ins[k][...]
-    for k, group in enumerate(groups):
-        mine = peer(group, 0)[1]
-
-        def take(r, _, k=k, group=group, mine=mine):
-            device, g = peer(group, r)
-            remote(ins[k], slots[k].at[g], send.at[k, r], recv.at[k, g], device).wait_recv()
-            return 0
-
-        lax.fori_loop(1, 16, take, 0)
-        total = slots[k][0]
-        for g in range(1, 16):
-            total = total + slots[k][g]
-        outs[k][...] = total
-    for k, group in enumerate(groups):
-        mine = peer(group, 0)[1]
-
-        def drain(r, _, k=k, group=group, mine=mine):
-            device, _g = peer(group, r)
-            remote(
-                ins[k], slots[k].at[mine], send.at[k, r], recv.at[k, mine], device
-            ).wait_send()
-            return 0
-
-        lax.fori_loop(1, 16, drain, 0)
-
-
-def small_sums(arrays, groups, cid):
-    n = len(groups)
-    return pl.pallas_call(
-        functools.partial(small_kernel, groups),
-        out_shape=[jax.ShapeDtypeStruct((8, 128), F32)] * n,
-        in_specs=[VMEM] * n,
-        out_specs=[VMEM] * n,
-        scratch_shapes=[pltpu.VMEM((16, 8, 128), F32)] * n + [DMA((n, 16)), DMA((n, 16))],
-        compiler_params=params(cid),
-    )(*arrays)
-
-
 def dot(a, b):
     return jnp.dot(a, b, preferred_element_type=F32)
 
@@ -184,22 +110,28 @@
     return high, (a - high.astype(F32)).astype(BF16)
 
 
-def attend(q, a, k, v, bias):
+def attend(units):
     scale = 128 ** (-0.5)
-    scores = dot_t(q, k) * scale + bias
-    top = jnp.max(scores, axis=1, keepdims=True)
-    expo = jnp.exp(scores - top)
-    probs = expo / jnp.sum(expo, axis=1, keepdims=True)
-    low = probs.astype(BF16)
-    attended = dot(low, v).astype(BF16)
-    value_grad = t_dot(low, a).astype(BF16)
-    prob_grad = dot_t(a, v)
-    inner = jnp.sum(probs * prob_grad, axis=1, keepdims=True)
-    score_grad = probs * (prob_grad - inner) * scale
-    high, rest = split(score_grad)
-    query_grad = (dot(high, k) + dot(rest, k)).astype(BF16)
-    key_grad = (t_dot(high, q) + t_dot(rest, q)).astype(BF16)
-    return attended, query_grad, key_grad, value_grad
+    scores = [dot_t(q, k) * scale + bias for q, a, k, v, bias in units]
+    prob_grads = [dot_t(a, v) for q, a, k, v, bias in units]
+    tops = [jnp.max(u, axis=1, keepdims=True) for u in scores]
+    expos = [jnp.exp(u - top) for u, top in zip(scores, tops)]
+    sums = [jnp.sum(u, axis=1, keepdims=True) for u in expos]
+    probs = [u / total for u, total in zip(expos, sums)]
+    lows = [u.astype(BF16) for u in probs]
+    inners = [jnp.sum(u * g, axis=1, keepdims=True) for u, g in zip(probs, prob_grads)]
+    score_grads = [u * (g - n) * scale for u, g, n in zip(probs, prob_grads, inners)]
+    splits = [split(u) for u in score_grads]
+    attended = [dot(low, u[3]).astype(BF16) for low, u in zip(lows, units)]
+    query_grads = [
+        (dot(high, u[2]) + dot(rest, u[2])).astype(BF16) for (high, rest), u in zip(splits, units)
+    ]
+    key_grads = [
+        (t_dot(high, u[0]) + t_dot(rest, u[0])).astype(BF16)
+        for (high, rest), u in zip(splits, units)
+    ]
+    value_grads = [t_dot(low, u[1]).astype(BF16) for low, u in zip(lows, units)]
+    return list(zip(attended, query_grads, key_grads, value_grads))
 
 
 def front_kernel(
@@ -217,9 +149,9 @@
     cot_all,
     dec_all,
     enc_all,
-    wq_t,
-    wk_t,
-    wv_t,
+    wq,
+    wk,
+    wv,
     wo,
     att,
     qg,
@@ -229,9 +161,6 @@
     cot_v,
     dec_v,
     enc_v,
-    wq,
-    wk,
-    wv,
     dec,
     enc,
     stat,
@@ -286,12 +215,15 @@
         ],
         axis=0,
     )
-    stat[...] = jnp.broadcast_to(sums, (384, 128)).T[:8]
+    sums = jnp.broadcast_to(sums, (384, 128)).T[:1]
+    stat[...] = jnp.zeros((8, 128), F32)
+    for n in range(3):
+        stat[n : n + 1] = sums[:, n * 128 : (n + 1) * 128]
     pl.semaphore_wait(barrier, len(near) + 15)
 
 
-    def slot(k, sub, chip, c):
-        so, to = seq_tensor(chip[0], chip[1], c)
+    def slot(k, sub, so, to, c):
+        so = so + c
         if k == 0:
             return cot_v.at[to, so * 2 + sub]
         if k == 1:
@@ -306,62 +238,71 @@
         return enc.at[pl.ds((k - 2) * 128 + sub * 64, 64)]
 
     position = (ring_position(0, x, y), ring_position(1, x, y))
-
-    def origin(k, way, j):
-        return ring_chip(k % 2, lax.rem(position[k % 2] + RING - (1 - 2 * way) * j, RING))
-
-    def onward(k, way, sub, j, src):
-        device = ring_device(k % 2, position[k % 2] + 1 - 2 * way, core)
-        block = slot(k, sub, origin(k, way, j), core)
+    own_so, own_to = seq_tensor(x, y, 0)
+    nexts = [
+        [ring_device(ring, position[ring] + 1 - 2 * way, core) for way in range(2)]
+        for ring in range(2)
+    ]
+
+    def origins(j):
+        return [
+            [
+                seq_tensor(
+                    *ring_chip(
+                        ring, lax.rem(position[ring] + RING - (1 - 2 * way) * j, RING)
+                    ),
+                    0,
+                )
+                for way in range(2)
+            ]
+            for ring in range(2)
+        ]
+
+    def onward(k, way, sub, j, src, dst):
         return remote(
-            src, block, p_send.at[k, way, sub, j], p_recv.at[k, way, sub, j], device
+            src, dst, p_send.at[k, way, sub, j], p_recv.at[k, way, sub, j], nexts[k % 2][way]
         )
 
-    def across(k, way, sub, j, src, c):
-        block = slot(k, sub, origin(k, way, j), c)
-        return remote(
-            src, block, s_send.at[k, way, sub, j], s_recv.at[k, way, sub, j], sibling
-        )
+    def across(k, way, sub, j, src, dst):
+        return remote(src, dst, s_send.at[k, way, sub, j], s_recv.at[k, way, sub, j], sibling)
 
     def keep(k, sub):
         return pltpu.make_async_copy(
-            source(k, sub), slot(k, sub, (x, y), core), own_sem.at[k, sub]
+            source(k, sub), slot(k, sub, own_so, own_to, core), own_sem.at[k, sub]
         )
 
     def begin(ks):
         for sub in range(2):
             for way in range(2):
                 for k in ks:
-                    onward(k, way, sub, 0, source(k, sub)).start()
+                    dst = slot(k, sub, own_so, own_to, core)
+                    onward(k, way, sub, 0, source(k, sub), dst).start()
         for k in ks:
             for sub in range(2):
-                across(k, 0, sub, 0, source(k, sub), core).start()
+                dst = slot(k, sub, own_so, own_to, core)
+                across(k, 0, sub, 0, source(k, sub), dst).start()
                 keep(k, sub).start()
 
     def gather_step(ks, j):
+        froms = origins(j + 1)
         for sub in range(2):
             for way in range(2):
                 for k in ks:
 
                     @pl.when(j < 8 - way)
                     def _(k=k, way=way, sub=sub):
-                        block = slot(k, sub, origin(k, way, j + 1), core)
-                        remote(
-                            block,
-                            block,
-                            p_send.at[k, way, sub, j],
-                            p_recv.at[k, way, sub, j],
-                            sibling,
-                        ).wait_recv()
+                        block = slot(k, sub, *froms[k % 2][way], core)
+                        onward(k, way, sub, j, block, block).wait_recv()
 
                         @pl.when(j < 7 - way)
                         def _():
-                            onward(k, way, sub, j + 1, block).start()
-
-                        across(k, way, sub, j + 1, block, core).start()
+                            onward(k, way, sub, j + 1, block, block).start()
+
+                        across(k, way, sub, j + 1, block, block).start()
 
     def gather_end(ks):
         def one(j, _):
+            froms = origins(j + 1)
             for k in ks:
                 for sub in range(2):
                     for way in range(2):
@@ -369,17 +310,20 @@
                         @pl.when(j < 8 - way)
                         def _(k=k, way=way, sub=sub):
                             src = source(k, sub)
-                            onward(k, way, sub, j, src).wait_send()
-                            across(k, way, sub, j + 1, src, core).wait_send()
-                            across(k, way, sub, j + 1, src, 1 - core).wait_recv()
+                            block = slot(k, sub, *froms[k % 2][way], 1 - core)
+                            onward(k, way, sub, j, src, src).wait_send()
+                            across(k, way, sub, j + 1, src, src).wait_send()
+                            across(k, way, sub, j + 1, block, block).wait_recv()
 
             return 0
 
         lax.fori_loop(0, 8, one, 0)
         for k in ks:
             for sub in range(2):
-                across(k, 0, sub, 0, source(k, sub), core).wait_send()
-                across(k, 0, sub, 0, source(k, sub), 1 - core).wait_recv()
+                src = source(k, sub)
+                block = slot(k, sub, own_so, own_to, 1 - core)
+                across(k, 0, sub, 0, src, src).wait_send()
+                across(k, 0, sub, 0, block, block).wait_recv()
                 keep(k, sub).wait()
 
 
@@ -399,7 +343,8 @@
         pltpu.make_async_copy(w.at[:, half], w_all.at[t], w_own.at[n])
         for n, (w, w_all) in enumerate(weights)
     ] + [pltpu.make_async_copy(wo_own.at[half, :], wo.at[t], w_own.at[3])]
-    begin((0,))
+    for copy in swaps[:2]:
+        copy.start()
     for copy in keeps:
         copy.start()
     stats[group] = stat[...]
@@ -414,21 +359,22 @@
     for g in range(1, 16):
         total = total + stats[g]
     squares[...] = total
-    scale = lax.rsqrt(total[:1] / WIDTH + EPS)
-    scale = jnp.broadcast_to(scale, (128, 384)).T[:, :1]
-    enc[...] = (neigh[...].astype(F32) * scale[128:] * enc_gain[...]).astype(BF16)
+    scale = lax.rsqrt(total / WIDTH + EPS)
+    scales = [jnp.broadcast_to(scale[n : n + 1], (128, 128)).T[:, :1] for n in range(3)]
+    for n in range(2):
+        rows = neigh[n * 128 : (n + 1) * 128].astype(F32)
+        normed = rows * scales[n + 1] * enc_gain[...]
+        enc[n * 128 : (n + 1) * 128] = normed.astype(BF16)
     begin((2, 3))
     rows = hidden[...].reshape(128, 512).astype(F32)
-    dec[...] = (rows * scale[:128] * dec_gain[...]).astype(BF16).reshape(2, 64, 512)
-    for copy in swaps:
-        copy.start()
+    dec[...] = (rows * scales[0] * dec_gain[...]).astype(BF16).reshape(2, 64, 512)
 
     def enc_step(j, _):
         gather_step((2, 3), j)
 
         @pl.when(j == 4)
         def _():
-            begin((1,))
+            begin((0, 1))
 
         @pl.when(j >= 6)
         def _():
@@ -444,12 +390,23 @@
         return 0
 
     lax.fori_loop(0, 4, zero, 0)
-    for n, copy in enumerate(keeps):
+    for copy in swaps[2:]:
+        copy.start()
+    for copy in keeps:
         copy.wait()
+
+    def swapped(n):
         swaps[n].wait_send()
-    for n, (w, w_all) in enumerate(weights):
-        remote(w.at[:, rest], w_all.at[1 - t], w_send.at[n], w_recv.at[n], partner).wait_recv()
-    remote(wo_own.at[rest, :], wo.at[1 - t], w_send.at[3], w_recv.at[3], partner).wait_recv()
+        if n < 3:
+            w, w_all = weights[n]
+            dst = w_all.at[1 - t]
+            remote(w.at[:, rest], dst, w_send.at[n], w_recv.at[n], partner).wait_recv()
+        else:
+            dst = wo.at[1 - t]
+            remote(wo_own.at[rest, :], dst, w_send.at[n], w_recv.at[n], partner).wait_recv()
+
+    swapped(0)
+    swapped(1)
     gather_end((2, 3))
     stores = [
         pltpu.make_async_copy(src, dst, out_sem.at[n])
@@ -519,17 +476,12 @@
         def _():
             gather_step((0, 1), lax.div(w, 2) + 2)
 
-        for n, (src, dst) in enumerate(((wq, wq_t), (wk, wk_t), (wv, wv_t))):
-
-            @pl.when(w == 4 + 2 * n)
-            def _(src=src, dst=dst):
-                for f in range(2):
-                    dst[f] = src[f].T
-
         return 0
 
     lax.fori_loop(0, 14, pair_item, 0)
     gather_end((0, 1))
+    swapped(2)
+    swapped(3)
     stores[0].start()
     stores[1].start()
     lax.fori_loop(0, 14, lambda w, _: (item(queries, w), 0)[1], 0)
@@ -537,21 +489,25 @@
     last(queries)
 
     for h in range(2):
-        for u in range(2):
-            n = h * 2 + u
-            for g in range(2):
-                head = slice(g * 128, (g + 1) * 128)
-                attended, query_grad, key_grad, value_grad = attend(
+        places = [(u, slice(g * 128, (g + 1) * 128)) for u in range(2) for g in range(2)]
+        results = attend(
+            [
+                (
                     qa_fin[h, u * 64 : (u + 1) * 64, head],
                     qa_fin[h, 128 + u * 64 : 128 + (u + 1) * 64, head],
                     kv_fin[h, u * 128 : (u + 1) * 128, head],
                     kv_fin[h, 256 + u * 128 : 256 + (u + 1) * 128, head],
-                    bias[pl.ds(z * 4 + n, 1), :],
+                    bias[pl.ds(z * 4 + h * 2 + u, 1), :],
                 )
-                att[n, :, head] = attended
-                qg[n, :, head] = query_grad
-                kg[n * 128 : (n + 1) * 128, head] = key_grad
-                vg[n * 128 : (n + 1) * 128, head] = value_grad
+                for u, head in places
+            ]
+        )
+        for (u, head), (attended, query_grad, key_grad, value_grad) in zip(places, results):
+            n = h * 2 + u
+            att[n, :, head] = attended
+            qg[n, :, head] = query_grad
+            kg[n * 128 : (n + 1) * 128, head] = key_grad
+            vg[n * 128 : (n + 1) * 128, head] = value_grad
 
     def chain_end(w, _):
         chain(pairs, lax.rem(w, 4), lax.div(w, 4), 1).wait_send()
@@ -572,15 +528,15 @@
             sds((2, 32, 64, 512), BF16),
             sds((2, 32, 64, 512), BF16),
             sds((2, 4096, 512), BF16),
-            sds((2, 256, 512), BF16),
-            sds((2, 256, 512), BF16),
-            sds((2, 256, 512), BF16),
+            sds((2, 512, 256), BF16),
+            sds((2, 512, 256), BF16),
+            sds((2, 512, 256), BF16),
             sds((2, 256, 512), BF16),
             sds((4, 64, 256), BF16),
             sds((4, 64, 256), BF16),
             sds((512, 256), BF16),
             sds((512, 256), BF16),
-            sds((8, 384), F32),
+            sds((8, 128), F32),
         ],
         in_specs=[VMEM] * 10 + [SMEM],
         out_specs=[ANY] * 3 + [VMEM] * 9,
@@ -588,13 +544,10 @@
             pltpu.VMEM((2, 32, 64, 512), BF16),
             pltpu.VMEM((2, 32, 64, 512), BF16),
             pltpu.VMEM((2, 4096, 512), BF16),
-            pltpu.VMEM((2, 512, 256), BF16),
-            pltpu.VMEM((2, 512, 256), BF16),
-            pltpu.VMEM((2, 512, 256), BF16),
             pltpu.VMEM((2, 64, 512), BF16),
             pltpu.VMEM((256, 512), BF16),
-            pltpu.VMEM((8, 384), F32),
-            pltpu.VMEM((16, 8, 384), F32),
+            pltpu.VMEM((8, 128), F32),
+            pltpu.VMEM((16, 8, 128), F32),
             pltpu.VMEM((4, 4, 512, 256), BF16),
             pltpu.VMEM((4, 5, 512, 256), BF16),
             pltpu.VMEM((4, 4, 256, 256), BF16),
@@ -634,11 +587,18 @@
     dec_hbm,
     enc_hbm,
     ids,
+    hidden,
+    neigh,
+    dec_gain,
+    enc_gain,
+    squares,
     dec_out,
     out_out,
     enc_out,
     grads,
     grads_in,
+    inner_out,
+    gain_out,
     att_all,
     qg_all,
     kg_all,
@@ -654,7 +614,14 @@
     chain_in,
     mine,
     acc,
+    pair_acc,
     grads_out,
+    inner,
+    gains,
+    inners,
+    gainses,
+    e_send,
+    e_recv,
     g_send,
     g_recv,
     own_sem,
@@ -674,9 +641,31 @@
         pltpu.make_async_copy(src, dst, x_sem.at[n])
         for n, (src, dst) in enumerate(((cot_hbm, cot), (dec_hbm, dec), (enc_hbm, enc)))
     ]
+    nexts = [
+        [ring_device(ring, position[ring] + 1 - 2 * way, core) for way in range(2)]
+        for ring in range(2)
+    ]
     owns = (att_own, qg_own, kg_own, vg_own)
     alls = (att_all, qg_all, kg_all, vg_all)
-    greet(plane_neighbours(x, y, core, s) + ring_neighbours(z))
+    group = z * 2 + t
+    sums = ((inner, inners, inner_out, group), (gains, gainses, gain_out, s))
+
+    def peer(n, r):
+        g = lax.rem(sums[n][3] + r, 16)
+        return ({"section": lax.div(g, 2), "tensor": lax.rem(g, 2)} if n == 0 else {"seq": g}), g
+
+    barrier = pltpu.get_barrier_semaphore()
+    near = plane_neighbours(x, y, core, s)
+    for device in near:
+        pl.semaphore_signal(barrier, inc=1, device_id=device, device_id_type=MESH)
+
+    def hello(r, _):
+        for n in range(2):
+            pl.semaphore_signal(barrier, inc=1, device_id=peer(n, r)[0], device_id_type=MESH)
+        return 0
+
+    lax.fori_loop(1, 16, hello, 0)
+    pl.semaphore_wait(barrier, len(near) + 30)
 
 
     def ring_block(n, place_z):
@@ -771,15 +760,15 @@
     def product(k, offset):
         sd, td = dest(k % 2, offset)
         if k == 0:
-            return dot(both(qg, sd * 128, 128), wq[td])
+            return dot_t(both(qg, sd * 128, 128), wq[td])
         if k == 1:
             return dot(both(att, sd * 128, 128), wo[td])
         base = sd * 256 + (k - 2) * 128
-        return dot(both(kg_all, base, 256), wk[td]) + dot(both(vg_all, base, 256), wv[td])
-
-    def across(k, i):
+        return dot_t(both(kg_all, base, 256), wk[td]) + dot_t(both(vg_all, base, 256), wv[td])
+
+    def across(k, i, four=0):
         return remote(
-            sib_out.at[k, lax.rem(i, 4)],
+            sib_out.at[k, four],
             sib_in.at[k, i],
             s_send.at[k, i],
             s_recv.at[k, i],
@@ -788,29 +777,30 @@
 
     def give(ks, i):
         half = lax.div(i, 2)
-        offset = 8 - half + lax.rem(i, 2) * (2 * half + 1)
+        four = lax.rem(i, 4)
+        offset = 8 - half + (i - 2 * half) * (2 * half + 1)
         for k in ks:
             total = product(k, offset)
 
             @pl.when(i >= 4)
             def _(k=k):
-                across(k, i - 4).wait_send()
-
-            sib_out[k, lax.rem(i, 4)] = total[128:].astype(BF16)
-            across(k, i).start()
-            mine[k % 2, lax.rem(i, 4)] = total[:128]
-
-    def onward(k, way, sub, j):
-        device = ring_device(k % 2, position[k % 2] + 1 - 2 * way, core)
+                across(k, i - 4, four).wait_send()
+
+            sib_out[k, four] = total[128:].astype(BF16)
+            across(k, i, four).start()
+            mine[k % 2, four] = total[:128]
+
+    def onward(k, way, sub, j, two):
         return remote(
-            chain_out.at[k, way, sub, lax.rem(j, 2)],
+            chain_out.at[k, way, sub, two],
             chain_in.at[k, way, sub, j + 1],
             c_send.at[k, way, sub, j],
             c_recv.at[k, way, sub, j],
-            device,
+            nexts[k % 2][way],
         )
 
     def chain_step(ks, j):
+        two = lax.rem(j, 2)
         for sub in range(2):
             part = slice(sub * 64, (sub + 1) * 64)
             for way in range(2):
@@ -819,25 +809,33 @@
                     @pl.when(j < 8 - way)
                     def _(k=k, way=way, sub=sub, part=part):
                         i = 2 * j + way
+                        four = 2 * two + way
                         if sub == 0:
                             across(k, i).wait_recv()
 
                         @pl.when(j > 0)
                         def _():
-                            onward(k, way, sub, j - 1).wait_recv()
+                            onward(k, way, sub, j - 1, two).wait_recv()
 
                         @pl.when(j > 1)
                         def _():
-                            onward(k, way, sub, j - 2).wait_send()
-
-                        total = mine[k % 2, lax.rem(i, 4), part] + sib_in[k, i, part].astype(F32)
+                            onward(k, way, sub, j - 2, two).wait_send()
+
+                        total = mine[k % 2, four, part] + sib_in[k, i, part].astype(F32)
                         total = total + chain_in[k, way, sub, j].astype(F32)
-                        chain_out[k, way, sub, lax.rem(j, 2)] = total.astype(BF16)
-                        onward(k, way, sub, j).start()
+                        chain_out[k, way, sub, two] = total.astype(BF16)
+                        onward(k, way, sub, j, two).start()
 
     def weight_swap(n):
         return remote(
-            grads_out.at[n], grads_in.at[n], w_send.at[n], w_recv.at[n], partner
+            grads_out.at[n], grads_in.at[n], w_send.at[n, 0], w_recv.at[n, 0], partner
+        )
+
+    def pair_swap(j):
+        n, m = 1 + lax.div(j, 4), lax.rem(j, 4)
+        rows = pl.ds(pl.multiple_of(m * 64, 64), 64)
+        return remote(
+            grads_out.at[n, rows], grads_in.at[n, rows], w_send.at[n, m], w_recv.at[n, m], partner
         )
 
     def weight_step(pairs, rows, j):
@@ -859,6 +857,13 @@
             @pl.when(j == 7)
             def _(a=a, n=n):
                 grads[n] = acc[a]
+
+    def pair_weights(place_z):
+        rows = pl.ds(pl.multiple_of(place_z * 512, 512), 512)
+        for a, left in enumerate((kg_all, vg_all)):
+            block = left[rows, :]
+            for f in range(2):
+                pair_acc[a, f] += t_dot(block, enc[f, rows, :])
 
     def scatter(ks, filler):
         give(ks, 0)
@@ -887,7 +892,7 @@
                 part = pl.ds(sub * 64, 64)
                 total = mine[k % 2, 3, part] + sib_in[k, 15, part].astype(F32)
                 for way in range(2):
-                    onward(k, way, sub, 7 - way).wait_recv()
+                    onward(k, way, sub, 7 - way, 0).wait_recv()
                     total = total + chain_in[k, way, sub, 8 - way].astype(F32)
                 outs[k][part, :] = total
         for k in ks:
@@ -895,31 +900,110 @@
                 across(k, i).wait_send()
             for way in range(2):
                 for sub in range(2):
-                    onward(k, way, sub, 6 - way).wait_send()
-                    onward(k, way, sub, 7 - way).wait_send()
+                    onward(k, way, sub, 6 - way, 0).wait_send()
+                    onward(k, way, sub, 7 - way, 1).wait_send()
 
     def token_filler(j):
         @pl.when(j == 0)
         def _():
             loads[0].wait()
             loads[1].wait()
+            loads[2].wait()
 
         weight_step(((0, qg, dec), (3, att, cot)), 512, j)
+
+        @pl.when(lax.rem(j, 2) == 0)
+        def _():
+            distance = lax.div(j, 2)
+            pair_weights(lax.rem(z + distance, DEPTH))
+
+            @pl.when(j > 0)
+            def _():
+                pair_weights(lax.rem(z + DEPTH - distance, DEPTH))
 
         @pl.when(lax.rem(j, 2) == 1)
         def _():
             ring_step((2, 3), lax.div(j, 2))
 
+    pair_acc[...] = jnp.zeros((2, 2, 256, 512), F32)
+    inner[...] = jnp.zeros((8, 128), F32)
+    gains[...] = jnp.zeros((8, 128), F32)
+    scale = lax.rsqrt(squares[...] / WIDTH + EPS)
+    scales = [jnp.broadcast_to(scale[n : n + 1], (128, 128)).T[:, :1] for n in range(3)]
     scatter((0, 1), token_filler)
-    loads[2].wait()
-    scatter((2, 3), lambda j: weight_step(((1, kg_all, enc), (2, vg_all, enc)), 1024, j))
+
+    def sum_rows(n):
+        part = slice(max(n - 1, 0) * 128, max(n - 1, 0) * 128 + 128)
+        upstream = dec_out[...] if n == 0 else enc_out[part, :]
+        unit = (hidden if n == 0 else neigh)[part, :].astype(F32) * scales[n]
+        product_of = upstream * unit
+        gain = (dec_gain if n == 0 else enc_gain)[...]
+        column = jnp.sum(product_of * gain, axis=1, keepdims=True)
+        inner[n : n + 1] = jnp.broadcast_to(column, (128, 128)).T[:1]
+        row = jnp.sum(product_of, axis=0, keepdims=True)
+        first = 0 if n == 0 else 4
+        for m in range(4):
+            gains[first + m : first + m + 1] += row[:, m * 128 : (m + 1) * 128]
+
+    def pair_filler(j):
+        @pl.when(j == 0)
+        def _():
+            pair_weights(lax.rem(z + 4, DEPTH))
+            for a in range(2):
+                grads_out[1 + a] = pair_acc[a, 1 - t].astype(BF16)
+                grads[1 + a] = pair_acc[a, t]
+
+        pair_swap(j).start()
+
+        @pl.when(j == 1)
+        def _():
+            sum_rows(0)
+
+    scatter((2, 3), pair_filler)
+
+
+    sum_rows(1)
+    sum_rows(2)
+
+    def tell(n, r):
+        src, slots, _out, own = sums[n]
+        return remote(src, slots.at[own], e_send.at[n, r], e_recv.at[n, own], peer(n, r)[0])
+
+    def tell_all(r, _):
+        for n in range(2):
+            tell(n, r).start()
+        return 0
+
+    def hear_all(r, _):
+        for n in range(2):
+            src, slots, _out, own = sums[n]
+            device, g = peer(n, r)
+            remote(src, slots.at[g], e_send.at[n, r], e_recv.at[n, g], device).wait_recv()
+        return 0
+
+    def told_all(r, _):
+        for n in range(2):
+            tell(n, r).wait_send()
+        return 0
+
+    lax.fori_loop(1, 16, tell_all, 0)
+    for src, slots, _out, own in sums:
+        slots[own] = src[...]
 
     for n in range(4):
         for way in range(2):
             for j in range(ring_hops(n, way)):
                 ring_copy(n, way, j).wait_send()
-    for n in range(4):
-        weight_swap(n).wait()
+    weight_swap(0).wait()
+    weight_swap(3).wait()
+    lax.fori_loop(0, 8, lambda j, _: (pair_swap(j).wait(), 0)[1], 0)
+    lax.fori_loop(1, 16, hear_all, 0)
+    for src, slots, out, own in sums:
+        total = slots[0]
+        for g in range(1, 16):
+            total = total + slots[g]
+        out[...] = total
+    lax.fori_loop(1, 16, told_all, 0)
 
 
 def back(*args):
@@ -932,9 +1016,11 @@
             sds((256, 512), F32),
             sds((4, 256, 512), F32),
             sds((4, 256, 512), BF16),
+            sds((8, 128), F32),
+            sds((8, 128), F32),
         ],
-        in_specs=[VMEM] * 8 + [ANY] * 3 + [SMEM],
-        out_specs=[VMEM] * 5,
+        in_specs=[VMEM] * 8 + [ANY] * 3 + [SMEM] + [VMEM] * 5,
+        out_specs=[VMEM] * 7,
         scratch_shapes=[
             pltpu.VMEM((32, 64, 256), BF16),
             pltpu.VMEM((32, 64, 256), BF16),
@@ -951,7 +1037,14 @@
             pltpu.VMEM((4, 2, 2, 9, 64, 512), BF16),
             pltpu.VMEM((2, 4, 128, 512), F32),
             pltpu.VMEM((2, 256, 512), F32),
+            pltpu.VMEM((2, 2, 256, 512), F32),
             pltpu.VMEM((4, 256, 512), BF16),
+            pltpu.VMEM((8, 128), F32),
+            pltpu.VMEM((8, 128), F32),
+            pltpu.VMEM((16, 8, 128), F32),
+            pltpu.VMEM((16, 8, 128), F32),
+            DMA((2, 16)),
+            DMA((2, 16)),
             DMA((4, 2, 4)),
             DMA((4, 2, 4)),
             DMA((4,)),
@@ -960,16 +1053,11 @@
             DMA((4, 16)),
             DMA((4, 2, 2, 8)),
             DMA((4, 2, 2, 8)),
-            DMA((4,)),
-            DMA((4,)),
+            DMA((4, 4)),
+            DMA((4, 4)),
         ],
-        compiler_params=params(2, 62),
+        compiler_params=params(2, 63),
     )(*args)
-
-
-def pack(*vectors):
-    flat = jnp.concatenate(vectors)
-    return jnp.pad(flat, (0, 1024 - flat.shape[0])).reshape(8, 128)
 
 
 def body(
@@ -1013,7 +1101,7 @@
         bias,
         inverse,
     )
-    dec_input, out_total, enc_input, own, got = back(
+    dec_input, out_total, enc_input, own, got, inner, gains = back(
         att,
         qg,
         kg,
@@ -1026,8 +1114,13 @@
         dec_all.reshape(2, 2048, 512),
         enc_all,
         neighbour_ids,
+        hidden,
+        neigh_states,
+        dec_gain[None],
+        enc_gain[None],
+        squares,
     )
-    scales = lax.rsqrt(squares[0] / WIDTH + EPS)
+    scales = lax.rsqrt(squares.reshape(-1)[:384] / WIDTH + EPS)
     dec_scale, enc_scale = scales[:rows, None], scales[rows:, None]
     dec_hat = dec_rows * dec_scale
     enc_hat = enc_rows * enc_scale
@@ -1040,14 +1133,6 @@
     layer_out = (dec_rows + out_total).astype(BF16)
     dec_scaled = dec_gain * dec_input
     enc_scaled = enc_gain * enc_input
-    inner, gains = small_sums(
-        [
-            pack(jnp.sum(dec_scaled * dec_hat, axis=1), jnp.sum(enc_scaled * enc_hat, axis=1)),
-            pack(jnp.sum(dec_input * dec_hat, axis=0), jnp.sum(enc_input * enc_hat, axis=0)),
-        ],
-        ("st", "seq"),
-        3,
-    )
     inner = inner.reshape(-1)[:384] / WIDTH
     gains = gains.reshape(-1)
     hidden_grad = cotangent.astype(F32) + dec_scale * (

time: 307 us -> 280 us (0.912)
  Pallas kernels: 287 us -> 262 us
    pallas_call x1, Pallas kernels: 150 us -> 127 us  [front(): pl.pallas_call(front_kernel, out_shape=[sds((2, 32, 64, 512), BF16), sds(...]
    pallas_call x1 -> x0, Pallas kernels: 12.3 us -> none  [small_sums(): pl.pallas_call(functools.partial(small_kernel, groups), out_shape=[jax.Sh...]
    pallas_call x1, Pallas kernels: 125 us -> 135 us  [back(): pl.pallas_call(back_kernel, out_shape=[sds((128, 512), F32), sds((128, 51...]
where the time goes in v5:
time: 280 us
  Pallas kernels  262 us (94%)
  other arithmetic  10.6 us (4%)
  local copies, waits for them, and re-layouts  5.96 us (2%)
    pallas_call x1, Pallas kernels, back(): pl.pallas_call(back_kernel, out_shape=[sds((128, 512), F32), sds((128, 51...  135 us
    pallas_call x1, Pallas kernels, front(): pl.pallas_call(front_kernel, out_shape=[sds((2, 32, 64, 512), BF16), sds(...  127 us

profile of v5, /device:TPU:1, one launch (start us, length us, event | category | flops | bytes accessed | tf_op | source)
XLA Modules:
  0.0 279.5 jit_solution(18214153131099527914)
XLA Ops:
  0.6 1.3 fusion.5.bias
  2.0 1.3 select_reduce_fusion.inverse
  3.3 127.3 %shard_map.178 = (bf16[2,32,64,512]{3,2,1,0:T(8,128)(2,1)}, bf16[2,32,64,512]{3,2,1,0:T(8,128)(2,1)}, bf16[2,4096,512]{2,1,0:T(8,128)(2,1)}, bf16[2,512,256]{2,1...) custom-call(bf16[2,64,512]{2,1,0:T(8,128)(2,1)} %bitcast.35, ...), custom_call_target="tpu_custom_call" | custom-call | tf_op jit(solution)/shard_map/pallas_call | solution.py:525
  130.6 134.9 %shard_map.179 = (f32[128,512]{1,0:T(8,128)}, f32[128,512]{1,0:T(8,128)}, f32[256,512]{1,0:T(8,128)}, f32[4,256,512]{2,1,0:T(8,128)}, bf16[4,256,512]{2,1,0:T(8,...) custom-call(bf16[4,64,256]{2,1,0:T(8,128)(2,1)} %get-tuple-element.28.att_own, ...), custom_call_target="tpu_custom_call" | custom-call | tf_op jit(solution)/shard_map/pallas_call | solution.py:1011
  265.4 1.5 convert_element_type.19
  267.0 3.0 %maximum_select_fusion = f32[4,512,512]{2,1,0:T(8,128)S(1)} fusion(f32[4,256,512]{2,1,0:T(8,128)S(1)} %convert_element_type.19, f32[4,256,512]{2,1,0:T(8,128)} %get-tuple-element.45, pred[]{:T(512)S(6)} %eq.19), kind=kLoop, calls=%fused_computation | loop fusion | flops 3145728 | bytes 8388609 | tf_op jit(solution)/shard_map/jit(_where)/select_n | solution.py:1128
  270.0 1.4 slice_bitcast_fusion
  271.4 0.0 copy-start.7
  271.4 0.0 copy-start
  271.4 0.0 copy-start.5
  271.4 0.0 copy-start.1
  271.4 0.0 copy-start.6
  271.4 0.0 copy-start.8
  271.5 1.3 copy.23
  272.8 0.0 copy-start.2
  272.8 0.0 copy-start.3
  272.8 0.0 copy-start.4
  272.8 1.3 copy.24
  274.1 1.3 copy.25
  275.4 0.7 slice_multiply_fusion
  276.1 0.0 copy-done.7
  276.1 0.0 copy-done
  276.1 0.0 copy-done.5
  276.1 0.0 copy-done.2
  276.1 1.0 subtract_multiply_fusion
  277.1 0.0 copy-done.1
  277.1 0.0 copy-done.6
  277.1 0.0 copy-done.3
  277.1 0.0 copy-done.4
  277.1 1.8 fusion.4
  278.9 0.0 copy-done.8
  278.9 0.6 slice_bitcast_fusion.4
  (3 shorter events, 0.0 us)
Async XLA Ops:
  271.4 4.6 %copy-start.7 = (f32[8,128]{1,0:T(8,128)S(1)}, f32[8,128]{1,0:T(8,128)}, u32[]{:S(2)}) copy-start(f32[8,128]{1,0:T(8,128)} %get-tuple-element.39.squares) | copy-start | bytes 12292
  271.4 4.6 %copy-start = (bf16[256,512]{1,0:T(8,128)(2,1)S(1)}, bf16[256,512]{1,0:T(8,128)(2,1)}, u32[]{:S(2)}) copy-start(bf16[256,512]{1,0:T(8,128)(2,1)} %neigh.3) | copy-start | bytes 786436
  271.4 4.7 %copy-start.5 = (f32[512]{0:T(512)S(1)}, f32[512]{0:T(512)}, u32[]{:S(2)}) copy-start(f32[512]{0:T(512)} %param.14) | copy-start | bytes 6148
  271.4 5.7 %copy-start.1 = (bf16[128,512]{1,0:T(8,128)(2,1)S(1)}, bf16[128,512]{1,0:T(8,128)(2,1)}, u32[]{:S(2)}) copy-start(bf16[128,512]{1,0:T(8,128)(2,1)} %hidden.1) | copy-start | bytes 393220
  271.4 5.7 %copy-start.6 = (f32[512]{0:T(512)S(1)}, f32[512]{0:T(512)}, u32[]{:S(2)}) copy-start(f32[512]{0:T(512)} %param.12) | copy-start | bytes 6148
  271.4 7.5 %copy-start.8 = (f32[8,128]{1,0:T(8,128)S(1)}, f32[8,128]{1,0:T(8,128)}, u32[]{:S(2)}) copy-start(f32[8,128]{1,0:T(8,128)} %get-tuple-element.44) | copy-start | bytes 12292
  272.8 3.3 %copy-start.2 = (f32[256,512]{1,0:T(8,128)S(1)}, f32[256,512]{1,0:T(8,128)}, u32[]{:S(2)}) copy-start(f32[256,512]{1,0:T(8,128)} %get-tuple-element.43) | copy-start | bytes 1572868
  272.8 4.3 %copy-start.3 = (bf16[128,512]{1,0:T(8,128)(2,1)S(1)}, bf16[128,512]{1,0:T(8,128)(2,1)}, u32[]{:S(2)}) copy-start(bf16[128,512]{1,0:T(8,128)(2,1)} %param.21) | copy-start | bytes 393220
  272.8 4.3 %copy-start.4 = (f32[128,512]{1,0:T(8,128)S(1)}, f32[128,512]{1,0:T(8,128)}, u32[]{:S(2)}) copy-start(f32[128,512]{1,0:T(8,128)} %get-tuple-element.41) | copy-start | bytes 786436

commit v6 on v5

--- a/solution.py
+++ b/solution.py
@@ -149,10 +149,10 @@
     cot_all,
     dec_all,
     enc_all,
-    wq,
-    wk,
-    wv,
-    wo,
+    wq_out,
+    wk_out,
+    wv_out,
+    wo_out,
     att,
     qg,
     kg,
@@ -161,6 +161,10 @@
     cot_v,
     dec_v,
     enc_v,
+    wq,
+    wk,
+    wv,
+    wo,
     dec,
     enc,
     stat,
@@ -410,9 +414,20 @@
     gather_end((2, 3))
     stores = [
         pltpu.make_async_copy(src, dst, out_sem.at[n])
-        for n, (src, dst) in enumerate(((cot_v, cot_all), (dec_v, dec_all), (enc_v, enc_all)))
+        for n, (src, dst) in enumerate(
+            (
+                (cot_v, cot_all),
+                (dec_v, dec_all),
+                (enc_v, enc_all),
+                (wk, wk_out),
+                (wv, wv_out),
+                (wq, wq_out),
+                (wo, wo_out),
+            )
+        )
     ]
-    stores[2].start()
+    for copy in stores[2:5]:
+        copy.start()
 
 
     def pair_part(d, h):
@@ -472,9 +487,9 @@
     def pair_item(w, _):
         item(pairs, w)
 
-        @pl.when((lax.rem(w, 2) == 1) & (w < 12))
-        def _():
-            gather_step((0, 1), lax.div(w, 2) + 2)
+        @pl.when((lax.rem(w, 2) == 1) & (w > 2))
+        def _():
+            gather_step((0, 1), lax.div(w, 2) + 1)
 
         return 0
 
@@ -482,10 +497,19 @@
     gather_end((0, 1))
     swapped(2)
     swapped(3)
-    stores[0].start()
-    stores[1].start()
-    lax.fori_loop(0, 14, lambda w, _: (item(queries, w), 0)[1], 0)
-    last(pairs)
+    for copy in stores[:2] + stores[5:]:
+        copy.start()
+
+    def query_item(w, _):
+        item(queries, w)
+
+        @pl.when(w == 7)
+        def _():
+            last(pairs)
+
+        return 0
+
+    lax.fori_loop(0, 14, query_item, 0)
     last(queries)
 
     for h in range(2):
@@ -538,12 +562,16 @@
             sds((512, 256), BF16),
             sds((8, 128), F32),
         ],
-        in_specs=[VMEM] * 10 + [SMEM],
-        out_specs=[ANY] * 3 + [VMEM] * 9,
+        in_specs=[VMEM] * 5 + [ANY] * 4 + [VMEM, SMEM],
+        out_specs=[ANY] * 7 + [VMEM] * 5,
         scratch_shapes=[
             pltpu.VMEM((2, 32, 64, 512), BF16),
             pltpu.VMEM((2, 32, 64, 512), BF16),
             pltpu.VMEM((2, 4096, 512), BF16),
+            pltpu.VMEM((2, 512, 256), BF16),
+            pltpu.VMEM((2, 512, 256), BF16),
+            pltpu.VMEM((2, 512, 256), BF16),
+            pltpu.VMEM((2, 256, 512), BF16),
             pltpu.VMEM((2, 64, 512), BF16),
             pltpu.VMEM((256, 512), BF16),
             pltpu.VMEM((8, 128), F32),
@@ -564,7 +592,7 @@
             DMA((4,)),
             DMA((4,)),
             DMA((4,)),
-            DMA((3,)),
+            DMA((7,)),
             DMA((4, 4)),
             DMA((4, 4)),
             DMA((4, 4)),
@@ -579,10 +607,10 @@
     qg_own,
     kg_own,
     vg_own,
-    wq,
-    wk,
-    wv,
-    wo,
+    wq_hbm,
+    wk_hbm,
+    wv_hbm,
+    wo_hbm,
     cot_hbm,
     dec_hbm,
     enc_hbm,
@@ -596,7 +624,9 @@
     out_out,
     enc_out,
     grads,
+    out_grad,
     grads_in,
+    out_grad_in,
     inner_out,
     gain_out,
     att_all,
@@ -608,14 +638,20 @@
     cot,
     dec,
     enc,
+    wq,
+    wk,
+    wv,
+    wo,
     sib_out,
     sib_in,
     chain_out,
     chain_in,
     mine,
     acc,
+    out_acc,
     pair_acc,
     grads_out,
+    out_grad_out,
     inner,
     gains,
     inners,
@@ -632,6 +668,7 @@
     c_recv,
     w_send,
     w_recv,
+    o_sem,
 ):
     z, s, t, x, y, core = place()
     sibling = {"seq": s + 1 - 2 * core}
@@ -639,7 +676,17 @@
     position = (ring_position(0, x, y), ring_position(1, x, y))
     loads = [
         pltpu.make_async_copy(src, dst, x_sem.at[n])
-        for n, (src, dst) in enumerate(((cot_hbm, cot), (dec_hbm, dec), (enc_hbm, enc)))
+        for n, (src, dst) in enumerate(
+            (
+                (cot_hbm, cot),
+                (dec_hbm, dec),
+                (enc_hbm, enc),
+                (wq_hbm, wq),
+                (wk_hbm, wk),
+                (wv_hbm, wv),
+                (wo_hbm, wo),
+            )
+        )
     ]
     nexts = [
         [ring_device(ring, position[ring] + 1 - 2 * way, core) for way in range(2)]
@@ -715,16 +762,31 @@
     ring_first((0, 1))
     for n in range(4):
         keep(n).start()
-    for copy in loads:
+    for copy in loads[2:] + loads[:2]:
         copy.start()
     for k in range(4):
         for way in range(2):
             for sub in range(2):
                 chain_in[k, way, sub, 0] = jnp.zeros((64, 512), BF16)
 
+    def pair_weights(place_z):
+        rows = pl.ds(pl.multiple_of(place_z * 512, 512), 512)
+        block = jnp.concatenate([kg_all[rows, :], vg_all[rows, :]], axis=1)
+        for f in range(2):
+            pair_acc[f] += t_dot(enc[f, rows, :], block)
+
+    pair_acc[...] = jnp.zeros((2, 512, 512), F32)
+
     def first_steps(j, _):
         ring_step((0, 1), j)
 
+        @pl.when(j == 1)
+        def _():
+            loads[2].wait()
+            keep(2).wait()
+            keep(3).wait()
+            pair_weights(z)
+
         @pl.when(j == 2)
         def _():
             ring_first((2, 3))
@@ -732,8 +794,10 @@
         return 0
 
     lax.fori_loop(0, 4, first_steps, 0)
-    for n in range(4):
-        keep(n).wait()
+    keep(0).wait()
+    keep(1).wait()
+    for copy in loads[3:]:
+        copy.wait()
 
     def token_order(b, _):
         rows = pl.ds(pl.multiple_of(b * 64, 64), 64)
@@ -826,44 +890,53 @@
                         chain_out[k, way, sub, two] = total.astype(BF16)
                         onward(k, way, sub, j, two).start()
 
-    def weight_swap(n):
+    def own_store(n):
+        if n == 0:
+            src, dst = acc, grads.at[0]
+        elif n == 3:
+            src, dst = out_acc, out_grad
+        else:
+            src, dst = pair_acc.at[t, :, pl.ds((n - 1) * 256, 256)], grads.at[n]
+        return pltpu.make_async_copy(src, dst, o_sem.at[n])
+
+    def query_swap():
         return remote(
-            grads_out.at[n], grads_in.at[n], w_send.at[n, 0], w_recv.at[n, 0], partner
+            grads_out.at[0], grads_in.at[0], w_send.at[0, 0], w_recv.at[0, 0], partner
         )
+
+    def out_swap():
+        return remote(out_grad_out, out_grad_in, w_send.at[3, 0], w_recv.at[3, 0], partner)
 
     def pair_swap(j):
         n, m = 1 + lax.div(j, 4), lax.rem(j, 4)
-        rows = pl.ds(pl.multiple_of(m * 64, 64), 64)
+        rows = pl.ds(pl.multiple_of(m * 128, 128), 128)
         return remote(
             grads_out.at[n, rows], grads_in.at[n, rows], w_send.at[n, m], w_recv.at[n, m], partner
         )
 
-    def weight_step(pairs, rows, j):
+    def weight_step(j):
         f = 1 - t + lax.div(j, 4) * (2 * t - 1)
-        here = pl.ds(pl.multiple_of(lax.rem(j, 4) * rows, rows), rows)
-        for a, (n, left, right) in enumerate(pairs):
-
-            @pl.when(lax.rem(j, 4) == 0)
-            def _(a=a):
-                acc[a] = jnp.zeros((256, 512), F32)
-
-            acc[a] += t_dot(left[here, :], right[f, here, :])
-
-            @pl.when(j == 3)
-            def _(a=a, n=n):
-                grads_out[n] = acc[a].astype(BF16)
-                weight_swap(n).start()
-
-            @pl.when(j == 7)
-            def _(a=a, n=n):
-                grads[n] = acc[a]
-
-    def pair_weights(place_z):
-        rows = pl.ds(pl.multiple_of(place_z * 512, 512), 512)
-        for a, left in enumerate((kg_all, vg_all)):
-            block = left[rows, :]
-            for f in range(2):
-                pair_acc[a, f] += t_dot(block, enc[f, rows, :])
+        here = pl.ds(pl.multiple_of(lax.rem(j, 4) * 512, 512), 512)
+
+        @pl.when(lax.rem(j, 4) == 0)
+        def _():
+            acc[...] = jnp.zeros((512, 256), F32)
+            out_acc[...] = jnp.zeros((256, 512), F32)
+
+        acc[...] += t_dot(dec[f, here, :], qg[here, :])
+        out_acc[...] += t_dot(att[here, :], cot[f, here, :])
+
+        @pl.when(j == 3)
+        def _():
+            grads_out[0] = acc[...].astype(BF16)
+            out_grad_out[...] = out_acc[...].astype(BF16)
+            query_swap().start()
+            out_swap().start()
+
+        @pl.when(j == 7)
+        def _():
+            own_store(0).start()
+            own_store(3).start()
 
     def scatter(ks, filler):
         give(ks, 0)
@@ -908,24 +981,19 @@
         def _():
             loads[0].wait()
             loads[1].wait()
-            loads[2].wait()
-
-        weight_step(((0, qg, dec), (3, att, cot)), 512, j)
-
-        @pl.when(lax.rem(j, 2) == 0)
+
+        weight_step(j)
+
+        @pl.when((lax.rem(j, 2) == 0) & (j > 0))
         def _():
             distance = lax.div(j, 2)
             pair_weights(lax.rem(z + distance, DEPTH))
-
-            @pl.when(j > 0)
-            def _():
-                pair_weights(lax.rem(z + DEPTH - distance, DEPTH))
+            pair_weights(lax.rem(z + DEPTH - distance, DEPTH))
 
         @pl.when(lax.rem(j, 2) == 1)
         def _():
             ring_step((2, 3), lax.div(j, 2))
 
-    pair_acc[...] = jnp.zeros((2, 2, 256, 512), F32)
     inner[...] = jnp.zeros((8, 128), F32)
     gains[...] = jnp.zeros((8, 128), F32)
     scale = lax.rsqrt(squares[...] / WIDTH + EPS)
@@ -950,8 +1018,9 @@
         def _():
             pair_weights(lax.rem(z + 4, DEPTH))
             for a in range(2):
-                grads_out[1 + a] = pair_acc[a, 1 - t].astype(BF16)
-                grads[1 + a] = pair_acc[a, t]
+                half = slice(a * 256, (a + 1) * 256)
+                grads_out[1 + a] = pair_acc[1 - t, :, half].astype(BF16)
+                own_store(1 + a).start()
 
         pair_swap(j).start()
 
@@ -994,8 +1063,10 @@
         for way in range(2):
             for j in range(ring_hops(n, way)):
                 ring_copy(n, way, j).wait_send()
-    weight_swap(0).wait()
-    weight_swap(3).wait()
+    query_swap().wait()
+    out_swap().wait()
+    for n in range(4):
+        own_store(n).wait()
     lax.fori_loop(0, 8, lambda j, _: (pair_swap(j).wait(), 0)[1], 0)
     lax.fori_loop(1, 16, hear_all, 0)
     for src, slots, out, own in sums:
@@ -1014,13 +1085,15 @@
             sds((128, 512), F32),
             sds((128, 512), F32),
             sds((256, 512), F32),
-            sds((4, 256, 512), F32),
-            sds((4, 256, 512), BF16),
+            sds((3, 512, 256), F32),
+            sds((256, 512), F32),
+            sds((3, 512, 256), BF16),
+            sds((256, 512), BF16),
             sds((8, 128), F32),
             sds((8, 128), F32),
         ],
-        in_specs=[VMEM] * 8 + [ANY] * 3 + [SMEM] + [VMEM] * 5,
-        out_specs=[VMEM] * 7,
+        in_specs=[VMEM] * 4 + [ANY] * 7 + [SMEM] + [VMEM] * 5,
+        out_specs=[VMEM] * 3 + [ANY] * 4 + [VMEM] * 2,
         scratch_shapes=[
             pltpu.VMEM((32, 64, 256), BF16),
             pltpu.VMEM((32, 64, 256), BF16),
@@ -1031,14 +1104,20 @@
             pltpu.VMEM((2, 2048, 512), BF16),
             pltpu.VMEM((2, 2048, 512), BF16),
             pltpu.VMEM((2, 4096, 512), BF16),
+            pltpu.VMEM((2, 512, 256), BF16),
+            pltpu.VMEM((2, 512, 256), BF16),
+            pltpu.VMEM((2, 512, 256), BF16),
+            pltpu.VMEM((2, 256, 512), BF16),
             pltpu.VMEM((4, 4, 128, 512), BF16),
             pltpu.VMEM((4, 16, 128, 512), BF16),
             pltpu.VMEM((4, 2, 2, 2, 64, 512), BF16),
             pltpu.VMEM((4, 2, 2, 9, 64, 512), BF16),
             pltpu.VMEM((2, 4, 128, 512), F32),
-            pltpu.VMEM((2, 256, 512), F32),
-            pltpu.VMEM((2, 2, 256, 512), F32),
-            pltpu.VMEM((4, 256, 512), BF16),
+            pltpu.VMEM((512, 256), F32),
+            pltpu.VMEM((256, 512), F32),
+            pltpu.VMEM((2, 512, 512), F32),
+            pltpu.VMEM((3, 512, 256), BF16),
+            pltpu.VMEM((256, 512), BF16),
             pltpu.VMEM((8, 128), F32),
             pltpu.VMEM((8, 128), F32),
             pltpu.VMEM((16, 8, 128), F32),
@@ -1048,13 +1127,14 @@
             DMA((4, 2, 4)),
             DMA((4, 2, 4)),
             DMA((4,)),
-            DMA((3,)),
+            DMA((7,)),
             DMA((4, 16)),
             DMA((4, 16)),
             DMA((4, 2, 2, 8)),
             DMA((4, 2, 2, 8)),
             DMA((4, 4)),
             DMA((4, 4)),
+            DMA((4,)),
         ],
         compiler_params=params(2, 63),
     )(*args)
@@ -1101,7 +1181,7 @@
         bias,
         inverse,
     )
-    dec_input, out_total, enc_input, own, got, inner, gains = back(
+    dec_input, out_total, enc_input, own, out_own, got, out_got, inner, gains = back(
         att,
         qg,
         kg,
@@ -1124,12 +1204,17 @@
     dec_scale, enc_scale = scales[:rows, None], scales[rows:, None]
     dec_hat = dec_rows * dec_scale
     enc_hat = enc_rows * enc_scale
-    got = got.astype(F32)
-    joined = jnp.where(
-        t == 0, jnp.concatenate([own, got], 1), jnp.concatenate([got, own], 1)
-    )
-    weight_grads = [joined[n].T for n in range(3)]
-    out_weight_grad = joined[3]
+
+    def join(mine, theirs, axis):
+        theirs = theirs.astype(F32)
+        return jnp.where(
+            t == 0,
+            jnp.concatenate([mine, theirs], axis),
+            jnp.concatenate([theirs, mine], axis),
+        )
+
+    weight_grads = [join(own[n], got[n], 1) for n in range(3)]
+    out_weight_grad = join(out_own, out_got, 0)
     layer_out = (dec_rows + out_total).astype(BF16)
     dec_scaled = dec_gain * dec_input
     enc_scaled = enc_gain * enc_input

time: 280 us -> 271 us (0.968)
  Pallas kernels: 262 us -> 256 us
  local copies, waits for them, and re-layouts: 5.96 us -> 2.16 us
    pallas_call x1, Pallas kernels: 135 us -> 127 us  [back(): pl.pallas_call(back_kernel, out_shape=[sds((128, 512), F32), sds((128, 51...]
    unnamed x21 -> x24, local copies, waits for them, and re-layouts: 3.96 us -> 0.06 us
where the time goes in v6:
time: 271 us
  Pallas kernels  256 us (94%)
  other arithmetic  11.5 us (4%)
    pallas_call x1, Pallas kernels, front(): pl.pallas_call(front_kernel, out_shape=[sds((2, 32, 64, 512), BF16), sds(...  130 us
    pallas_call x1, Pallas kernels, back(): pl.pallas_call(back_kernel, out_shape=[sds((128, 512), F32), sds((128, 51...  127 us

profile of v6, /device:TPU:1, one launch (start us, length us, event | category | flops | bytes accessed | tf_op | source)
XLA Modules:
  0.0 270.6 jit_solution(5998681004790209115)
XLA Ops:
  0.6 1.3 fusion.5.bias
  2.0 1.3 select_reduce_fusion.inverse
  3.3 129.6 %shard_map.178 = (bf16[2,32,64,512]{3,2,1,0:T(8,128)(2,1)}, bf16[2,32,64,512]{3,2,1,0:T(8,128)(2,1)}, bf16[2,4096,512]{2,1,0:T(8,128)(2,1)}, bf16[2,512,256]{2,1...) custom-call(bf16[2,64,512]{2,1,0:T(8,128)(2,1)} %bitcast.36, ...), custom_call_target="tpu_custom_call" | custom-call | tf_op jit(solution)/shard_map/pallas_call | solution.py:549
  132.8 126.5 %shard_map.179 = (f32[128,512]{1,0:T(8,128)}, f32[128,512]{1,0:T(8,128)}, f32[256,512]{1,0:T(8,128)}, f32[3,512,256]{2,1,0:T(8,128)}, f32[256,512]{1,0:T(8,128)}...) custom-call(bf16[4,64,256]{2,1,0:T(8,128)(2,1)} %get-tuple-element.30.att_own, ...), custom_call_target="tpu_custom_call" | custom-call | tf_op jit(solution)/shard_map/pallas_call | solution.py:1082
  259.4 0.0 copy-start.4
  259.4 1.5 slice_bitcast_fusion
  260.9 2.0 bitcast_convert_fusion
  262.9 0.0 copy-done.4
  262.9 0.1 convert_element_type.43
  263.0 0.0 copy-start.11
  263.0 0.0 copy-start.9
  263.0 0.0 copy-start
  263.0 0.0 copy-start.2
  263.0 0.0 copy-start.7
  263.0 0.0 copy-start.1
  263.1 0.0 copy-start.3
  263.1 0.0 copy-start.5
  263.1 0.0 copy-start.6
  263.1 0.0 copy-start.8
  263.1 3.3 %maximum_select_fusion.2 = (f32[512,512]{1,0:T(8,128)}, f32[512,512]{1,0:T(8,128)}) fusion(f32[512,256]{1,0:T(8,128)} %get-tuple-element.54, f32[512,256]{1,0:T(8,128)S(1)} %get-tuple-element.51, pred[]{:T(512)S(6)} %eq.22, f32[256,512]{1,0:T(8,128)} %get-tuple-element.49, f32[256,512]{1,0:T(8,128)S(1)} %convert_element_type.43), kind=kLoop, calls=%fused_computation.2 | loop fusion | flops 1572864 | bytes 4194305 | tf_op jit(solution)/shard_map/jit(_where)/select_n | solution.py:1210
  266.4 0.0 copy-start.10
  266.4 1.7 maximum_select_fusion
  268.0 0.0 copy-done.11
  268.1 0.0 copy-done.9
  268.1 0.0 copy-done
  268.1 0.0 copy-done.2
  268.1 0.0 copy-done.7
  268.1 1.0 subtract_multiply_fusion
  269.1 0.0 copy-done.1
  269.1 0.0 copy-done.3
  269.1 0.0 copy-done.5
  269.1 0.0 copy-done.6
  269.1 0.0 copy-done.8
  269.1 0.9 fusion.4
  270.0 0.0 copy-done.10
  270.0 0.6 slice_bitcast_fusion.3
  (4 shorter events, 0.0 us)
Async XLA Ops:
  259.4 3.6 %copy-start.4 = (bf16[256,512]{1,0:T(8,128)(2,1)S(1)}, bf16[256,512]{1,0:T(8,128)(2,1)}, u32[]{:S(2)}) copy-start(bf16[256,512]{1,0:T(8,128)(2,1)} %get-tuple-element.50) | copy-start | bytes 786436
  263.0 5.1 %copy-start.11 = (f32[8,128]{1,0:T(8,128)S(1)}, f32[8,128]{1,0:T(8,128)}, u32[]{:S(2)}) copy-start(f32[8,128]{1,0:T(8,128)} %get-tuple-element.44) | copy-start | bytes 12292
  263.0 5.1 %copy-start.9 = (f32[8,128]{1,0:T(8,128)S(1)}, f32[8,128]{1,0:T(8,128)}, u32[]{:S(2)}) copy-start(f32[8,128]{1,0:T(8,128)} %get-tuple-element.41.squares) | copy-start | bytes 12292
  263.0 5.1 %copy-start = (bf16[256,512]{1,0:T(8,128)(2,1)S(1)}, bf16[256,512]{1,0:T(8,128)(2,1)}, u32[]{:S(2)}) copy-start(bf16[256,512]{1,0:T(8,128)(2,1)} %neigh.3) | copy-start | bytes 786436
  263.0 5.1 %copy-start.2 = (f32[256,512]{1,0:T(8,128)S(1)}, f32[256,512]{1,0:T(8,128)}, u32[]{:S(2)}) copy-start(f32[256,512]{1,0:T(8,128)} %get-tuple-element.45) | copy-start | bytes 1572868
  263.0 5.1 %copy-start.7 = (f32[512]{0:T(512)S(1)}, f32[512]{0:T(512)}, u32[]{:S(2)}) copy-start(f32[512]{0:T(512)} %param.14) | copy-start | bytes 6148
  263.0 6.1 %copy-start.1 = (bf16[128,512]{1,0:T(8,128)(2,1)S(1)}, bf16[128,512]{1,0:T(8,128)(2,1)}, u32[]{:S(2)}) copy-start(bf16[128,512]{1,0:T(8,128)(2,1)} %hidden.1) | copy-start | bytes 393220
  263.1 6.1 %copy-start.3 = (bf16[128,512]{1,0:T(8,128)(2,1)S(1)}, bf16[128,512]{1,0:T(8,128)(2,1)}, u32[]{:S(2)}) copy-start(bf16[128,512]{1,0:T(8,128)(2,1)} %param.21) | copy-start | bytes 393220
  263.1 6.1 %copy-start.5 = (f32[128,512]{1,0:T(8,128)S(1)}, f32[128,512]{1,0:T(8,128)}, u32[]{:S(2)}) copy-start(f32[128,512]{1,0:T(8,128)} %get-tuple-element.43) | copy-start | bytes 786436
  263.1 6.0 %copy-start.6 = (f32[128,512]{1,0:T(8,128)S(1)}, f32[128,512]{1,0:T(8,128)}, u32[]{:S(2)}) copy-start(f32[128,512]{1,0:T(8,128)} %get-tuple-element.42) | copy-start | bytes 786436
  263.1 6.0 %copy-start.8 = (f32[512]{0:T(512)S(1)}, f32[512]{0:T(512)}, u32[]{:S(2)}) copy-start(f32[512]{0:T(512)} %param.12) | copy-start | bytes 6148
  266.4 3.6 %copy-start.10 = (f32[8,128]{1,0:T(8,128)S(1)}, f32[8,128]{1,0:T(8,128)}, u32[]{:S(2)}) copy-start(f32[8,128]{1,0:T(8,128)} %get-tuple-element.46) | copy-start | bytes 12292

commit v7 on v6

--- a/solution.py
+++ b/solution.py
@@ -1140,6 +1140,31 @@
     )(*args)
 
 
+def join_kernel(tensor, own, got, out_own, out_got, q_out, k_out, v_out, o_out):
+    t = tensor[0]
+    step = pl.program_id(0)
+    mine = pl.ds(pl.multiple_of(t * 256, 256), 256)
+    theirs = pl.ds(pl.multiple_of((1 - t) * 256, 256), 256)
+    for n, out in enumerate((q_out, k_out, v_out)):
+        out[:, mine] = own[n]
+        out[:, theirs] = got[n].astype(F32)
+    o_out[pl.ds(pl.multiple_of(t * 256 + step * 64, 64), 64), :] = out_own[...]
+    o_out[pl.ds(pl.multiple_of((1 - t) * 256 + step * 64, 64), 64), :] = out_got[...].astype(F32)
+
+
+def join(tensor, own, got, out_own, out_got):
+    triple = pl.BlockSpec((3, 128, 256), lambda i: (0, i, 0))
+    strip = pl.BlockSpec((64, 512), lambda i: (i, 0))
+    block = pl.BlockSpec((128, 512), lambda i: (i, 0))
+    return pl.pallas_call(
+        join_kernel,
+        grid=(4,),
+        out_shape=[jax.ShapeDtypeStruct((512, 512), F32)] * 4,
+        in_specs=[SMEM, triple, triple, strip, strip],
+        out_specs=[block] * 3 + [pl.BlockSpec((512, 512), lambda i: (0, 0))],
+    )(tensor, own, got, out_own, out_got)
+
+
 def body(
     hidden,
     dec_gain,
@@ -1204,17 +1229,7 @@
     dec_scale, enc_scale = scales[:rows, None], scales[rows:, None]
     dec_hat = dec_rows * dec_scale
     enc_hat = enc_rows * enc_scale
-
-    def join(mine, theirs, axis):
-        theirs = theirs.astype(F32)
-        return jnp.where(
-            t == 0,
-            jnp.concatenate([mine, theirs], axis),
-            jnp.concatenate([theirs, mine], axis),
-        )
-
-    weight_grads = [join(own[n], got[n], 1) for n in range(3)]
-    out_weight_grad = join(out_own, out_got, 0)
+    joined = join(jnp.full((1,), t, jnp.int32), own, got, out_own, out_got)
     layer_out = (dec_rows + out_total).astype(BF16)
     dec_scaled = dec_gain * dec_input
     enc_scaled = enc_gain * enc_input
@@ -1230,10 +1245,7 @@
         neighbour_grad,
         gains[:512],
         gains[512:],
-        weight_grads[0],
-        weight_grads[1],
-        weight_grads[2],
-        out_weight_grad,
+        *joined,
     )
 
 

time: 271 us -> 268 us (0.989)
  other arithmetic: 11.5 us -> 6.19 us
  Pallas kernels: 256 us -> 260 us
    select_n x2 -> x0, other arithmetic: 4.95 us -> none  [join(): jnp.where(t == 0, jnp.concatenate([mine, theirs], axis), jnp.concatenate(...]
    pallas_call x0 -> x1, Pallas kernels: none -> 4.61 us  [join(): pl.pallas_call(join_kernel, grid=(4,), out_shape=[jax.ShapeDtypeStruct((5...]
where the time goes in v7:
time: 268 us
  Pallas kernels  260 us (97%)
  other arithmetic  6.19 us (2%)
    pallas_call x1, Pallas kernels, front(): pl.pallas_call(front_kernel, out_shape=[sds((2, 32, 64, 512), BF16), sds(...  130 us
    pallas_call x1, Pallas kernels, back(): pl.pallas_call(back_kernel, out_shape=[sds((128, 512), F32), sds((128, 51...  126 us

profile of v7, /device:TPU:1, one launch (start us, length us, event | category | flops | bytes accessed | tf_op | source)
XLA Modules:
  0.0 268.1 jit_solution(1040500897364223129)
XLA Ops:
  0.6 1.3 fusion.5.bias
  2.0 1.3 select_reduce_fusion.inverse
  3.3 129.6 %shard_map.178 = (bf16[2,32,64,512]{3,2,1,0:T(8,128)(2,1)}, bf16[2,32,64,512]{3,2,1,0:T(8,128)(2,1)}, bf16[2,4096,512]{2,1,0:T(8,128)(2,1)}, bf16[2,512,256]{2,1...) custom-call(bf16[2,64,512]{2,1,0:T(8,128)(2,1)} %bitcast.22, ...), custom_call_target="tpu_custom_call" | custom-call | tf_op jit(solution)/shard_map/pallas_call | solution.py:549
  132.8 0.0 copy-start.7
  132.8 0.0 copy-start
  132.8 0.0 copy-start.5
  132.9 126.3 %shard_map.179 = (f32[128,512]{1,0:T(8,128)}, f32[128,512]{1,0:T(8,128)}, f32[256,512]{1,0:T(8,128)}, f32[3,512,256]{2,1,0:T(8,128)}, f32[256,512]{1,0:T(8,128)}...) custom-call(bf16[4,64,256]{2,1,0:T(8,128)(2,1)} %get-tuple-element.34.att_own, ...), custom_call_target="tpu_custom_call" | custom-call | tf_op jit(solution)/shard_map/pallas_call | solution.py:1082
  259.2 0.0 copy-start.1
  259.2 0.0 copy-start.2
  259.2 0.0 copy-start.3
  259.2 0.0 copy-start.4
  259.2 0.0 copy-start.6
  259.2 0.0 copy-start.8
  259.2 4.6 %shard_map.180 = (f32[512,512]{1,0:T(8,128)}, f32[512,512]{1,0:T(8,128)}, f32[512,512]{1,0:T(8,128)}, f32[512,512]{1,0:T(8,128)}) custom-call(s32[1]{0:T(128)} %bitcast.12.tensor, f32[3,512,256]{2,1,0:T(8,128)} %get-tuple-element.51.own, bf16[3,512,256]{2,1,0:T(8,128)(2,1)} %get-tuple-element.52.got, f32[256,512]{1,0:T(8,128)} %get-tuple-element.53.out_own, ...), custom_call_target="tpu_custom_call" | custom-call | tf_op jit(solution)/shard_map/pallas_call | solution.py:1159
  263.9 0.7 slice_multiply_fusion
  264.5 0.0 copy-done.7
  264.6 0.0 copy-done
  264.6 0.0 copy-done.5
  264.6 2.0 subtract_multiply_fusion
  266.6 0.0 copy-done.1
  266.6 0.0 copy-done.2
  266.6 0.0 copy-done.3
  266.6 0.0 copy-done.4
  266.6 0.0 copy-done.6
  266.7 0.9 fusion.4
  267.5 0.0 copy-done.8
  267.5 0.6 slice_bitcast_fusion
  (3 shorter events, 0.0 us)
Async XLA Ops:
  132.8 131.7 %copy-start.7 = (f32[8,128]{1,0:T(8,128)S(1)}, f32[8,128]{1,0:T(8,128)}, u32[]{:S(2)}) copy-start(f32[8,128]{1,0:T(8,128)} %get-tuple-element.45.squares) | copy-start | bytes 12292
  132.8 131.7 %copy-start = (bf16[256,512]{1,0:T(8,128)(2,1)S(1)}, bf16[256,512]{1,0:T(8,128)(2,1)}, u32[]{:S(2)}) copy-start(bf16[256,512]{1,0:T(8,128)(2,1)} %neigh.3) | copy-start | bytes 786436
  132.8 131.7 %copy-start.5 = (f32[512]{0:T(512)S(1)}, f32[512]{0:T(512)}, u32[]{:S(2)}) copy-start(f32[512]{0:T(512)} %param.14) | copy-start | bytes 6148
  259.2 7.4 %copy-start.1 = (bf16[128,512]{1,0:T(8,128)(2,1)S(1)}, bf16[128,512]{1,0:T(8,128)(2,1)}, u32[]{:S(2)}) copy-start(bf16[128,512]{1,0:T(8,128)(2,1)} %hidden.1) | copy-start | bytes 393220
  259.2 7.4 %copy-start.2 = (bf16[128,512]{1,0:T(8,128)(2,1)S(1)}, bf16[128,512]{1,0:T(8,128)(2,1)}, u32[]{:S(2)}) copy-start(bf16[128,512]{1,0:T(8,128)(2,1)} %param.21) | copy-start | bytes 393220
  259.2 7.4 %copy-start.3 = (f32[128,512]{1,0:T(8,128)S(1)}, f32[128,512]{1,0:T(8,128)}, u32[]{:S(2)}) copy-start(f32[128,512]{1,0:T(8,128)} %get-tuple-element.47) | copy-start | bytes 786436
  259.2 7.4 %copy-start.4 = (f32[128,512]{1,0:T(8,128)S(1)}, f32[128,512]{1,0:T(8,128)}, u32[]{:S(2)}) copy-start(f32[128,512]{1,0:T(8,128)} %get-tuple-element.46) | copy-start | bytes 786436
  259.2 7.4 %copy-start.6 = (f32[512]{0:T(512)S(1)}, f32[512]{0:T(512)}, u32[]{:S(2)}) copy-start(f32[512]{0:T(512)} %param.12) | copy-start | bytes 6148
  259.2 8.3 %copy-start.8 = (f32[8,128]{1,0:T(8,128)S(1)}, f32[8,128]{1,0:T(8,128)}, u32[]{:S(2)}) copy-start(f32[8,128]{1,0:T(8,128)} %get-tuple-element.50) | copy-start | bytes 12292
